TPU v7x, 256 devices: a whole 4x4x8 slice. The times are simulated.
256 devices in a mesh: dp: 32 (over z_hi, x, core), tensor: 8 (over z_lo, y).
Axes of the slice: x: 4, y: 4, z: 8 (z_hi: 4, z_lo: 2; z = z_hi * 2 + z_lo), core: 2. Of those that a mesh axis runs over, the one named last changes fastest.
Arguments:
- hidden: bfloat16 [16384, 16384], P('dp')
- head: bfloat16 [2048, 16384], P('tensor', 'dp')
- targets: int32 [16384], P('dp'), may hold values from 0 to 127999, as said below
- block_index: int32 [2], replicated, may hold values from 0 to 124, as said below
- lse_rest: float32 [16384], P('dp'), may hold values from 6 to 12
- cotangent: float32 [16384], P('dp'), may hold values from 0.5 to 1.5
Outputs:
- loss: float32 [16384], P('dp')
- head_grad: float32 [2048, 16384], P('tensor', 'dp')
Inputs may be any that keep to these rules, and one draw needn't show every extreme that they name: `block_index`: distinct block numbers of the vocabulary. Every target lies in one of the window's blocks: targets // 1024 is an entry of block_index.
All inputs are finite; a program needn't handle non-finite values.
Results may differ from a plain program's by a relative error of at most 0.003.
Values may be sent and summed in bfloat16 or wider, within the bound.
No kernel may reach another device: no remote copies, remote signals or barrier semaphores. Data moves between devices by JAX's collectives and lax.ppermute only.
A program may use at most 128 MiB of HBM per device.

v0:
```python
import jax
import jax.numpy as jnp
from jax import lax
from jax.experimental import pallas as pl
from jax.experimental.pallas import tpu as pltpu
from jax.sharding import Mesh
from jax.sharding import PartitionSpec as P

BLOCK = 1024
z_weight = 0.0001

AXES = ("zh", "x", "c", "zl", "y")
SIZES = (4, 4, 2, 2, 4)
DP = ("zh", "x", "c")
TENSOR = ("zl", "y")

ROWS = 256
TOK = 512
WIDE = 512
PR, QR = 192, 64
PH, QH, RH = PR // 2, QR // 2, ROWS // 2

F32 = jnp.float32
BF16 = jnp.bfloat16
MIB = 1024 * 1024


def move(value, axis, by):
    n = SIZES[AXES.index(axis)]
    return lax.ppermute(value, axis, [(i, (i + by) % n) for i in range(n)])


def params(mib):
    return pltpu.CompilerParams(vmem_limit_bytes=mib * MIB)


def whole(shape):
    return pl.BlockSpec(shape, lambda: (0,) * len(shape))


def local_call(body, outs, *args):
    size = sum(a.size * a.dtype.itemsize for a in args) + sum(
        o.size * o.dtype.itemsize for o in outs
    )
    return pl.pallas_call(
        body,
        out_shape=outs,
        in_specs=[whole(a.shape) for a in args],
        out_specs=[whole(o.shape) for o in outs],
        compiler_params=params(16),
        cost_estimate=pl.CostEstimate(flops=0, bytes_accessed=size, transcendentals=0),
    )(*args)


def pick(hidden, at):
    n = at.shape[0]

    def body(at_ref, h_ref, o_ref, arrived):
        copies = [
            pltpu.make_async_copy(
                h_ref.at[:, pl.ds(pl.multiple_of(at_ref[k] * WIDE, WIDE), WIDE)],
                o_ref.at[k],
                arrived.at[k],
            )
            for k in range(n)
        ]
        for copy in copies:
            copy.start()
        for copy in copies:
            copy.wait()

    return pl.pallas_call(
        body,
        out_shape=jax.ShapeDtypeStruct((n, TOK, WIDE), BF16),
        in_specs=[
            pl.BlockSpec(memory_space=pltpu.SMEM),
            pl.BlockSpec(memory_space=pl.ANY),
        ],
        out_specs=pl.BlockSpec(memory_space=pltpu.VMEM),
        scratch_shapes=[pltpu.SemaphoreType.DMA((n,))],
        compiler_params=params(50),
        cost_estimate=pl.CostEstimate(
            flops=0, bytes_accessed=2 * n * TOK * WIDE * 2, transcendentals=0
        ),
    )(at, hidden)


def block_call(compute, slots, outs, blocks, others, rows):
    at, hidden, theirs = blocks
    places = max(slots) + 1

    def body(at_ref, h_ref, t_ref, *refs):
        hold, arrived = refs[-2:]

        def copies(place, slot):
            start = pl.multiple_of(at_ref[slot] * WIDE, WIDE)
            for side, ref in enumerate((h_ref.at[:, pl.ds(start, WIDE)], t_ref.at[slot])):
                yield pltpu.make_async_copy(
                    ref, hold.at[place, pl.ds(side * TOK, TOK)], arrived.at[place, side]
                )

        for place, slot in slots.items():
            for copy in copies(place, slot):
                copy.start()

        def block(place, wait=True):
            if wait:
                for copy in copies(place, 0):
                    copy.wait()
            return hold[place]

        compute(block, refs[: len(others)], refs[len(others) : -2])

    return pl.pallas_call(
        body,
        out_shape=outs,
        in_specs=[pl.BlockSpec(memory_space=pltpu.SMEM)]
        + [pl.BlockSpec(memory_space=pl.ANY)] * 2
        + [whole(o.shape) for o in others],
        out_specs=[whole(o.shape) for o in outs],
        scratch_shapes=[
            pltpu.VMEM((places, 2 * TOK, WIDE), BF16),
            pltpu.SemaphoreType.DMA((places, 2)),
        ],
        compiler_params=params(50),
        cost_estimate=pl.CostEstimate(
            flops=4 * rows * WIDE * TOK,
            bytes_accessed=2 * len(slots) * TOK * WIDE * 2,
            transcendentals=0,
        ),
    )(at, hidden, theirs, *others)


def times(a, block):
    return lax.dot_general(a, block, (((1,), (1,)), ((), ())), preferred_element_type=F32)


def rows_at(k, size):
    return pl.ds(pl.multiple_of(k * size, size), size)


LOGITS = jax.ShapeDtypeStruct((ROWS, 2 * TOK), F32)
AHEAD = (1, 3, 2)


def statistics(partial, other, hit):
    def body(mine, theirs, hit_ref, logits, stats):
        total = mine[...] + jnp.concatenate([theirs[:, TOK:], theirs[:, :TOK]], axis=1)
        logits[...] = total
        top = jnp.max(total, axis=0, keepdims=True)
        stats[0:1, :] = top
        stats[1:2, :] = jnp.sum(jnp.exp(total - top), axis=0, keepdims=True)
        stats[2:3, :] = jnp.sum(total * hit_ref[...], axis=0, keepdims=True)

    outs = [
        jax.ShapeDtypeStruct((ROWS, 2 * TOK), F32),
        jax.ShapeDtypeStruct((3, 2 * TOK), F32),
    ]
    return local_call(body, outs, partial, other, hit)


def gradient(logits, hit, stats, lse_rest, cotangent):
    def body(logits_ref, hit_ref, s, rest, cot, loss, grad):
        top = s[0]
        row_max = jnp.max(top, axis=0, keepdims=True)
        row_total = jnp.sum(s[1] * jnp.exp(top - row_max), axis=0, keepdims=True)
        target_logit = jnp.sum(s[2], axis=0, keepdims=True)
        lse_window = row_max + jnp.log(row_total)
        larger = jnp.maximum(lse_window, rest[...])
        log_total = larger + jnp.log(
            jnp.exp(lse_window - larger) + jnp.exp(rest[...] - larger)
        )
        loss[...] = log_total - target_logit + z_weight * log_total * log_total
        softmax = jnp.exp(logits_ref[...] - log_total)
        grad[...] = (
            cot[...] * (softmax * (1.0 + 2.0 * z_weight * log_total) - hit_ref[...])
        ).astype(BF16)

    outs = [
        jax.ShapeDtypeStruct((1, 2 * TOK), F32),
        jax.ShapeDtypeStruct((ROWS, 2 * TOK), BF16),
    ]
    return local_call(body, outs, logits, hit, stats, lse_rest, cotangent)


def gathered_logits(head, hidden, at, sibling_at):
    zb, za = move(head[:PR], "zh", 1), move(head[:PR], "zh", -1)
    xb, xa = move(head, "x", 1), move(head, "x", -1)
    picked = pick(hidden, sibling_at)
    zb, za, xb, xa, picked = lax.optimization_barrier((zb, za, xb, xa, picked))
    theirs = move(picked, "c", 1)
    zf1, zf2 = move(zb[:PH], "zh", 1), move(za[PH:], "zh", -1)
    xf1, xf2 = move(xb[:RH], "x", 1), move(xa[RH:], "x", -1)
    zf1, zf2, xf1, xf2 = lax.optimization_barrier((zf1, zf2, xf1, xf2))
    p = jnp.concatenate([za, zb, zf1, zf2], axis=0)
    q = jnp.concatenate([head[PR:], xa[PR:], xb[PR:], xf2[PR - RH :]], axis=0)
    pb, pa = move(p, "x", 1), move(p, "x", -1)
    qb, qa = move(q, "zh", 1), move(q, "zh", -1)
    blocks = (at, hidden, theirs)

    def first(block, refs, outs):
        (out,) = outs
        head_ref, xa_ref, xb_ref, xf1_ref, xf2_ref, p_ref = refs
        out[...] = times(head_ref[...], block(0))
        out[...] += times(xa_ref[...], block(1))
        out[...] += times(xb_ref[...], block(2))
        far = block(3)
        out[:RH, :] += times(xf1_ref[...], far)
        out[RH:, :] += times(xf2_ref[...], far)

        @pl.loop(0, 3)
        def _(k):
            out[:PR, :] += times(p_ref[rows_at(k, PR), :], block(4 + k))

    slots = {0: 0, 1: 1, 2: 3, 3: 2} | {4 + k: 4 * dz for k, dz in enumerate(AHEAD)}
    (total,) = block_call(
        first, slots, [LOGITS], blocks, [head, xa, xb, xf1, xf2, p], 4 * ROWS + 3 * PR
    )
    pb, pa, qb, qa, total = lax.optimization_barrier((pb, pa, qb, qa, total))
    pf1, pf2 = move(pb[: 3 * PH], "x", 1), move(pa[3 * PH :], "x", -1)
    qf1, qf2 = move(qb[: 2 * QR], "zh", 1), move(qa[2 * QR :], "zh", -1)

    places = {4 * i + j: 4 * dz + dx for i, dz in enumerate(AHEAD) for j, dx in enumerate((0,) + AHEAD)}

    def second(block, refs, outs):
        (out,) = outs
        pa_ref, pb_ref, qa_ref, qb_ref, total_ref = refs
        out[...] = total_ref[...]

        @pl.loop(0, 3)
        def _(k):
            part = rows_at(k, PR)
            out[:PR, :] += times(pa_ref[part, :], block(4 * k + 1))
            out[:PR, :] += times(pb_ref[part, :], block(4 * k + 2))

        for j in range(4):
            new = j in (0, 3)
            part = slice(j * QR, (j + 1) * QR)
            out[PR:, :] += times(qa_ref[part, :], block(j, new))
            out[PR:, :] += times(qb_ref[part, :], block(4 + j, new))

    slots = {k: v for k, v in places.items() if k not in (8, 11)}
    (total,) = block_call(
        second, slots, [LOGITS], blocks, [pa, pb, qa, qb, total], 6 * PR + 8 * QR
    )

    def third(block, refs, outs):
        (out,) = outs
        pf1_ref, pf2_ref, qf1_ref, qf2_ref, total_ref = refs
        out[...] = total_ref[...]
        out[:PR, :] += times(pf1_ref[:PR, :], block(3))
        middle = block(7)
        out[:PH, :] += times(pf1_ref[PR:, :], middle)
        out[PH:PR, :] += times(pf2_ref[:PH, :], middle)
        out[:PR, :] += times(pf2_ref[PH:, :], block(11))
        out[PR:, :] += times(qf1_ref[:QR, :], block(8))
        out[PR:, :] += times(qf1_ref[QR:, :], block(9))
        out[PR:, :] += times(qf2_ref[:QR, :], block(10))
        out[PR:, :] += times(qf2_ref[QR:, :], block(11, False))

    slots = {k: places[k] for k in (3, 7, 8, 9, 10, 11)}
    (total,) = block_call(
        third, slots, [LOGITS], blocks, [pf1, pf2, qf1, qf2, total], 3 * PR + 4 * QR
    )
    return total, blocks


def scattered_gradient(grad, blocks):
    def array(rows, dtype):
        return jax.ShapeDtypeStruct((rows, WIDE), dtype)

    outs = [
        array(3 * PR, BF16),
        array(3 * PR, BF16),
        array(4 * QR, BF16),
        array(4 * QR, BF16),
        array(3 * PH, F32),
        array(3 * PH, F32),
        array(3 * PR, F32),
        array(4 * QH, F32),
        array(4 * QH, F32),
    ]
    def others_terms(block, refs, outs):
        (g_ref,) = refs
        p_up, p_down, q_up, q_down, p_ahead, p_behind, p_here, q_ahead, q_behind = outs

        @pl.loop(0, 3)
        def _(k):
            first, last = pl.ds(pl.multiple_of(k * PR, PR), PH), pl.ds(pl.multiple_of(k * PR + PH, PH), PH)
            kept = rows_at(k, PH)
            for dx in range(4):
                term = jnp.dot(g_ref[...], block(4 * k + dx), preferred_element_type=F32)
                one, two, three, four = term[:PH], term[PH:PR], term[PR : PR + QH], term[PR + QH :]
                if dx == 0:
                    p_here[rows_at(k, PR), :] = term[:PR]
                elif dx == 1:
                    p_ahead[kept, :] = one
                    p_up[last, :] = two.astype(BF16)
                elif dx == 2:
                    p_up[first, :] = one.astype(BF16)
                    p_down[last, :] = two.astype(BF16)
                else:
                    p_down[first, :] = one.astype(BF16)
                    p_behind[kept, :] = two
                start, middle = dx * QR, dx * QR + QH

                @pl.when(k == 0)
                def _():
                    q_ahead[dx * QH : (dx + 1) * QH, :] = three
                    q_up[middle : middle + QH, :] = four.astype(BF16)

                @pl.when(k == 1)
                def _():
                    q_up[start:middle, :] = three.astype(BF16)
                    q_down[middle : middle + QH, :] = four.astype(BF16)

                @pl.when(k == 2)
                def _():
                    q_down[start:middle, :] = three.astype(BF16)
                    q_behind[dx * QH : (dx + 1) * QH, :] = four

    slots = {place: 4 + place for place in range(12)}
    p_up, p_down, q_up, q_down, p_ahead, p_behind, p_here, q_ahead, q_behind = block_call(
        others_terms, slots, outs, blocks, [grad], 12 * ROWS
    )
    p_up, p_down = move(p_up, "x", 1), move(p_down, "x", -1)
    q_up, q_down = move(q_up, "zh", 1), move(q_down, "zh", -1)
    def own_terms(block, refs, outs):
        (g_ref,) = refs
        own, q_here = outs

        @pl.loop(0, 4)
        def _(dx):
            term = jnp.dot(g_ref[...], block(dx), preferred_element_type=F32)
            own[rows_at(dx, PR), :] = term[:PR]
            q_here[rows_at(dx, QR), :] = term[PR:]

    outs = [array(4 * PR, F32), array(4 * QR, F32)]
    own, q_here = block_call(
        own_terms, {dx: dx for dx in range(4)}, outs, blocks, [grad], 4 * ROWS
    )
    p_up, p_down, own, q_here = lax.optimization_barrier((p_up, p_down, own, q_here))

    def forward(kept_ahead, kept_behind, up, down, n, half):
        def body(a, b, u, d, up_out, down_out):
            for k in range(n):
                to, first, last = k * half, 2 * k * half, (2 * k + 1) * half
                up_out[to : to + half, :] = (
                    a[to : to + half, :] + u[first : first + half, :].astype(F32)
                ).astype(BF16)
                down_out[to : to + half, :] = (
                    b[to : to + half, :] + d[last : last + half, :].astype(F32)
                ).astype(BF16)

        return local_call(
            body, [array(n * half, BF16)] * 2, kept_ahead, kept_behind, up, down
        )

    def settle(kept, up, down, up2, down2, n, half, k):
        to, first, last = k * half, 2 * k * half, (2 * k + 1) * half
        one = kept[first : first + half, :] + down[first : first + half, :].astype(F32)
        two = kept[last : last + half, :] + up[last : last + half, :].astype(F32)
        return (
            one + up2[to : to + half, :].astype(F32),
            two + down2[to : to + half, :].astype(F32),
        )

    p_up2, p_down2 = forward(p_ahead, p_behind, p_up, p_down, 3, PH)
    p_up2, p_down2 = move(p_up2, "x", 1), move(p_down2, "x", -1)
    q_up2, q_down2 = forward(q_ahead, q_behind, q_up, q_down, 4, QH)
    q_up2, q_down2 = move(q_up2, "zh", 1), move(q_down2, "zh", -1)

    def p_body(kept, up, down, up2, down2, up_out, down_out, ahead, behind):
        for dz in (1, 2, 3):
            one, two = settle(kept, up, down, up2, down2, 3, PH, dz - 1)
            if dz == 1:
                ahead[...] = one
                up_out[PH:, :] = two.astype(BF16)
            elif dz == 2:
                up_out[:PH, :] = one.astype(BF16)
                down_out[PH:, :] = two.astype(BF16)
            else:
                down_out[:PH, :] = one.astype(BF16)
                behind[...] = two

    z_up, z_down, z_ahead, z_behind = local_call(
        p_body,
        [array(PR, BF16), array(PR, BF16), array(PH, F32), array(PH, F32)],
        p_here, p_up, p_down, p_up2, p_down2,
    )
    z_up, z_down = move(z_up, "zh", 1), move(z_down, "zh", -1)

    def q_body(own, kept, up, down, up2, down2, up_out, down_out, ahead, behind, here):
        rest = PR - RH
        for dx in range(4):
            one, two = settle(kept, up, down, up2, down2, 4, QH, dx)
            first = own[dx * PR : dx * PR + RH, :]
            last = own[dx * PR + RH : (dx + 1) * PR, :]
            for ref, at_last, low in {
                0: ((here, RH, 0),),
                1: ((up_out, RH, 1),),
                2: ((down_out, RH, 1),),
                3: ((behind, 0, 0),),
            }[dx]:
                ref[at_last : at_last + rest, :] = last.astype(ref.dtype)
                ref[at_last + rest : at_last + rest + QH, :] = one.astype(ref.dtype)
                ref[at_last + rest + QH : at_last + RH, :] = two.astype(ref.dtype)
            ref = (here, ahead, up_out, down_out)[dx]
            ref[:RH, :] = first.astype(ref.dtype)

    x_up, x_down, x_ahead, x_behind, x_here = local_call(
        q_body,
        [array(ROWS, BF16), array(ROWS, BF16), array(RH, F32), array(RH, F32), array(ROWS, F32)],
        own, q_here, q_up, q_down, q_up2, q_down2,
    )
    x_up, x_down = move(x_up, "x", 1), move(x_down, "x", -1)

    z_up2, z_down2 = forward(z_ahead, z_behind, z_up, z_down, 1, PH)
    z_up2, z_down2 = move(z_up2, "zh", 1), move(z_down2, "zh", -1)
    x_up2, x_down2 = forward(x_ahead, x_behind, x_up, x_down, 1, RH)
    x_up2, x_down2 = move(x_up2, "x", 1), move(x_down2, "x", -1)

    def last_body(here, xu, xd, xu2, xd2, zu, zd, zu2, zd2, out):
        out[:RH, :] = here[:RH, :] + xd[:RH, :].astype(F32) + xu2[...].astype(F32)
        out[RH:, :] = here[RH:, :] + xu[RH:, :].astype(F32) + xd2[...].astype(F32)
        out[:PH, :] += zd[:PH, :].astype(F32) + zu2[...].astype(F32)
        out[PH:PR, :] += zu[PH:, :].astype(F32) + zd2[...].astype(F32)

    (out,) = local_call(
        last_body, [array(ROWS, F32)],
        x_here, x_up, x_down, x_up2, x_down2, z_up, z_down, z_up2, z_down2,
    )
    return out


def shards(hidden, head, targets, block_index, lse_rest, cotangent):
    zh, x, c = (lax.axis_index(a) for a in DP)
    first_row = lax.axis_index(TENSOR) * ROWS
    row_ids = first_row + lax.iota(jnp.int32, ROWS)
    block_of = row_ids // BLOCK
    block_match = (block_of[:, None] == lax.iota(jnp.int32, block_index.shape[0])[None, :]).astype(
        jnp.int32
    )
    vocab_ids = jnp.sum(block_match * block_index[None, :], axis=1) * BLOCK + row_ids % BLOCK

    k = lax.iota(jnp.int32, 16)
    at = (((zh + k // 4) % 4) * 4 + (x + k % 4) % 4) * 2
    at, sibling_at = at + c, at + (1 - c)

    facts = jnp.stack([targets.astype(F32), lse_rest, cotangent])
    facts = jnp.concatenate([facts, move(facts, "c", 1)], axis=1)
    hit = (vocab_ids[:, None] == facts[0].astype(jnp.int32)[None, :]).astype(F32)

    partial, blocks = gathered_logits(head, hidden, at, sibling_at)
    logits, stats = statistics(partial, move(partial, "c", 1), hit)
    stats = lax.all_to_all(
        jnp.broadcast_to(stats[None], (8,) + stats.shape), TENSOR, split_axis=0, concat_axis=0, tiled=True
    )
    loss, grad = gradient(
        logits, hit, jnp.swapaxes(stats, 0, 1), facts[1:2], facts[2:3]
    )
    return loss[0, :TOK], scattered_gradient(grad, blocks)


def solution(mesh):
    mesh = Mesh(mesh.devices.reshape(SIZES), AXES)
    placed = (P(DP, None), P(TENSOR, DP), P(DP), P(), P(DP), P(DP))
    return jax.shard_map(
        shards, mesh=mesh, in_specs=placed, out_specs=(P(DP), P(TENSOR, DP)), check_vma=False
    )
```

profile of v0, /device:TPU:8, one launch (start us, length us, event | category | flops | bytes accessed | tf_op | source)
XLA Modules:
  0.0 149.5 jit_solution(5233307946176308707)
XLA Ops:
  4.9 3.3 %collective-permute-start = (bf16[192,512]{1,0:T(8,128)(2,1)S(1)}, bf16[192,512]{1,0:T(8,128)(2,1)S(1)}, u32[]{:S(2)}, u32[]{:S(2)}) collective-permute-start(bf16[192,512]{1,0:T(8,128)(2,1)S(1)} %slice.52), channel_id=1, source_target_pairs={{0,64},{64,128},{128,192},{192,0},{1,65},{65,129},{129,193},{193,1... | collective-permute-start | bytes 589832 | tf_op jit(solution)/shard_map/ppermute | solution.py:30
  8.3 3.1 %collective-permute-start.1 = (bf16[192,512]{1,0:T(8,128)(2,1)S(1)}, bf16[192,512]{1,0:T(8,128)(2,1)S(1)}, u32[]{:S(2)}, u32[]{:S(2)}) collective-permute-start(bf16[192,512]{1,0:T(8,128)(2,1)S(1)} %slice.52), channel_id=1, source_target_pairs={{0,192},{64,0},{128,64},{192,128},{1,193},{65,1},{129,65},{193,129... | collective-permute-start | bytes 589832 | tf_op jit(solution)/shard_map/ppermute | solution.py:30
  11.4 7.5 %shard_map.77 = bf16[16,512,512]{2,1,0:T(8,128)(2,1)} custom-call(s32[16]{0:T(128)S(1)} %broadcast_add_fusion.at_ref, bf16[512,16384]{1,0:T(8,128)(2,1)} %h_ref.11), custom_call_target="tpu_custom_call" | custom-call | bytes 16777216 | tf_op jit(solution)/shard_map/pallas_call | solution.py:72
  18.9 2.1 %collective-permute-done.1 = bf16[192,512]{1,0:T(8,128)(2,1)S(1)} collective-permute-done((bf16[192,512]{1,0:T(8,128)(2,1)S(1)}, bf16[192,512]{1,0:T(8,128)(2,1)S(1)}, u32[]{:S(2)}, u32[]{:S(2)}) %collective-permute-start.1) | collective-permute-done | bytes 196640 | tf_op jit(solution)/shard_map/ppermute | solution.py:30
  21.4 3.0 %collective-permute-start.8 = (bf16[128,512]{1,0:T(8,128)(2,1)S(1)}, bf16[128,512]{1,0:T(8,128)(2,1)S(1)}, u32[]{:S(2)}, u32[]{:S(2)}) collective-permute-start(bf16[128,512]{1,0:T(8,128)(2,1)S(1)} %slice.56), channel_id=1, source_target_pairs={{0,48},{16,0},{32,16},{48,32},{1,49},{17,1},{33,17},{49,33},{2,50}... | collective-permute-start | bytes 393224 | tf_op jit(solution)/shard_map/ppermute | solution.py:30
  24.5 3.7 %collective-permute-start.5 = (bf16[96,512]{1,0:T(8,128)(2,1)S(1)}, bf16[96,512]{1,0:T(8,128)(2,1)S(1)}, u32[]{:S(2)}, u32[]{:S(2)}) collective-permute-start(bf16[96,512]{1,0:T(8,128)(2,1)S(1)} %slice.53), channel_id=1, source_target_pairs={{0,64},{64,128},{128,192},{192,0},{1,65},{65,129},{129,193},{193,1... | collective-permute-start | bytes 294920 | tf_op jit(solution)/shard_map/ppermute | solution.py:30
  28.7 3.6 %collective-permute-done.5 = bf16[96,512]{1,0:T(8,128)(2,1)S(1)} collective-permute-done((bf16[96,512]{1,0:T(8,128)(2,1)S(1)}, bf16[96,512]{1,0:T(8,128)(2,1)S(1)}, u32[]{:S(2)}, u32[]{:S(2)}) %collective-permute-start.5) | collective-permute-done | bytes 98336 | tf_op jit(solution)/shard_map/ppermute | solution.py:30
  32.4 3.2 %collective-permute-done.6 = bf16[96,512]{1,0:T(8,128)(2,1)S(1)} collective-permute-done((bf16[96,512]{1,0:T(8,128)(2,1)S(1)}, bf16[96,512]{1,0:T(8,128)(2,1)S(1)}, u32[]{:S(2)}, u32[]{:S(2)}) %collective-permute-start.6) | collective-permute-done | bytes 98336 | tf_op jit(solution)/shard_map/ppermute | solution.py:30
  35.7 3.2 %collective-permute-start.10 = (bf16[576,512]{1,0:T(8,128)(2,1)S(1)}, bf16[576,512]{1,0:T(8,128)(2,1)S(1)}, u32[]{:S(2)}, u32[]{:S(2)}) collective-permute-start(bf16[576,512]{1,0:T(8,128)(2,1)S(1)} %constant_dynamic-update-slice_fusion.refs_5_), channel_id=1, source_target_pairs={{0,48},{16,0},{32,16},{48,32},{1,49},{17,1},{33,17},{49,33},{2,50}... | collective-permute-start | bytes 1769480 | tf_op jit(solution)/shard_map/ppermute | solution.py:30
  40.8 2.3 %collective-permute-start.12 = (bf16[256,512]{1,0:T(8,128)(2,1)S(1)}, bf16[256,512]{1,0:T(8,128)(2,1)S(1)}, u32[]{:S(2)}, u32[]{:S(2)}) collective-permute-start(bf16[256,512]{1,0:T(8,128)(2,1)S(1)} %pad_maximum_fusion), channel_id=1, source_target_pairs={{0,192},{64,0},{128,64},{192,128},{1,193},{65,1},{129,65},{193,129... | collective-permute-start | bytes 786440 | tf_op jit(solution)/shard_map/ppermute | solution.py:30
  43.2 5.5 %shard_map.78.refs_4_ = f32[256,1024]{1,0:T(8,128)S(1)} custom-call(s32[16]{0:T(128)S(1)} %broadcast_add_fusion.1.at_ref, bf16[512,16384]{1,0:T(8,128)(2,1)} %h_ref.11, bf16[16,512,512]{2,1,0:T(8,128)(2,1)} %collective-permute-done.4.t_ref, bf16[256,512]{1,0:T(8,128)(2,1)S(1)} %copy-done.1, bf16[256,512]{1,0:T(8,128)(2,1)S(1)} %collective-permute-done.3.refs_1_, ...), custom_call_target="tpu_custom_call" | custom-call | flops 1677721600 | bytes 7340032 | tf_op jit(solution)/shard_map/pallas_call | solution.py:114
  53.0 3.0 %collective-permute-start.14 = (bf16[288,512]{1,0:T(8,128)(2,1)S(1)}, bf16[288,512]{1,0:T(8,128)(2,1)S(1)}, u32[]{:S(2)}, u32[]{:S(2)}) collective-permute-start(bf16[288,512]{1,0:T(8,128)(2,1)S(1)} %slice.62), channel_id=1, source_target_pairs={{0,48},{16,0},{32,16},{48,32},{1,49},{17,1},{33,17},{49,33},{2,50}... | collective-permute-start | bytes 884744 | tf_op jit(solution)/shard_map/ppermute | solution.py:30
  56.1 1.9 %collective-permute-start.15 = (bf16[128,512]{1,0:T(8,128)(2,1)S(1)}, bf16[128,512]{1,0:T(8,128)(2,1)S(1)}, u32[]{:S(2)}, u32[]{:S(2)}) collective-permute-start(bf16[128,512]{1,0:T(8,128)(2,1)S(1)} %slice.63), channel_id=1, source_target_pairs={{0,64},{64,128},{128,192},{192,0},{1,65},{65,129},{129,193},{193,1... | collective-permute-start | bytes 393224 | tf_op jit(solution)/shard_map/ppermute | solution.py:30
  58.0 2.4 %collective-permute-start.16 = (bf16[128,512]{1,0:T(8,128)(2,1)S(1)}, bf16[128,512]{1,0:T(8,128)(2,1)S(1)}, u32[]{:S(2)}, u32[]{:S(2)}) collective-permute-start(bf16[128,512]{1,0:T(8,128)(2,1)S(1)} %slice.64), channel_id=1, source_target_pairs={{0,192},{64,0},{128,64},{192,128},{1,193},{65,1},{129,65},{193,129... | collective-permute-start | bytes 393224 | tf_op jit(solution)/shard_map/ppermute | solution.py:30
  60.4 8.2 %shard_map.79.refs_4_ = f32[256,1024]{1,0:T(8,128)S(1)} custom-call(s32[16]{0:T(128)S(1)} %broadcast_add_fusion.1.at_ref, bf16[512,16384]{1,0:T(8,128)(2,1)} %h_ref.11, bf16[16,512,512]{2,1,0:T(8,128)(2,1)} %collective-permute-done.4.t_ref, bf16[576,512]{1,0:T(8,128)(2,1)S(1)} %collective-permute-done.10.refs_0_, ...), custom_call_target="tpu_custom_call" | custom-call | flops 1744830464 | bytes 10485760 | tf_op jit(solution)/shard_map/pallas_call | solution.py:114
  68.6 5.5 %shard_map.80.mine = f32[256,1024]{1,0:T(8,128)S(1)} custom-call(s32[16]{0:T(128)S(1)} %broadcast_add_fusion.1.at_ref, bf16[512,16384]{1,0:T(8,128)(2,1)} %h_ref.11, bf16[16,512,512]{2,1,0:T(8,128)(2,1)} %collective-permute-done.4.t_ref, bf16[288,512]{1,0:T(8,128)(2,1)S(1)} %collective-permute-done.13.refs_0_, ...), custom_call_target="tpu_custom_call" | custom-call | flops 872415232 | bytes 6291456 | tf_op jit(solution)/shard_map/pallas_call | solution.py:114
  75.0 1.9 %collective-permute-done.18 = f32[3,512]{1,0:T(4,128)S(1)} collective-permute-done((f32[3,512]{1,0:T(4,128)S(1)}, f32[3,512]{1,0:T(4,128)S(1)}, u32[]{:S(2)}, u32[]{:S(2)}) %collective-permute-start.18) | collective-permute-done | bytes 6176 | tf_op jit(solution)/shard_map/ppermute | solution.py:30
  77.9 11.1 %all_to_all.5 = f32[8,3,1024]{2,1,0:T(4,128)S(1)} all-to-all(f32[8,3,1024]{2,1,0:T(4,128)S(1)} %broadcast_in_dim.2), channel_id=1, replica_groups=mesh['zh'=4,'x'=4,'c'=2,'zl'=2,'y'=4] {'zl','y'}, dimensions={0} | all-to-all | bytes 196608 | tf_op jit(solution)/shard_map/all_to_all | solution.py:456
  89.3 8.6 %shard_map.83 = (bf16[576,512]{1,0:T(8,128)(2,1)S(1)}, bf16[576,512]{1,0:T(8,128)(2,1)S(1)}, bf16[256,512]{1,0:T(8,128)(2,1)S(1)}, bf16[256,512]{1,0:T(8,128)(2,...) custom-call(s32[16]{0:T(128)S(1)} %broadcast_add_fusion.1.at_ref, ...), custom_call_target="tpu_custom_call" | custom-call | flops 3221225472 | bytes 12582912 | tf_op jit(solution)/shard_map/pallas_call | solution.py:114
  98.0 3.2 %collective-permute-start.20 = (bf16[576,512]{1,0:T(8,128)(2,1)S(1)}, bf16[576,512]{1,0:T(8,128)(2,1)S(1)}, u32[]{:S(2)}, u32[]{:S(2)}) collective-permute-start(bf16[576,512]{1,0:T(8,128)(2,1)S(1)} %get-tuple-element.71), channel_id=1, source_target_pairs={{0,48},{16,0},{32,16},{48,32},{1,49},{17,1},{33,17},{49,33},{2,50}... | collective-permute-start | bytes 1769480 | tf_op jit(solution)/shard_map/ppermute | solution.py:30
  101.7 3.7 %collective-permute-start.22 = (bf16[256,512]{1,0:T(8,128)(2,1)S(1)}, bf16[256,512]{1,0:T(8,128)(2,1)S(1)}, u32[]{:S(2)}, u32[]{:S(2)}) collective-permute-start(bf16[256,512]{1,0:T(8,128)(2,1)S(1)} %get-tuple-element.77), channel_id=1, source_target_pairs={{0,192},{64,0},{128,64},{192,128},{1,193},{65,1},{129,65},{193,129... | collective-permute-start | bytes 786440 | tf_op jit(solution)/shard_map/ppermute | solution.py:30
  105.4 3.7 %shard_map.84 = (f32[768,512]{1,0:T(8,128)S(1)}, f32[256,512]{1,0:T(8,128)S(1)}) custom-call(s32[16]{0:T(128)S(1)} %broadcast_add_fusion.1.at_ref, bf16[512,16384]{1,0:T(8,128)(2,1)} %h_ref.11, bf16[16,512,512]{2,1,0:T(8,128)(2,1)} %collective-permute-done.4.t_ref, bf16[256,1024]{1,0:T(8,128)(2,1)S(1)} %get-tuple-element.69.refs_0_), custom_call_target="tpu_custom_call" | custom-call | flops 1073741824 | bytes 4194304 | tf_op jit(solution)/shard_map/pallas_call | solution.py:114
  109.1 4.1 %collective-permute-done.19.u.up = bf16[576,512]{1,0:T(8,128)(2,1)S(1)} collective-permute-done((bf16[576,512]{1,0:T(8,128)(2,1)S(1)}, bf16[576,512]{1,0:T(8,128)(2,1)S(1)}, u32[]{:S(2)}, u32[]{:S(2)}) %collective-permute-start.19) | collective-permute-done | bytes 589856 | tf_op jit(solution)/shard_map/ppermute | solution.py:30
  113.4 3.2 %collective-permute-start.30 = (bf16[288,512]{1,0:T(8,128)(2,1)S(1)}, bf16[288,512]{1,0:T(8,128)(2,1)S(1)}, u32[]{:S(2)}, u32[]{:S(2)}) collective-permute-start(bf16[288,512]{1,0:T(8,128)(2,1)S(1)} %get-tuple-element.95), channel_id=1, source_target_pairs={{0,48},{16,0},{32,16},{48,32},{1,49},{17,1},{33,17},{49,33},{2,50}... | collective-permute-start | bytes 884744 | tf_op jit(solution)/shard_map/ppermute | solution.py:30
  117.4 3.4 %collective-permute-start.24 = (bf16[128,512]{1,0:T(8,128)(2,1)S(1)}, bf16[128,512]{1,0:T(8,128)(2,1)S(1)}, u32[]{:S(2)}, u32[]{:S(2)}) collective-permute-start(bf16[128,512]{1,0:T(8,128)(2,1)S(1)} %get-tuple-element.81), channel_id=1, source_target_pairs={{0,192},{64,0},{128,64},{192,128},{1,193},{65,1},{129,65},{193,129... | collective-permute-start | bytes 393224 | tf_op jit(solution)/shard_map/ppermute | solution.py:30
  120.9 4.3 %collective-permute-done.23.up2 = bf16[128,512]{1,0:T(8,128)(2,1)S(1)} collective-permute-done((bf16[128,512]{1,0:T(8,128)(2,1)S(1)}, bf16[128,512]{1,0:T(8,128)(2,1)S(1)}, u32[]{:S(2)}, u32[]{:S(2)}) %collective-permute-start.23) | collective-permute-done | bytes 131104 | tf_op jit(solution)/shard_map/ppermute | solution.py:30
  125.5 3.2 %collective-permute-start.26 = (bf16[256,512]{1,0:T(8,128)(2,1)S(1)}, bf16[256,512]{1,0:T(8,128)(2,1)S(1)}, u32[]{:S(2)}, u32[]{:S(2)}) collective-permute-start(bf16[256,512]{1,0:T(8,128)(2,1)S(1)} %get-tuple-element.84), channel_id=1, source_target_pairs={{0,48},{16,0},{32,16},{48,32},{1,49},{17,1},{33,17},{49,33},{2,50}... | collective-permute-start | bytes 786440 | tf_op jit(solution)/shard_map/ppermute | solution.py:30
  128.9 3.0 %collective-permute-start.31 = (bf16[192,512]{1,0:T(8,128)(2,1)S(1)}, bf16[192,512]{1,0:T(8,128)(2,1)S(1)}, u32[]{:S(2)}, u32[]{:S(2)}) collective-permute-start(bf16[192,512]{1,0:T(8,128)(2,1)S(1)} %get-tuple-element.96), channel_id=1, source_target_pairs={{0,64},{64,128},{128,192},{192,0},{1,65},{65,129},{129,193},{193,1... | collective-permute-start | bytes 589832 | tf_op jit(solution)/shard_map/ppermute | solution.py:30
  133.3 3.2 %collective-permute-start.28 = (bf16[128,512]{1,0:T(8,128)(2,1)S(1)}, bf16[128,512]{1,0:T(8,128)(2,1)S(1)}, u32[]{:S(2)}, u32[]{:S(2)}) collective-permute-start(bf16[128,512]{1,0:T(8,128)(2,1)S(1)} %get-tuple-element.88), channel_id=1, source_target_pairs={{0,48},{16,0},{32,16},{48,32},{1,49},{17,1},{33,17},{49,33},{2,50}... | collective-permute-start | bytes 393224 | tf_op jit(solution)/shard_map/ppermute | solution.py:30
  136.5 3.2 %collective-permute-done.31.u.zu = bf16[192,512]{1,0:T(8,128)(2,1)S(1)} collective-permute-done((bf16[192,512]{1,0:T(8,128)(2,1)S(1)}, bf16[192,512]{1,0:T(8,128)(2,1)S(1)}, u32[]{:S(2)}, u32[]{:S(2)}) %collective-permute-start.31) | collective-permute-done | bytes 196640 | tf_op jit(solution)/shard_map/ppermute | solution.py:30
  139.8 3.2 %collective-permute-start.33 = (bf16[96,512]{1,0:T(8,128)(2,1)S(1)}, bf16[96,512]{1,0:T(8,128)(2,1)S(1)}, u32[]{:S(2)}, u32[]{:S(2)}) collective-permute-start(bf16[96,512]{1,0:T(8,128)(2,1)S(1)} %get-tuple-element.100), channel_id=1, source_target_pairs={{0,64},{64,128},{128,192},{192,0},{1,65},{65,129},{129,193},{193,1... | collective-permute-start | bytes 294920 | tf_op jit(solution)/shard_map/ppermute | solution.py:30
  144.6 2.8 %collective-permute-done.33.zu2 = bf16[96,512]{1,0:T(8,128)(2,1)S(1)} collective-permute-done((bf16[96,512]{1,0:T(8,128)(2,1)S(1)}, bf16[96,512]{1,0:T(8,128)(2,1)S(1)}, u32[]{:S(2)}, u32[]{:S(2)}) %collective-permute-start.33) | collective-permute-done | bytes 98336 | tf_op jit(solution)/shard_map/ppermute | solution.py:30
  (96 shorter events, 20.8 us)
Async XLA Ops:
  0.6 20.4 %collective-permute-start.2 = (bf16[256,512]{1,0:T(8,128)(2,1)}, bf16[256,512]{1,0:T(8,128)(2,1)S(1)}, u32[]{:S(2)}, u32[]{:S(2)}) collective-permute-start(bf16[256,512]{1,0:T(8,128)(2,1)} %refs_0_.1), channel_id=1, source_target_pairs={{0,16},{16,32},{32,48},{48,0},{1,17},{17,33},{33,49},{49,1},{2,18}... | collective-permute-start | bytes 786440 | tf_op jit(solution)/shard_map/ppermute | solution.py:30
  2.2 18.8 %collective-permute-start.3 = (bf16[256,512]{1,0:T(8,128)(2,1)}, bf16[256,512]{1,0:T(8,128)(2,1)S(1)}, u32[]{:S(2)}, u32[]{:S(2)}) collective-permute-start(bf16[256,512]{1,0:T(8,128)(2,1)} %refs_0_.1), channel_id=1, source_target_pairs={{0,48},{16,0},{32,16},{48,32},{1,49},{17,1},{33,17},{49,33},{2,50}... | collective-permute-start | bytes 786440 | tf_op jit(solution)/shard_map/ppermute | solution.py:30
  4.9 14.0 %collective-permute-start = (bf16[192,512]{1,0:T(8,128)(2,1)S(1)}, bf16[192,512]{1,0:T(8,128)(2,1)S(1)}, u32[]{:S(2)}, u32[]{:S(2)}) collective-permute-start(bf16[192,512]{1,0:T(8,128)(2,1)S(1)} %slice.52), channel_id=1, source_target_pairs={{0,64},{64,128},{128,192},{192,0},{1,65},{65,129},{129,193},{193,1... | collective-permute-start | bytes 589832 | tf_op jit(solution)/shard_map/ppermute | solution.py:30
  8.3 12.8 %collective-permute-start.1 = (bf16[192,512]{1,0:T(8,128)(2,1)S(1)}, bf16[192,512]{1,0:T(8,128)(2,1)S(1)}, u32[]{:S(2)}, u32[]{:S(2)}) collective-permute-start(bf16[192,512]{1,0:T(8,128)(2,1)S(1)} %slice.52), channel_id=1, source_target_pairs={{0,192},{64,0},{128,64},{192,128},{1,193},{65,1},{129,65},{193,129... | collective-permute-start | bytes 589832 | tf_op jit(solution)/shard_map/ppermute | solution.py:30
  21.0 22.2 %collective-permute-start.4 = (bf16[16,512,512]{2,1,0:T(8,128)(2,1)}, bf16[16,512,512]{2,1,0:T(8,128)(2,1)}, u32[]{:S(2)}, u32[]{:S(2)}) collective-permute-start(bf16[16,512,512]{2,1,0:T(8,128)(2,1)} %shard_map.77), channel_id=1, source_target_pairs={{0,8},{8,0},{1,9},{9,1},{2,10},{10,2},{3,11},{11,3},{4,12},{12,4},... | collective-permute-start | bytes 25165832 | tf_op jit(solution)/shard_map/ppermute | solution.py:30
  21.1 14.5 %collective-permute-start.7 = (bf16[128,512]{1,0:T(8,128)(2,1)S(1)}, bf16[128,512]{1,0:T(8,128)(2,1)S(1)}, u32[]{:S(2)}, u32[]{:S(2)}) collective-permute-start(bf16[128,512]{1,0:T(8,128)(2,1)S(1)} %slice.55), channel_id=1, source_target_pairs={{0,16},{16,32},{32,48},{48,0},{1,17},{17,33},{33,49},{49,1},{2,18}... | collective-permute-start | bytes 393224 | tf_op jit(solution)/shard_map/ppermute | solution.py:30
  21.4 14.1 %collective-permute-start.8 = (bf16[128,512]{1,0:T(8,128)(2,1)S(1)}, bf16[128,512]{1,0:T(8,128)(2,1)S(1)}, u32[]{:S(2)}, u32[]{:S(2)}) collective-permute-start(bf16[128,512]{1,0:T(8,128)(2,1)S(1)} %slice.56), channel_id=1, source_target_pairs={{0,48},{16,0},{32,16},{48,32},{1,49},{17,1},{33,17},{49,33},{2,50}... | collective-permute-start | bytes 393224 | tf_op jit(solution)/shard_map/ppermute | solution.py:30
  24.5 7.9 %collective-permute-start.5 = (bf16[96,512]{1,0:T(8,128)(2,1)S(1)}, bf16[96,512]{1,0:T(8,128)(2,1)S(1)}, u32[]{:S(2)}, u32[]{:S(2)}) collective-permute-start(bf16[96,512]{1,0:T(8,128)(2,1)S(1)} %slice.53), channel_id=1, source_target_pairs={{0,64},{64,128},{128,192},{192,0},{1,65},{65,129},{129,193},{193,1... | collective-permute-start | bytes 294920 | tf_op jit(solution)/shard_map/ppermute | solution.py:30
  28.3 7.3 %collective-permute-start.6 = (bf16[96,512]{1,0:T(8,128)(2,1)S(1)}, bf16[96,512]{1,0:T(8,128)(2,1)S(1)}, u32[]{:S(2)}, u32[]{:S(2)}) collective-permute-start(bf16[96,512]{1,0:T(8,128)(2,1)S(1)} %slice.54), channel_id=1, source_target_pairs={{0,192},{64,0},{128,64},{192,128},{1,193},{65,1},{129,65},{193,129... | collective-permute-start | bytes 294920 | tf_op jit(solution)/shard_map/ppermute | solution.py:30
  35.6 16.8 %collective-permute-start.9 = (bf16[576,512]{1,0:T(8,128)(2,1)S(1)}, bf16[576,512]{1,0:T(8,128)(2,1)S(1)}, u32[]{:S(2)}, u32[]{:S(2)}) collective-permute-start(bf16[576,512]{1,0:T(8,128)(2,1)S(1)} %constant_dynamic-update-slice_fusion.refs_5_), channel_id=1, source_target_pairs={{0,16},{16,32},{32,48},{48,0},{1,17},{17,33},{33,49},{49,1},{2,18}... | collective-permute-start | bytes 1769480 | tf_op jit(solution)/shard_map/ppermute | solution.py:30
  35.7 16.8 %collective-permute-start.10 = (bf16[576,512]{1,0:T(8,128)(2,1)S(1)}, bf16[576,512]{1,0:T(8,128)(2,1)S(1)}, u32[]{:S(2)}, u32[]{:S(2)}) collective-permute-start(bf16[576,512]{1,0:T(8,128)(2,1)S(1)} %constant_dynamic-update-slice_fusion.refs_5_), channel_id=1, source_target_pairs={{0,48},{16,0},{32,16},{48,32},{1,49},{17,1},{33,17},{49,33},{2,50}... | collective-permute-start | bytes 1769480 | tf_op jit(solution)/shard_map/ppermute | solution.py:30
  39.0 11.6 %collective-permute-start.11 = (bf16[256,512]{1,0:T(8,128)(2,1)S(1)}, bf16[256,512]{1,0:T(8,128)(2,1)S(1)}, u32[]{:S(2)}, u32[]{:S(2)}) collective-permute-start(bf16[256,512]{1,0:T(8,128)(2,1)S(1)} %pad_maximum_fusion), channel_id=1, source_target_pairs={{0,64},{64,128},{128,192},{192,0},{1,65},{65,129},{129,193},{193,1... | collective-permute-start | bytes 786440 | tf_op jit(solution)/shard_map/ppermute | solution.py:30
  40.8 11.6 %collective-permute-start.12 = (bf16[256,512]{1,0:T(8,128)(2,1)S(1)}, bf16[256,512]{1,0:T(8,128)(2,1)S(1)}, u32[]{:S(2)}, u32[]{:S(2)}) collective-permute-start(bf16[256,512]{1,0:T(8,128)(2,1)S(1)} %pad_maximum_fusion), channel_id=1, source_target_pairs={{0,192},{64,0},{128,64},{192,128},{1,193},{65,1},{129,65},{193,129... | collective-permute-start | bytes 786440 | tf_op jit(solution)/shard_map/ppermute | solution.py:30
  52.5 16.2 %collective-permute-start.13 = (bf16[288,512]{1,0:T(8,128)(2,1)S(1)}, bf16[288,512]{1,0:T(8,128)(2,1)S(1)}, u32[]{:S(2)}, u32[]{:S(2)}) collective-permute-start(bf16[288,512]{1,0:T(8,128)(2,1)S(1)} %slice.61), channel_id=1, source_target_pairs={{0,16},{16,32},{32,48},{48,0},{1,17},{17,33},{33,49},{49,1},{2,18}... | collective-permute-start | bytes 884744 | tf_op jit(solution)/shard_map/ppermute | solution.py:30
  53.0 15.6 %collective-permute-start.14 = (bf16[288,512]{1,0:T(8,128)(2,1)S(1)}, bf16[288,512]{1,0:T(8,128)(2,1)S(1)}, u32[]{:S(2)}, u32[]{:S(2)}) collective-permute-start(bf16[288,512]{1,0:T(8,128)(2,1)S(1)} %slice.62), channel_id=1, source_target_pairs={{0,48},{16,0},{32,16},{48,32},{1,49},{17,1},{33,17},{49,33},{2,50}... | collective-permute-start | bytes 884744 | tf_op jit(solution)/shard_map/ppermute | solution.py:30
  56.1 12.5 %collective-permute-start.15 = (bf16[128,512]{1,0:T(8,128)(2,1)S(1)}, bf16[128,512]{1,0:T(8,128)(2,1)S(1)}, u32[]{:S(2)}, u32[]{:S(2)}) collective-permute-start(bf16[128,512]{1,0:T(8,128)(2,1)S(1)} %slice.63), channel_id=1, source_target_pairs={{0,64},{64,128},{128,192},{192,0},{1,65},{65,129},{129,193},{193,1... | collective-permute-start | bytes 393224 | tf_op jit(solution)/shard_map/ppermute | solution.py:30
  58.0 10.7 %collective-permute-start.16 = (bf16[128,512]{1,0:T(8,128)(2,1)S(1)}, bf16[128,512]{1,0:T(8,128)(2,1)S(1)}, u32[]{:S(2)}, u32[]{:S(2)}) collective-permute-start(bf16[128,512]{1,0:T(8,128)(2,1)S(1)} %slice.64), channel_id=1, source_target_pairs={{0,192},{64,0},{128,64},{192,128},{1,193},{65,1},{129,65},{193,129... | collective-permute-start | bytes 393224 | tf_op jit(solution)/shard_map/ppermute | solution.py:30
  97.9 15.2 %collective-permute-start.19 = (bf16[576,512]{1,0:T(8,128)(2,1)S(1)}, bf16[576,512]{1,0:T(8,128)(2,1)S(1)}, u32[]{:S(2)}, u32[]{:S(2)}) collective-permute-start(bf16[576,512]{1,0:T(8,128)(2,1)S(1)} %get-tuple-element.70), channel_id=1, source_target_pairs={{0,16},{16,32},{32,48},{48,0},{1,17},{17,33},{33,49},{49,1},{2,18}... | collective-permute-start | bytes 1769480 | tf_op jit(solution)/shard_map/ppermute | solution.py:30
  98.0 15.1 %collective-permute-start.20 = (bf16[576,512]{1,0:T(8,128)(2,1)S(1)}, bf16[576,512]{1,0:T(8,128)(2,1)S(1)}, u32[]{:S(2)}, u32[]{:S(2)}) collective-permute-start(bf16[576,512]{1,0:T(8,128)(2,1)S(1)} %get-tuple-element.71), channel_id=1, source_target_pairs={{0,48},{16,0},{32,16},{48,32},{1,49},{17,1},{33,17},{49,33},{2,50}... | collective-permute-start | bytes 1769480 | tf_op jit(solution)/shard_map/ppermute | solution.py:30
  101.2 15.3 %collective-permute-start.21 = (bf16[256,512]{1,0:T(8,128)(2,1)S(1)}, bf16[256,512]{1,0:T(8,128)(2,1)S(1)}, u32[]{:S(2)}, u32[]{:S(2)}) collective-permute-start(bf16[256,512]{1,0:T(8,128)(2,1)S(1)} %get-tuple-element.76), channel_id=1, source_target_pairs={{0,64},{64,128},{128,192},{192,0},{1,65},{65,129},{129,193},{193,1... | collective-permute-start | bytes 786440 | tf_op jit(solution)/shard_map/ppermute | solution.py:30
  101.7 14.9 %collective-permute-start.22 = (bf16[256,512]{1,0:T(8,128)(2,1)S(1)}, bf16[256,512]{1,0:T(8,128)(2,1)S(1)}, u32[]{:S(2)}, u32[]{:S(2)}) collective-permute-start(bf16[256,512]{1,0:T(8,128)(2,1)S(1)} %get-tuple-element.77), channel_id=1, source_target_pairs={{0,192},{64,0},{128,64},{192,128},{1,193},{65,1},{129,65},{193,129... | collective-permute-start | bytes 786440 | tf_op jit(solution)/shard_map/ppermute | solution.py:30
  113.3 15.4 %collective-permute-start.29 = (bf16[288,512]{1,0:T(8,128)(2,1)S(1)}, bf16[288,512]{1,0:T(8,128)(2,1)S(1)}, u32[]{:S(2)}, u32[]{:S(2)}) collective-permute-start(bf16[288,512]{1,0:T(8,128)(2,1)S(1)} %get-tuple-element.94), channel_id=1, source_target_pairs={{0,16},{16,32},{32,48},{48,0},{1,17},{17,33},{33,49},{49,1},{2,18}... | collective-permute-start | bytes 884744 | tf_op jit(solution)/shard_map/ppermute | solution.py:30
  113.4 15.3 %collective-permute-start.30 = (bf16[288,512]{1,0:T(8,128)(2,1)S(1)}, bf16[288,512]{1,0:T(8,128)(2,1)S(1)}, u32[]{:S(2)}, u32[]{:S(2)}) collective-permute-start(bf16[288,512]{1,0:T(8,128)(2,1)S(1)} %get-tuple-element.95), channel_id=1, source_target_pairs={{0,48},{16,0},{32,16},{48,32},{1,49},{17,1},{33,17},{49,33},{2,50}... | collective-permute-start | bytes 884744 | tf_op jit(solution)/shard_map/ppermute | solution.py:30
  116.7 8.6 %collective-permute-start.23 = (bf16[128,512]{1,0:T(8,128)(2,1)S(1)}, bf16[128,512]{1,0:T(8,128)(2,1)S(1)}, u32[]{:S(2)}, u32[]{:S(2)}) collective-permute-start(bf16[128,512]{1,0:T(8,128)(2,1)S(1)} %get-tuple-element.80), channel_id=1, source_target_pairs={{0,64},{64,128},{128,192},{192,0},{1,65},{65,129},{129,193},{193,1... | collective-permute-start | bytes 393224 | tf_op jit(solution)/shard_map/ppermute | solution.py:30
  117.4 7.8 %collective-permute-start.24 = (bf16[128,512]{1,0:T(8,128)(2,1)S(1)}, bf16[128,512]{1,0:T(8,128)(2,1)S(1)}, u32[]{:S(2)}, u32[]{:S(2)}) collective-permute-start(bf16[128,512]{1,0:T(8,128)(2,1)S(1)} %get-tuple-element.81), channel_id=1, source_target_pairs={{0,192},{64,0},{128,64},{192,128},{1,193},{65,1},{129,65},{193,129... | collective-permute-start | bytes 393224 | tf_op jit(solution)/shard_map/ppermute | solution.py:30
  125.4 7.7 %collective-permute-start.25 = (bf16[256,512]{1,0:T(8,128)(2,1)S(1)}, bf16[256,512]{1,0:T(8,128)(2,1)S(1)}, u32[]{:S(2)}, u32[]{:S(2)}) collective-permute-start(bf16[256,512]{1,0:T(8,128)(2,1)S(1)} %get-tuple-element.83), channel_id=1, source_target_pairs={{0,16},{16,32},{32,48},{48,0},{1,17},{17,33},{33,49},{49,1},{2,18}... | collective-permute-start | bytes 786440 | tf_op jit(solution)/shard_map/ppermute | solution.py:30
  125.5 7.7 %collective-permute-start.26 = (bf16[256,512]{1,0:T(8,128)(2,1)S(1)}, bf16[256,512]{1,0:T(8,128)(2,1)S(1)}, u32[]{:S(2)}, u32[]{:S(2)}) collective-permute-start(bf16[256,512]{1,0:T(8,128)(2,1)S(1)} %get-tuple-element.84), channel_id=1, source_target_pairs={{0,48},{16,0},{32,16},{48,32},{1,49},{17,1},{33,17},{49,33},{2,50}... | collective-permute-start | bytes 786440 | tf_op jit(solution)/shard_map/ppermute | solution.py:30
  128.9 10.8 %collective-permute-start.31 = (bf16[192,512]{1,0:T(8,128)(2,1)S(1)}, bf16[192,512]{1,0:T(8,128)(2,1)S(1)}, u32[]{:S(2)}, u32[]{:S(2)}) collective-permute-start(bf16[192,512]{1,0:T(8,128)(2,1)S(1)} %get-tuple-element.96), channel_id=1, source_target_pairs={{0,64},{64,128},{128,192},{192,0},{1,65},{65,129},{129,193},{193,1... | collective-permute-start | bytes 589832 | tf_op jit(solution)/shard_map/ppermute | solution.py:30
  131.9 7.9 %collective-permute-start.32 = (bf16[192,512]{1,0:T(8,128)(2,1)S(1)}, bf16[192,512]{1,0:T(8,128)(2,1)S(1)}, u32[]{:S(2)}, u32[]{:S(2)}) collective-permute-start(bf16[192,512]{1,0:T(8,128)(2,1)S(1)} %get-tuple-element.97), channel_id=1, source_target_pairs={{0,192},{64,0},{128,64},{192,128},{1,193},{65,1},{129,65},{193,129... | collective-permute-start | bytes 589832 | tf_op jit(solution)/shard_map/ppermute | solution.py:30
  133.2 11.4 %collective-permute-start.27 = (bf16[128,512]{1,0:T(8,128)(2,1)S(1)}, bf16[128,512]{1,0:T(8,128)(2,1)S(1)}, u32[]{:S(2)}, u32[]{:S(2)}) collective-permute-start(bf16[128,512]{1,0:T(8,128)(2,1)S(1)} %get-tuple-element.87), channel_id=1, source_target_pairs={{0,16},{16,32},{32,48},{48,0},{1,17},{17,33},{33,49},{49,1},{2,18}... | collective-permute-start | bytes 393224 | tf_op jit(solution)/shard_map/ppermute | solution.py:30
  133.3 11.3 %collective-permute-start.28 = (bf16[128,512]{1,0:T(8,128)(2,1)S(1)}, bf16[128,512]{1,0:T(8,128)(2,1)S(1)}, u32[]{:S(2)}, u32[]{:S(2)}) collective-permute-start(bf16[128,512]{1,0:T(8,128)(2,1)S(1)} %get-tuple-element.88), channel_id=1, source_target_pairs={{0,48},{16,0},{32,16},{48,32},{1,49},{17,1},{33,17},{49,33},{2,50}... | collective-permute-start | bytes 393224 | tf_op jit(solution)/shard_map/ppermute | solution.py:30
  139.8 7.6 %collective-permute-start.33 = (bf16[96,512]{1,0:T(8,128)(2,1)S(1)}, bf16[96,512]{1,0:T(8,128)(2,1)S(1)}, u32[]{:S(2)}, u32[]{:S(2)}) collective-permute-start(bf16[96,512]{1,0:T(8,128)(2,1)S(1)} %get-tuple-element.100), channel_id=1, source_target_pairs={{0,64},{64,128},{128,192},{192,0},{1,65},{65,129},{129,193},{193,1... | collective-permute-start | bytes 294920 | tf_op jit(solution)/shard_map/ppermute | solution.py:30
  (9 other events, 89.1 us)
where the time goes:
time: 152 us; the launch traced here: 150 us
  starting transfers between devices  63.4 us (42%)
  Pallas kernels  41.5 us (27%)
  waiting for transfers between devices  30.3 us (20%)
  blocking collectives  11.1 us (7%)
  local copies, waits for them, and re-layouts  1.83 us (1%)
    ppermute x35, starting transfers between devices, move(): return lax.ppermute(value, axis, [(i, (i + by) % n) for i in range(n)])  63.4 us
    pallas_call x5, Pallas kernels, block_call(): pl.pallas_call(body, out_shape=outs, in_specs=[pl.BlockSpec(memory_space=...  31.4 us
    ppermute x35, waiting for transfers between devices, move(): return lax.ppermute(value, axis, [(i, (i + by) % n) for i in range(n)])  30.3 us
    all_to_all x1, blocking collectives, shards(): lax.all_to_all(jnp.broadcast_to(stats[None], (8,) + stats.shape), TENSOR,...  11.1 us
    pallas_call x1, Pallas kernels, pick(): pl.pallas_call(body, out_shape=jax.ShapeDtypeStruct((n, TOK, WIDE), BF16)...  7.48 us
  transfers between devices with their start and end apart: 35, of which 11 were waited for; matrix products, arithmetic and copies ran while one was open for 1% of the time, Pallas kernels for 17%

commit v1 on v0

--- a/solution.py
+++ b/solution.py
@@ -52,7 +52,7 @@
     )(*args)
 
 
-def pick(hidden, at):
+def pick(hidden, at, mib):
     n = at.shape[0]
 
     def body(at_ref, h_ref, o_ref, arrived):
@@ -78,7 +78,7 @@
         ],
         out_specs=pl.BlockSpec(memory_space=pltpu.VMEM),
         scratch_shapes=[pltpu.SemaphoreType.DMA((n,))],
-        compiler_params=params(50),
+        compiler_params=params(mib),
         cost_estimate=pl.CostEstimate(
             flops=0, bytes_accessed=2 * n * TOK * WIDE * 2, transcendentals=0
         ),
@@ -86,15 +86,14 @@
 
 
 def block_call(compute, slots, outs, blocks, others, rows):
-    at, hidden, theirs = blocks
+    mine, theirs = blocks
     places = max(slots) + 1
 
-    def body(at_ref, h_ref, t_ref, *refs):
+    def body(m_ref, t_ref, *refs):
         hold, arrived = refs[-2:]
 
         def copies(place, slot):
-            start = pl.multiple_of(at_ref[slot] * WIDE, WIDE)
-            for side, ref in enumerate((h_ref.at[:, pl.ds(start, WIDE)], t_ref.at[slot])):
+            for side, ref in enumerate((m_ref.at[slot], t_ref.at[slot])):
                 yield pltpu.make_async_copy(
                     ref, hold.at[place, pl.ds(side * TOK, TOK)], arrived.at[place, side]
                 )
@@ -114,8 +113,7 @@
     return pl.pallas_call(
         body,
         out_shape=outs,
-        in_specs=[pl.BlockSpec(memory_space=pltpu.SMEM)]
-        + [pl.BlockSpec(memory_space=pl.ANY)] * 2
+        in_specs=[pl.BlockSpec(memory_space=pl.ANY)] * 2
         + [whole(o.shape) for o in others],
         out_specs=[whole(o.shape) for o in outs],
         scratch_shapes=[
@@ -128,7 +126,20 @@
             bytes_accessed=2 * len(slots) * TOK * WIDE * 2,
             transcendentals=0,
         ),
-    )(at, hidden, theirs, *others)
+    )(mine, theirs, *others)
+
+
+def logits_call(compute, blocks, others):
+    mine, theirs = blocks
+
+    def body(m_ref, t_ref, *refs):
+        def add(out, a, slot):
+            out[:, :TOK] += times(a, m_ref[slot])
+            out[:, TOK:] += times(a, t_ref[slot])
+
+        compute(add, refs[:-1], refs[-1])
+
+    return local_call(body, [LOGITS], mine, theirs, *others)[0]
 
 
 def times(a, block):
@@ -186,82 +197,66 @@
 def gathered_logits(head, hidden, at, sibling_at):
     zb, za = move(head[:PR], "zh", 1), move(head[:PR], "zh", -1)
     xb, xa = move(head, "x", 1), move(head, "x", -1)
-    picked = pick(hidden, sibling_at)
+    picked = pick(hidden, sibling_at, 50)
     zb, za, xb, xa, picked = lax.optimization_barrier((zb, za, xb, xa, picked))
     theirs = move(picked, "c", 1)
     zf1, zf2 = move(zb[:PH], "zh", 1), move(za[PH:], "zh", -1)
-    xf1, xf2 = move(xb[:RH], "x", 1), move(xa[RH:], "x", -1)
-    zf1, zf2, xf1, xf2 = lax.optimization_barrier((zf1, zf2, xf1, xf2))
+    xf1, xf2 = move(xb[PR : PR + QH], "x", 1), move(xa[PR + QH :], "x", -1)
     p = jnp.concatenate([za, zb, zf1, zf2], axis=0)
-    q = jnp.concatenate([head[PR:], xa[PR:], xb[PR:], xf2[PR - RH :]], axis=0)
+    q = jnp.concatenate([head[PR:], xa[PR:], xb[PR:], xf1, xf2], axis=0)
     pb, pa = move(p, "x", 1), move(p, "x", -1)
     qb, qa = move(q, "zh", 1), move(q, "zh", -1)
-    blocks = (at, hidden, theirs)
-
-    def first(block, refs, outs):
-        (out,) = outs
+    zf1, zf2, at = lax.optimization_barrier((zf1, zf2, at))
+    mine = pick(hidden, at, 40)
+    blocks = (mine, theirs)
+
+    def first(add, refs, out):
         head_ref, xa_ref, xb_ref, xf1_ref, xf2_ref, p_ref = refs
-        out[...] = times(head_ref[...], block(0))
-        out[...] += times(xa_ref[...], block(1))
-        out[...] += times(xb_ref[...], block(2))
-        far = block(3)
-        out[:RH, :] += times(xf1_ref[...], far)
-        out[RH:, :] += times(xf2_ref[...], far)
-
-        @pl.loop(0, 3)
-        def _(k):
-            out[:PR, :] += times(p_ref[rows_at(k, PR), :], block(4 + k))
-
-    slots = {0: 0, 1: 1, 2: 3, 3: 2} | {4 + k: 4 * dz for k, dz in enumerate(AHEAD)}
-    (total,) = block_call(
-        first, slots, [LOGITS], blocks, [head, xa, xb, xf1, xf2, p], 4 * ROWS + 3 * PR
-    )
+        out[...] = jnp.zeros_like(out)
+        add(out, head_ref[...], 0)
+        add(out, xa_ref[...], 1)
+        add(out, xb_ref[...], 3)
+        add(out.at[PR : PR + QH], xf1_ref[...], 2)
+        add(out.at[PR + QH :], xf2_ref[...], 2)
+        for k, dz in enumerate(AHEAD):
+            add(out.at[:PR], p_ref[k * PR : (k + 1) * PR, :], 4 * dz)
+
+    total = logits_call(first, blocks, [head, xa, xb, xf1, xf2, p])
     pb, pa, qb, qa, total = lax.optimization_barrier((pb, pa, qb, qa, total))
-    pf1, pf2 = move(pb[: 3 * PH], "x", 1), move(pa[3 * PH :], "x", -1)
+    pf1 = jnp.concatenate([pb[: 3 * PH], xb[:PH]], axis=0)
+    pf2 = jnp.concatenate([pa[3 * PH :], xa[PH:PR]], axis=0)
+    pf1, pf2 = move(pf1, "x", 1), move(pf2, "x", -1)
     qf1, qf2 = move(qb[: 2 * QR], "zh", 1), move(qa[2 * QR :], "zh", -1)
 
-    places = {4 * i + j: 4 * dz + dx for i, dz in enumerate(AHEAD) for j, dx in enumerate((0,) + AHEAD)}
-
-    def second(block, refs, outs):
-        (out,) = outs
+    def second(add, refs, out):
         pa_ref, pb_ref, qa_ref, qb_ref, total_ref = refs
         out[...] = total_ref[...]
-
-        @pl.loop(0, 3)
-        def _(k):
-            part = rows_at(k, PR)
-            out[:PR, :] += times(pa_ref[part, :], block(4 * k + 1))
-            out[:PR, :] += times(pb_ref[part, :], block(4 * k + 2))
-
-        for j in range(4):
-            new = j in (0, 3)
+        for k, dz in enumerate(AHEAD):
+            part = slice(k * PR, (k + 1) * PR)
+            add(out.at[:PR], pa_ref[part, :], 4 * dz + 1)
+            add(out.at[:PR], pb_ref[part, :], 4 * dz + 3)
+        for j, dx in enumerate((0,) + AHEAD):
             part = slice(j * QR, (j + 1) * QR)
-            out[PR:, :] += times(qa_ref[part, :], block(j, new))
-            out[PR:, :] += times(qb_ref[part, :], block(4 + j, new))
-
-    slots = {k: v for k, v in places.items() if k not in (8, 11)}
-    (total,) = block_call(
-        second, slots, [LOGITS], blocks, [pa, pb, qa, qb, total], 6 * PR + 8 * QR
-    )
-
-    def third(block, refs, outs):
-        (out,) = outs
+            add(out.at[PR:], qa_ref[part, :], 4 + dx)
+            add(out.at[PR:], qb_ref[part, :], 12 + dx)
+
+    total = logits_call(second, blocks, [pa, pb, qa, qb, total])
+
+    def third(add, refs, out):
         pf1_ref, pf2_ref, qf1_ref, qf2_ref, total_ref = refs
         out[...] = total_ref[...]
-        out[:PR, :] += times(pf1_ref[:PR, :], block(3))
-        middle = block(7)
-        out[:PH, :] += times(pf1_ref[PR:, :], middle)
-        out[PH:PR, :] += times(pf2_ref[:PH, :], middle)
-        out[:PR, :] += times(pf2_ref[PH:, :], block(11))
-        out[PR:, :] += times(qf1_ref[:QR, :], block(8))
-        out[PR:, :] += times(qf1_ref[QR:, :], block(9))
-        out[PR:, :] += times(qf2_ref[:QR, :], block(10))
-        out[PR:, :] += times(qf2_ref[QR:, :], block(11, False))
-
-    slots = {k: places[k] for k in (3, 7, 8, 9, 10, 11)}
-    (total,) = block_call(
-        third, slots, [LOGITS], blocks, [pf1, pf2, qf1, qf2, total], 3 * PR + 4 * QR
-    )
+        add(out.at[:PR], pf1_ref[:PR, :], 4 + 2)
+        add(out.at[:PH], pf1_ref[PR : 3 * PH, :], 12 + 2)
+        add(out.at[PH:PR], pf2_ref[:PH, :], 12 + 2)
+        add(out.at[:PR], pf2_ref[PH : 3 * PH, :], 8 + 2)
+        add(out.at[:PH], pf1_ref[3 * PH :, :], 2)
+        add(out.at[PH:PR], pf2_ref[3 * PH :, :], 2)
+        add(out.at[PR:], qf1_ref[:QR, :], 8)
+        add(out.at[PR:], qf1_ref[QR:, :], 8 + 1)
+        add(out.at[PR:], qf2_ref[:QR, :], 8 + 3)
+        add(out.at[PR:], qf2_ref[QR:, :], 8 + 2)
+
+    total = logits_call(third, blocks, [pf1, pf2, qf1, qf2, total])
     return total, blocks
 
 
@@ -341,8 +336,9 @@
     )
     p_up, p_down, own, q_here = lax.optimization_barrier((p_up, p_down, own, q_here))
 
-    def forward(kept_ahead, kept_behind, up, down, n, half):
-        def body(a, b, u, d, up_out, down_out):
+    def forward(kept_ahead, kept_behind, up, down, n, half, *after):
+        def body(a, b, u, d, *rest):
+            up_out, down_out = rest[-2:]
             for k in range(n):
                 to, first, last = k * half, 2 * k * half, (2 * k + 1) * half
                 up_out[to : to + half, :] = (
@@ -353,7 +349,7 @@
                 ).astype(BF16)
 
         return local_call(
-            body, [array(n * half, BF16)] * 2, kept_ahead, kept_behind, up, down
+            body, [array(n * half, BF16)] * 2, kept_ahead, kept_behind, up, down, *after
         )
 
     def settle(kept, up, down, up2, down2, n, half, k):
@@ -388,9 +384,10 @@
         [array(PR, BF16), array(PR, BF16), array(PH, F32), array(PH, F32)],
         p_here, p_up, p_down, p_up2, p_down2,
     )
+    p_sent = z_up
     z_up, z_down = move(z_up, "zh", 1), move(z_down, "zh", -1)
 
-    def q_body(own, kept, up, down, up2, down2, up_out, down_out, ahead, behind, here):
+    def q_body(own, kept, up, down, up2, down2, _, up_out, down_out, ahead, behind, here):
         rest = PR - RH
         for dx in range(4):
             one, two = settle(kept, up, down, up2, down2, 4, QH, dx)
@@ -411,13 +408,13 @@
     x_up, x_down, x_ahead, x_behind, x_here = local_call(
         q_body,
         [array(ROWS, BF16), array(ROWS, BF16), array(RH, F32), array(RH, F32), array(ROWS, F32)],
-        own, q_here, q_up, q_down, q_up2, q_down2,
+        own, q_here, q_up, q_down, q_up2, q_down2, p_sent,
     )
     x_up, x_down = move(x_up, "x", 1), move(x_down, "x", -1)
 
     z_up2, z_down2 = forward(z_ahead, z_behind, z_up, z_down, 1, PH)
+    x_up2, x_down2 = forward(x_ahead, x_behind, x_up, x_down, 1, RH, z_up2)
     z_up2, z_down2 = move(z_up2, "zh", 1), move(z_down2, "zh", -1)
-    x_up2, x_down2 = forward(x_ahead, x_behind, x_up, x_down, 1, RH)
     x_up2, x_down2 = move(x_up2, "x", 1), move(x_down2, "x", -1)
 
     def last_body(here, xu, xd, xu2, xd2, zu, zd, zu2, zd2, out):

time: 152 us -> 146 us (0.961)
  Pallas kernels: 41.5 us -> 36 us
  waiting for transfers between devices: 30.3 us -> 33 us
  starting transfers between devices: 63.4 us -> 61.1 us
    pallas_call x5 -> x2, Pallas kernels: 31.4 us -> 11.2 us  [block_call(): pl.pallas_call(body, out_shape=outs, in_specs=[pl.BlockSpec(memory_space=...]
    pallas_call x9 -> x12, Pallas kernels: 2.57 us -> 13.1 us  [local_call(): pl.pallas_call(body, out_shape=outs, in_specs=[whole(a.shape) for a in ar...]
    pallas_call x1 -> x2, Pallas kernels: 7.48 us -> 11.7 us  [pick(): pl.pallas_call(body, out_shape=jax.ShapeDtypeStruct((n, TOK, WIDE), BF16)...]
    ppermute x35, waiting for transfers between devices: 30.3 us -> 33 us  [move(): return lax.ppermute(value, axis, [(i, (i + by) % n) for i in range(n)])]
    ppermute x35, starting transfers between devices: 63.4 us -> 61.1 us  [move(): return lax.ppermute(value, axis, [(i, (i + by) % n) for i in range(n)])]
  transfers between devices with their start and end apart: 35 -> 35, of which waited for: 11 -> 15; matrix products, arithmetic and copies ran while one was open for 1% -> 1% of each run, Pallas kernels for 17% -> 16%
where the time goes in v1:
time: 146 us; the launch traced here: 143 us
  starting transfers between devices  61.1 us (42%)
  Pallas kernels  36 us (25%)
  waiting for transfers between devices  33 us (23%)
  blocking collectives  10.1 us (7%)
  local copies, waits for them, and re-layouts  1.84 us (1%)
    ppermute x35, starting transfers between devices, move(): return lax.ppermute(value, axis, [(i, (i + by) % n) for i in range(n)])  61.1 us
    ppermute x35, waiting for transfers between devices, move(): return lax.ppermute(value, axis, [(i, (i + by) % n) for i in range(n)])  33 us
    pallas_call x12, Pallas kernels, local_call(): pl.pallas_call(body, out_shape=outs, in_specs=[whole(a.shape) for a in ar...  13.1 us
    pallas_call x2, Pallas kernels, pick(): pl.pallas_call(body, out_shape=jax.ShapeDtypeStruct((n, TOK, WIDE), BF16)...  11.7 us
    pallas_call x2, Pallas kernels, block_call(): pl.pallas_call(body, out_shape=outs, in_specs=[pl.BlockSpec(memory_space=...  11.2 us
    all_to_all x1, blocking collectives, shards(): lax.all_to_all(jnp.broadcast_to(stats[None], (8,) + stats.shape), TENSOR,...  10.1 us
  transfers between devices with their start and end apart: 35, of which 15 were waited for; matrix products, arithmetic and copies ran while one was open for 1% of the time, Pallas kernels for 16%

profile of v1, /device:TPU:8, one launch (start us, length us, event | category | flops | bytes accessed | tf_op | source)
XLA Modules:
  0.0 143.5 jit_solution(5252329786893331491)
XLA Ops:
  4.9 3.3 %collective-permute-start = (bf16[192,512]{1,0:T(8,128)(2,1)S(1)}, bf16[192,512]{1,0:T(8,128)(2,1)S(1)}, u32[]{:S(2)}, u32[]{:S(2)}) collective-permute-start(bf16[192,512]{1,0:T(8,128)(2,1)S(1)} %slice.55), channel_id=1, source_target_pairs={{0,64},{64,128},{128,192},{192,0},{1,65},{65,129},{129,193},{193,1... | collective-permute-start | bytes 589832 | tf_op jit(solution)/shard_map/ppermute | solution.py:30
  8.3 3.1 %collective-permute-start.1 = (bf16[192,512]{1,0:T(8,128)(2,1)S(1)}, bf16[192,512]{1,0:T(8,128)(2,1)S(1)}, u32[]{:S(2)}, u32[]{:S(2)}) collective-permute-start(bf16[192,512]{1,0:T(8,128)(2,1)S(1)} %slice.55), channel_id=1, source_target_pairs={{0,192},{64,0},{128,64},{192,128},{1,193},{65,1},{129,65},{193,129... | collective-permute-start | bytes 589832 | tf_op jit(solution)/shard_map/ppermute | solution.py:30
  11.4 7.5 %shard_map.77 = bf16[16,512,512]{2,1,0:T(8,128)(2,1)} custom-call(s32[16]{0:T(128)S(1)} %broadcast_add_fusion.1.at_ref, bf16[512,16384]{1,0:T(8,128)(2,1)} %h_ref.3), custom_call_target="tpu_custom_call" | custom-call | bytes 16777216 | tf_op jit(solution)/shard_map/pallas_call | solution.py:72
  18.9 2.1 %collective-permute-done.1 = bf16[192,512]{1,0:T(8,128)(2,1)S(1)} collective-permute-done((bf16[192,512]{1,0:T(8,128)(2,1)S(1)}, bf16[192,512]{1,0:T(8,128)(2,1)S(1)}, u32[]{:S(2)}, u32[]{:S(2)}) %collective-permute-start.1) | collective-permute-done | bytes 196640 | tf_op jit(solution)/shard_map/ppermute | solution.py:30
  21.1 3.7 %collective-permute-start.4 = (bf16[96,512]{1,0:T(8,128)(2,1)S(1)}, bf16[96,512]{1,0:T(8,128)(2,1)S(1)}, u32[]{:S(2)}, u32[]{:S(2)}) collective-permute-start(bf16[96,512]{1,0:T(8,128)(2,1)S(1)} %slice.56), channel_id=1, source_target_pairs={{0,64},{64,128},{128,192},{192,0},{1,65},{65,129},{129,193},{193,1... | collective-permute-start | bytes 294920 | tf_op jit(solution)/shard_map/ppermute | solution.py:30
  27.5 2.0 %collective-permute-done.4 = bf16[96,512]{1,0:T(8,128)(2,1)S(1)} collective-permute-done((bf16[96,512]{1,0:T(8,128)(2,1)S(1)}, bf16[96,512]{1,0:T(8,128)(2,1)S(1)}, u32[]{:S(2)}, u32[]{:S(2)}) %collective-permute-start.4) | collective-permute-done | bytes 98336 | tf_op jit(solution)/shard_map/ppermute | solution.py:30
  29.5 3.1 %collective-permute-done.5 = bf16[96,512]{1,0:T(8,128)(2,1)S(1)} collective-permute-done((bf16[96,512]{1,0:T(8,128)(2,1)S(1)}, bf16[96,512]{1,0:T(8,128)(2,1)S(1)}, u32[]{:S(2)}, u32[]{:S(2)}) %collective-permute-start.5) | collective-permute-done | bytes 98336 | tf_op jit(solution)/shard_map/ppermute | solution.py:30
  32.9 3.0 %collective-permute-start.8 = (bf16[576,512]{1,0:T(8,128)(2,1)S(1)}, bf16[576,512]{1,0:T(8,128)(2,1)S(1)}, u32[]{:S(2)}, u32[]{:S(2)}) collective-permute-start(bf16[576,512]{1,0:T(8,128)(2,1)S(1)} %constant_dynamic-update-slice_fusion.refs_5_), channel_id=1, source_target_pairs={{0,48},{16,0},{32,16},{48,32},{1,49},{17,1},{33,17},{49,33},{2,50}... | collective-permute-start | bytes 1769480 | tf_op jit(solution)/shard_map/ppermute | solution.py:30
  36.8 3.4 %collective-permute-start.12 = (bf16[256,512]{1,0:T(8,128)(2,1)S(1)}, bf16[256,512]{1,0:T(8,128)(2,1)S(1)}, u32[]{:S(2)}, u32[]{:S(2)}) collective-permute-start(bf16[256,512]{1,0:T(8,128)(2,1)S(1)} %constant_dynamic-update-slice_fusion.4), channel_id=1, source_target_pairs={{0,192},{64,0},{128,64},{192,128},{1,193},{65,1},{129,65},{193,129... | collective-permute-start | bytes 786440 | tf_op jit(solution)/shard_map/ppermute | solution.py:30
  40.2 4.2 %shard_map.78.m_ref = bf16[16,512,512]{2,1,0:T(8,128)(2,1)S(1)} custom-call(s32[16]{0:T(128)S(1)} %broadcast_add_fusion.at_ref, bf16[512,16384]{1,0:T(8,128)(2,1)} %h_ref.3), custom_call_target="tpu_custom_call" | custom-call | bytes 16777216 | tf_op jit(solution)/shard_map/pallas_call | solution.py:72
  44.4 2.6 %shard_map.79.refs_4_ = f32[256,1024]{1,0:T(8,128)S(1)} custom-call(bf16[16,512,512]{2,1,0:T(8,128)(2,1)S(1)} %shard_map.78.m_ref, bf16[16,512,512]{2,1,0:T(8,128)(2,1)S(1)} %collective-permute-done.6.t_ref, bf16[256,512]{1,0:T(8,128)(2,1)S(1)} %copy-done.3, bf16[256,512]{1,0:T(8,128)(2,1)S(1)} %collective-permute-done.3.refs_1_, ...), custom_call_target="tpu_custom_call" | custom-call | bytes 19267584 | tf_op jit(solution)/shard_map/pallas_call | solution.py:45
  49.6 2.6 %collective-permute-start.14 = (bf16[384,512]{1,0:T(8,128)(2,1)S(1)}, bf16[384,512]{1,0:T(8,128)(2,1)S(1)}, u32[]{:S(2)}, u32[]{:S(2)}) collective-permute-start(bf16[384,512]{1,0:T(8,128)(2,1)S(1)} %pad_maximum_fusion.1), channel_id=1, source_target_pairs={{0,48},{16,0},{32,16},{48,32},{1,49},{17,1},{33,17},{49,33},{2,50}... | collective-permute-start | bytes 1179656 | tf_op jit(solution)/shard_map/ppermute | solution.py:30
  53.7 3.0 %collective-permute-start.16 = (bf16[128,512]{1,0:T(8,128)(2,1)S(1)}, bf16[128,512]{1,0:T(8,128)(2,1)S(1)}, u32[]{:S(2)}, u32[]{:S(2)}) collective-permute-start(bf16[128,512]{1,0:T(8,128)(2,1)S(1)} %slice.68), channel_id=1, source_target_pairs={{0,192},{64,0},{128,64},{192,128},{1,193},{65,1},{129,65},{193,129... | collective-permute-start | bytes 393224 | tf_op jit(solution)/shard_map/ppermute | solution.py:30
  56.7 4.6 %shard_map.80.refs_4_ = f32[256,1024]{1,0:T(8,128)S(1)} custom-call(bf16[16,512,512]{2,1,0:T(8,128)(2,1)S(1)} %shard_map.78.m_ref, bf16[16,512,512]{2,1,0:T(8,128)(2,1)S(1)} %collective-permute-done.6.t_ref, bf16[576,512]{1,0:T(8,128)(2,1)S(1)} %collective-permute-done.8.refs_0_, bf16[576,512]{1,0:T(8,128)(2,1)S(1)} %collective-permute-done.7.refs_1_, ...), custom_call_target="tpu_custom_call" | custom-call | bytes 20578304 | tf_op jit(solution)/shard_map/pallas_call | solution.py:45
  62.9 3.3 %shard_map.81.mine = f32[256,1024]{1,0:T(8,128)S(1)} custom-call(bf16[16,512,512]{2,1,0:T(8,128)(2,1)S(1)} %shard_map.78.m_ref, bf16[16,512,512]{2,1,0:T(8,128)(2,1)S(1)} %collective-permute-done.6.t_ref, bf16[384,512]{1,0:T(8,128)(2,1)S(1)} %collective-permute-done.13.refs_0_, bf16[384,512]{1,0:T(8,128)(2,1)S(1)} %collective-permute-done.14.refs_1_, ...), custom_call_target="tpu_custom_call" | custom-call | bytes 19922944 | tf_op jit(solution)/shard_map/pallas_call | solution.py:45
  67.1 1.9 %collective-permute-done.18 = f32[3,512]{1,0:T(4,128)S(1)} collective-permute-done((f32[3,512]{1,0:T(4,128)S(1)}, f32[3,512]{1,0:T(4,128)S(1)}, u32[]{:S(2)}, u32[]{:S(2)}) %collective-permute-start.18) | collective-permute-done | bytes 6176 | tf_op jit(solution)/shard_map/ppermute | solution.py:30
  69.9 10.1 %all_to_all.5 = f32[8,3,1024]{2,1,0:T(4,128)S(1)} all-to-all(f32[8,3,1024]{2,1,0:T(4,128)S(1)} %broadcast_in_dim.2), channel_id=1, replica_groups=mesh['zh'=4,'x'=4,'c'=2,'zl'=2,'y'=4] {'zl','y'}, dimensions={0} | all-to-all | bytes 196608 | tf_op jit(solution)/shard_map/all_to_all | solution.py:453
  80.4 8.1 %shard_map.84 = (bf16[576,512]{1,0:T(8,128)(2,1)S(1)}, bf16[576,512]{1,0:T(8,128)(2,1)S(1)}, bf16[256,512]{1,0:T(8,128)(2,1)S(1)}, bf16[256,512]{1,0:T(8,128)(2,...) custom-call(bf16[16,512,512]{2,1,0:T(8,128)(2,1)} %copy-done, ...), custom_call_target="tpu_custom_call" | custom-call | flops 3221225472 | bytes 12582912 | tf_op jit(solution)/shard_map/pallas_call | solution.py:113
  88.6 3.2 %collective-permute-start.20 = (bf16[576,512]{1,0:T(8,128)(2,1)S(1)}, bf16[576,512]{1,0:T(8,128)(2,1)S(1)}, u32[]{:S(2)}, u32[]{:S(2)}) collective-permute-start(bf16[576,512]{1,0:T(8,128)(2,1)S(1)} %get-tuple-element.65), channel_id=1, source_target_pairs={{0,48},{16,0},{32,16},{48,32},{1,49},{17,1},{33,17},{49,33},{2,50}... | collective-permute-start | bytes 1769480 | tf_op jit(solution)/shard_map/ppermute | solution.py:30
  91.8 2.2 %collective-permute-start.21 = (bf16[256,512]{1,0:T(8,128)(2,1)S(1)}, bf16[256,512]{1,0:T(8,128)(2,1)S(1)}, u32[]{:S(2)}, u32[]{:S(2)}) collective-permute-start(bf16[256,512]{1,0:T(8,128)(2,1)S(1)} %get-tuple-element.70), channel_id=1, source_target_pairs={{0,64},{64,128},{128,192},{192,0},{1,65},{65,129},{129,193},{193,1... | collective-permute-start | bytes 786440 | tf_op jit(solution)/shard_map/ppermute | solution.py:30
  95.9 3.1 %shard_map.85 = (f32[768,512]{1,0:T(8,128)S(1)}, f32[256,512]{1,0:T(8,128)S(1)}) custom-call(bf16[16,512,512]{2,1,0:T(8,128)(2,1)} %copy-done, bf16[16,512,512]{2,1,0:T(8,128)(2,1)} %copy-done.1, bf16[256,1024]{1,0:T(8,128)(2,1)S(1)} %get-tuple-element.63.refs_0_), custom_call_target="tpu_custom_call" | custom-call | flops 1073741824 | bytes 4194304 | tf_op jit(solution)/shard_map/pallas_call | solution.py:113
  99.0 4.7 %collective-permute-done.19.u.up = bf16[576,512]{1,0:T(8,128)(2,1)S(1)} collective-permute-done((bf16[576,512]{1,0:T(8,128)(2,1)S(1)}, bf16[576,512]{1,0:T(8,128)(2,1)S(1)}, u32[]{:S(2)}, u32[]{:S(2)}) %collective-permute-start.19) | collective-permute-done | bytes 589856 | tf_op jit(solution)/shard_map/ppermute | solution.py:30
  103.9 3.2 %collective-permute-start.26 = (bf16[288,512]{1,0:T(8,128)(2,1)S(1)}, bf16[288,512]{1,0:T(8,128)(2,1)S(1)}, u32[]{:S(2)}, u32[]{:S(2)}) collective-permute-start(bf16[288,512]{1,0:T(8,128)(2,1)S(1)} %get-tuple-element.82), channel_id=1, source_target_pairs={{0,48},{16,0},{32,16},{48,32},{1,49},{17,1},{33,17},{49,33},{2,50}... | collective-permute-start | bytes 884744 | tf_op jit(solution)/shard_map/ppermute | solution.py:30
  107.2 2.3 %collective-permute-start.23 = (bf16[128,512]{1,0:T(8,128)(2,1)S(1)}, bf16[128,512]{1,0:T(8,128)(2,1)S(1)}, u32[]{:S(2)}, u32[]{:S(2)}) collective-permute-start(bf16[128,512]{1,0:T(8,128)(2,1)S(1)} %get-tuple-element.74), channel_id=1, source_target_pairs={{0,64},{64,128},{128,192},{192,0},{1,65},{65,129},{129,193},{193,1... | collective-permute-start | bytes 393224 | tf_op jit(solution)/shard_map/ppermute | solution.py:30
  109.5 1.9 %collective-permute-start.24 = (bf16[128,512]{1,0:T(8,128)(2,1)S(1)}, bf16[128,512]{1,0:T(8,128)(2,1)S(1)}, u32[]{:S(2)}, u32[]{:S(2)}) collective-permute-start(bf16[128,512]{1,0:T(8,128)(2,1)S(1)} %get-tuple-element.75), channel_id=1, source_target_pairs={{0,192},{64,0},{128,64},{192,128},{1,193},{65,1},{129,65},{193,129... | collective-permute-start | bytes 393224 | tf_op jit(solution)/shard_map/ppermute | solution.py:30
  112.0 3.3 %collective-permute-done.23.up2 = bf16[128,512]{1,0:T(8,128)(2,1)S(1)} collective-permute-done((bf16[128,512]{1,0:T(8,128)(2,1)S(1)}, bf16[128,512]{1,0:T(8,128)(2,1)S(1)}, u32[]{:S(2)}, u32[]{:S(2)}) %collective-permute-start.23) | collective-permute-done | bytes 131104 | tf_op jit(solution)/shard_map/ppermute | solution.py:30
  117.0 3.2 %collective-permute-start.28 = (bf16[256,512]{1,0:T(8,128)(2,1)S(1)}, bf16[256,512]{1,0:T(8,128)(2,1)S(1)}, u32[]{:S(2)}, u32[]{:S(2)}) collective-permute-start(bf16[256,512]{1,0:T(8,128)(2,1)S(1)} %get-tuple-element.86), channel_id=1, source_target_pairs={{0,48},{16,0},{32,16},{48,32},{1,49},{17,1},{33,17},{49,33},{2,50}... | collective-permute-start | bytes 786440 | tf_op jit(solution)/shard_map/ppermute | solution.py:30
  120.3 3.0 %collective-permute-start.29 = (bf16[192,512]{1,0:T(8,128)(2,1)S(1)}, bf16[192,512]{1,0:T(8,128)(2,1)S(1)}, u32[]{:S(2)}, u32[]{:S(2)}) collective-permute-start(bf16[192,512]{1,0:T(8,128)(2,1)S(1)} %get-tuple-element.83._), channel_id=1, source_target_pairs={{0,64},{64,128},{128,192},{192,0},{1,65},{65,129},{129,193},{193,1... | collective-permute-start | bytes 589832 | tf_op jit(solution)/shard_map/ppermute | solution.py:30
  124.4 6.0 %collective-permute-done.29.u.zu = bf16[192,512]{1,0:T(8,128)(2,1)S(1)} collective-permute-done((bf16[192,512]{1,0:T(8,128)(2,1)S(1)}, bf16[192,512]{1,0:T(8,128)(2,1)S(1)}, u32[]{:S(2)}, u32[]{:S(2)}) %collective-permute-start.29) | collective-permute-done | bytes 196640 | tf_op jit(solution)/shard_map/ppermute | solution.py:30
  132.1 3.2 %collective-permute-start.32 = (bf16[128,512]{1,0:T(8,128)(2,1)S(1)}, bf16[128,512]{1,0:T(8,128)(2,1)S(1)}, u32[]{:S(2)}, u32[]{:S(2)}) collective-permute-start(bf16[128,512]{1,0:T(8,128)(2,1)S(1)} %get-tuple-element.94), channel_id=1, source_target_pairs={{0,48},{16,0},{32,16},{48,32},{1,49},{17,1},{33,17},{49,33},{2,50}... | collective-permute-start | bytes 393224 | tf_op jit(solution)/shard_map/ppermute | solution.py:30
  136.6 2.9 %collective-permute-start.34 = (bf16[96,512]{1,0:T(8,128)(2,1)S(1)}, bf16[96,512]{1,0:T(8,128)(2,1)S(1)}, u32[]{:S(2)}, u32[]{:S(2)}) collective-permute-start(bf16[96,512]{1,0:T(8,128)(2,1)S(1)} %get-tuple-element.95), channel_id=1, source_target_pairs={{0,192},{64,0},{128,64},{192,128},{1,193},{65,1},{129,65},{193,129... | collective-permute-start | bytes 294920 | tf_op jit(solution)/shard_map/ppermute | solution.py:30
  140.1 2.0 %collective-permute-done.33.zu2 = bf16[96,512]{1,0:T(8,128)(2,1)S(1)} collective-permute-done((bf16[96,512]{1,0:T(8,128)(2,1)S(1)}, bf16[96,512]{1,0:T(8,128)(2,1)S(1)}, u32[]{:S(2)}, u32[]{:S(2)}) %collective-permute-start.33) | collective-permute-done | bytes 98336 | tf_op jit(solution)/shard_map/ppermute | solution.py:30
  (105 shorter events, 26.4 us)
Async XLA Ops:
  0.6 20.4 %collective-permute-start.2 = (bf16[256,512]{1,0:T(8,128)(2,1)}, bf16[256,512]{1,0:T(8,128)(2,1)S(1)}, u32[]{:S(2)}, u32[]{:S(2)}) collective-permute-start(bf16[256,512]{1,0:T(8,128)(2,1)} %refs_0_.1), channel_id=1, source_target_pairs={{0,16},{16,32},{32,48},{48,0},{1,17},{17,33},{33,49},{49,1},{2,18}... | collective-permute-start | bytes 786440 | tf_op jit(solution)/shard_map/ppermute | solution.py:30
  2.2 18.8 %collective-permute-start.3 = (bf16[256,512]{1,0:T(8,128)(2,1)}, bf16[256,512]{1,0:T(8,128)(2,1)S(1)}, u32[]{:S(2)}, u32[]{:S(2)}) collective-permute-start(bf16[256,512]{1,0:T(8,128)(2,1)} %refs_0_.1), channel_id=1, source_target_pairs={{0,48},{16,0},{32,16},{48,32},{1,49},{17,1},{33,17},{49,33},{2,50}... | collective-permute-start | bytes 786440 | tf_op jit(solution)/shard_map/ppermute | solution.py:30
  4.9 14.0 %collective-permute-start = (bf16[192,512]{1,0:T(8,128)(2,1)S(1)}, bf16[192,512]{1,0:T(8,128)(2,1)S(1)}, u32[]{:S(2)}, u32[]{:S(2)}) collective-permute-start(bf16[192,512]{1,0:T(8,128)(2,1)S(1)} %slice.55), channel_id=1, source_target_pairs={{0,64},{64,128},{128,192},{192,0},{1,65},{65,129},{129,193},{193,1... | collective-permute-start | bytes 589832 | tf_op jit(solution)/shard_map/ppermute | solution.py:30
  8.3 12.8 %collective-permute-start.1 = (bf16[192,512]{1,0:T(8,128)(2,1)S(1)}, bf16[192,512]{1,0:T(8,128)(2,1)S(1)}, u32[]{:S(2)}, u32[]{:S(2)}) collective-permute-start(bf16[192,512]{1,0:T(8,128)(2,1)S(1)} %slice.55), channel_id=1, source_target_pairs={{0,192},{64,0},{128,64},{192,128},{1,193},{65,1},{129,65},{193,129... | collective-permute-start | bytes 589832 | tf_op jit(solution)/shard_map/ppermute | solution.py:30
  21.0 23.4 %collective-permute-start.6 = (bf16[16,512,512]{2,1,0:T(8,128)(2,1)}, bf16[16,512,512]{2,1,0:T(8,128)(2,1)S(1)}, u32[]{:S(2)}, u32[]{:S(2)}) collective-permute-start(bf16[16,512,512]{2,1,0:T(8,128)(2,1)} %shard_map.77), channel_id=1, source_target_pairs={{0,8},{8,0},{1,9},{9,1},{2,10},{10,2},{3,11},{11,3},{4,12},{12,4},... | collective-permute-start | bytes 25165832 | tf_op jit(solution)/shard_map/ppermute | solution.py:30
  21.1 8.4 %collective-permute-start.4 = (bf16[96,512]{1,0:T(8,128)(2,1)S(1)}, bf16[96,512]{1,0:T(8,128)(2,1)S(1)}, u32[]{:S(2)}, u32[]{:S(2)}) collective-permute-start(bf16[96,512]{1,0:T(8,128)(2,1)S(1)} %slice.56), channel_id=1, source_target_pairs={{0,64},{64,128},{128,192},{192,0},{1,65},{65,129},{129,193},{193,1... | collective-permute-start | bytes 294920 | tf_op jit(solution)/shard_map/ppermute | solution.py:30
  24.8 7.7 %collective-permute-start.5 = (bf16[96,512]{1,0:T(8,128)(2,1)S(1)}, bf16[96,512]{1,0:T(8,128)(2,1)S(1)}, u32[]{:S(2)}, u32[]{:S(2)}) collective-permute-start(bf16[96,512]{1,0:T(8,128)(2,1)S(1)} %slice.57), channel_id=1, source_target_pairs={{0,192},{64,0},{128,64},{192,128},{1,193},{65,1},{129,65},{193,129... | collective-permute-start | bytes 294920 | tf_op jit(solution)/shard_map/ppermute | solution.py:30
  25.4 10.5 %collective-permute-start.10 = (bf16[32,512]{1,0:T(8,128)(2,1)S(1)}, bf16[32,512]{1,0:T(8,128)(2,1)S(1)}, u32[]{:S(2)}, u32[]{:S(2)}) collective-permute-start(bf16[32,512]{1,0:T(8,128)(2,1)S(1)} %slice.62), channel_id=1, source_target_pairs={{0,48},{16,0},{32,16},{48,32},{1,49},{17,1},{33,17},{49,33},{2,50}... | collective-permute-start | bytes 98312 | tf_op jit(solution)/shard_map/ppermute | solution.py:30
  26.9 9.0 %collective-permute-start.9 = (bf16[32,512]{1,0:T(8,128)(2,1)S(1)}, bf16[32,512]{1,0:T(8,128)(2,1)S(1)}, u32[]{:S(2)}, u32[]{:S(2)}) collective-permute-start(bf16[32,512]{1,0:T(8,128)(2,1)S(1)} %slice.61), channel_id=1, source_target_pairs={{0,16},{16,32},{32,48},{48,0},{1,17},{17,33},{33,49},{49,1},{2,18}... | collective-permute-start | bytes 98312 | tf_op jit(solution)/shard_map/ppermute | solution.py:30
  32.6 17.0 %collective-permute-start.7 = (bf16[576,512]{1,0:T(8,128)(2,1)S(1)}, bf16[576,512]{1,0:T(8,128)(2,1)S(1)}, u32[]{:S(2)}, u32[]{:S(2)}) collective-permute-start(bf16[576,512]{1,0:T(8,128)(2,1)S(1)} %constant_dynamic-update-slice_fusion.refs_5_), channel_id=1, source_target_pairs={{0,16},{16,32},{32,48},{48,0},{1,17},{17,33},{33,49},{49,1},{2,18}... | collective-permute-start | bytes 1769480 | tf_op jit(solution)/shard_map/ppermute | solution.py:30
  32.9 16.6 %collective-permute-start.8 = (bf16[576,512]{1,0:T(8,128)(2,1)S(1)}, bf16[576,512]{1,0:T(8,128)(2,1)S(1)}, u32[]{:S(2)}, u32[]{:S(2)}) collective-permute-start(bf16[576,512]{1,0:T(8,128)(2,1)S(1)} %constant_dynamic-update-slice_fusion.refs_5_), channel_id=1, source_target_pairs={{0,48},{16,0},{32,16},{48,32},{1,49},{17,1},{33,17},{49,33},{2,50}... | collective-permute-start | bytes 1769480 | tf_op jit(solution)/shard_map/ppermute | solution.py:30
  35.9 12.5 %collective-permute-start.11 = (bf16[256,512]{1,0:T(8,128)(2,1)S(1)}, bf16[256,512]{1,0:T(8,128)(2,1)S(1)}, u32[]{:S(2)}, u32[]{:S(2)}) collective-permute-start(bf16[256,512]{1,0:T(8,128)(2,1)S(1)} %constant_dynamic-update-slice_fusion.4), channel_id=1, source_target_pairs={{0,64},{64,128},{128,192},{192,0},{1,65},{65,129},{129,193},{193,1... | collective-permute-start | bytes 786440 | tf_op jit(solution)/shard_map/ppermute | solution.py:30
  36.8 12.8 %collective-permute-start.12 = (bf16[256,512]{1,0:T(8,128)(2,1)S(1)}, bf16[256,512]{1,0:T(8,128)(2,1)S(1)}, u32[]{:S(2)}, u32[]{:S(2)}) collective-permute-start(bf16[256,512]{1,0:T(8,128)(2,1)S(1)} %constant_dynamic-update-slice_fusion.4), channel_id=1, source_target_pairs={{0,192},{64,0},{128,64},{192,128},{1,193},{65,1},{129,65},{193,129... | collective-permute-start | bytes 786440 | tf_op jit(solution)/shard_map/ppermute | solution.py:30
  49.6 11.8 %collective-permute-start.14 = (bf16[384,512]{1,0:T(8,128)(2,1)S(1)}, bf16[384,512]{1,0:T(8,128)(2,1)S(1)}, u32[]{:S(2)}, u32[]{:S(2)}) collective-permute-start(bf16[384,512]{1,0:T(8,128)(2,1)S(1)} %pad_maximum_fusion.1), channel_id=1, source_target_pairs={{0,48},{16,0},{32,16},{48,32},{1,49},{17,1},{33,17},{49,33},{2,50}... | collective-permute-start | bytes 1179656 | tf_op jit(solution)/shard_map/ppermute | solution.py:30
  52.3 10.7 %collective-permute-start.13 = (bf16[384,512]{1,0:T(8,128)(2,1)S(1)}, bf16[384,512]{1,0:T(8,128)(2,1)S(1)}, u32[]{:S(2)}, u32[]{:S(2)}) collective-permute-start(bf16[384,512]{1,0:T(8,128)(2,1)S(1)} %pad_maximum_fusion), channel_id=1, source_target_pairs={{0,16},{16,32},{32,48},{48,0},{1,17},{17,33},{33,49},{49,1},{2,18}... | collective-permute-start | bytes 1179656 | tf_op jit(solution)/shard_map/ppermute | solution.py:30
  52.4 9.0 %collective-permute-start.15 = (bf16[128,512]{1,0:T(8,128)(2,1)S(1)}, bf16[128,512]{1,0:T(8,128)(2,1)S(1)}, u32[]{:S(2)}, u32[]{:S(2)}) collective-permute-start(bf16[128,512]{1,0:T(8,128)(2,1)S(1)} %slice.67), channel_id=1, source_target_pairs={{0,64},{64,128},{128,192},{192,0},{1,65},{65,129},{129,193},{193,1... | collective-permute-start | bytes 393224 | tf_op jit(solution)/shard_map/ppermute | solution.py:30
  53.7 7.7 %collective-permute-start.16 = (bf16[128,512]{1,0:T(8,128)(2,1)S(1)}, bf16[128,512]{1,0:T(8,128)(2,1)S(1)}, u32[]{:S(2)}, u32[]{:S(2)}) collective-permute-start(bf16[128,512]{1,0:T(8,128)(2,1)S(1)} %slice.68), channel_id=1, source_target_pairs={{0,192},{64,0},{128,64},{192,128},{1,193},{65,1},{129,65},{193,129... | collective-permute-start | bytes 393224 | tf_op jit(solution)/shard_map/ppermute | solution.py:30
  88.5 15.2 %collective-permute-start.19 = (bf16[576,512]{1,0:T(8,128)(2,1)S(1)}, bf16[576,512]{1,0:T(8,128)(2,1)S(1)}, u32[]{:S(2)}, u32[]{:S(2)}) collective-permute-start(bf16[576,512]{1,0:T(8,128)(2,1)S(1)} %get-tuple-element.64), channel_id=1, source_target_pairs={{0,16},{16,32},{32,48},{48,0},{1,17},{17,33},{33,49},{49,1},{2,18}... | collective-permute-start | bytes 1769480 | tf_op jit(solution)/shard_map/ppermute | solution.py:30
  88.6 15.1 %collective-permute-start.20 = (bf16[576,512]{1,0:T(8,128)(2,1)S(1)}, bf16[576,512]{1,0:T(8,128)(2,1)S(1)}, u32[]{:S(2)}, u32[]{:S(2)}) collective-permute-start(bf16[576,512]{1,0:T(8,128)(2,1)S(1)} %get-tuple-element.65), channel_id=1, source_target_pairs={{0,48},{16,0},{32,16},{48,32},{1,49},{17,1},{33,17},{49,33},{2,50}... | collective-permute-start | bytes 1769480 | tf_op jit(solution)/shard_map/ppermute | solution.py:30
  91.8 15.3 %collective-permute-start.21 = (bf16[256,512]{1,0:T(8,128)(2,1)S(1)}, bf16[256,512]{1,0:T(8,128)(2,1)S(1)}, u32[]{:S(2)}, u32[]{:S(2)}) collective-permute-start(bf16[256,512]{1,0:T(8,128)(2,1)S(1)} %get-tuple-element.70), channel_id=1, source_target_pairs={{0,64},{64,128},{128,192},{192,0},{1,65},{65,129},{129,193},{193,1... | collective-permute-start | bytes 786440 | tf_op jit(solution)/shard_map/ppermute | solution.py:30
  94.0 13.1 %collective-permute-start.22 = (bf16[256,512]{1,0:T(8,128)(2,1)S(1)}, bf16[256,512]{1,0:T(8,128)(2,1)S(1)}, u32[]{:S(2)}, u32[]{:S(2)}) collective-permute-start(bf16[256,512]{1,0:T(8,128)(2,1)S(1)} %get-tuple-element.71), channel_id=1, source_target_pairs={{0,192},{64,0},{128,64},{192,128},{1,193},{65,1},{129,65},{193,129... | collective-permute-start | bytes 786440 | tf_op jit(solution)/shard_map/ppermute | solution.py:30
  103.8 8.0 %collective-permute-start.25 = (bf16[288,512]{1,0:T(8,128)(2,1)S(1)}, bf16[288,512]{1,0:T(8,128)(2,1)S(1)}, u32[]{:S(2)}, u32[]{:S(2)}) collective-permute-start(bf16[288,512]{1,0:T(8,128)(2,1)S(1)} %get-tuple-element.81), channel_id=1, source_target_pairs={{0,16},{16,32},{32,48},{48,0},{1,17},{17,33},{33,49},{49,1},{2,18}... | collective-permute-start | bytes 884744 | tf_op jit(solution)/shard_map/ppermute | solution.py:30
  103.9 7.9 %collective-permute-start.26 = (bf16[288,512]{1,0:T(8,128)(2,1)S(1)}, bf16[288,512]{1,0:T(8,128)(2,1)S(1)}, u32[]{:S(2)}, u32[]{:S(2)}) collective-permute-start(bf16[288,512]{1,0:T(8,128)(2,1)S(1)} %get-tuple-element.82), channel_id=1, source_target_pairs={{0,48},{16,0},{32,16},{48,32},{1,49},{17,1},{33,17},{49,33},{2,50}... | collective-permute-start | bytes 884744 | tf_op jit(solution)/shard_map/ppermute | solution.py:30
  107.2 8.2 %collective-permute-start.23 = (bf16[128,512]{1,0:T(8,128)(2,1)S(1)}, bf16[128,512]{1,0:T(8,128)(2,1)S(1)}, u32[]{:S(2)}, u32[]{:S(2)}) collective-permute-start(bf16[128,512]{1,0:T(8,128)(2,1)S(1)} %get-tuple-element.74), channel_id=1, source_target_pairs={{0,64},{64,128},{128,192},{192,0},{1,65},{65,129},{129,193},{193,1... | collective-permute-start | bytes 393224 | tf_op jit(solution)/shard_map/ppermute | solution.py:30
  109.5 7.3 %collective-permute-start.24 = (bf16[128,512]{1,0:T(8,128)(2,1)S(1)}, bf16[128,512]{1,0:T(8,128)(2,1)S(1)}, u32[]{:S(2)}, u32[]{:S(2)}) collective-permute-start(bf16[128,512]{1,0:T(8,128)(2,1)S(1)} %get-tuple-element.75), channel_id=1, source_target_pairs={{0,192},{64,0},{128,64},{192,128},{1,193},{65,1},{129,65},{193,129... | collective-permute-start | bytes 393224 | tf_op jit(solution)/shard_map/ppermute | solution.py:30
  117.0 15.0 %collective-permute-start.27 = (bf16[256,512]{1,0:T(8,128)(2,1)S(1)}, bf16[256,512]{1,0:T(8,128)(2,1)S(1)}, u32[]{:S(2)}, u32[]{:S(2)}) collective-permute-start(bf16[256,512]{1,0:T(8,128)(2,1)S(1)} %get-tuple-element.85), channel_id=1, source_target_pairs={{0,16},{16,32},{32,48},{48,0},{1,17},{17,33},{33,49},{49,1},{2,18}... | collective-permute-start | bytes 786440 | tf_op jit(solution)/shard_map/ppermute | solution.py:30
  117.0 14.9 %collective-permute-start.28 = (bf16[256,512]{1,0:T(8,128)(2,1)S(1)}, bf16[256,512]{1,0:T(8,128)(2,1)S(1)}, u32[]{:S(2)}, u32[]{:S(2)}) collective-permute-start(bf16[256,512]{1,0:T(8,128)(2,1)S(1)} %get-tuple-element.86), channel_id=1, source_target_pairs={{0,48},{16,0},{32,16},{48,32},{1,49},{17,1},{33,17},{49,33},{2,50}... | collective-permute-start | bytes 786440 | tf_op jit(solution)/shard_map/ppermute | solution.py:30
  120.3 10.2 %collective-permute-start.29 = (bf16[192,512]{1,0:T(8,128)(2,1)S(1)}, bf16[192,512]{1,0:T(8,128)(2,1)S(1)}, u32[]{:S(2)}, u32[]{:S(2)}) collective-permute-start(bf16[192,512]{1,0:T(8,128)(2,1)S(1)} %get-tuple-element.83._), channel_id=1, source_target_pairs={{0,64},{64,128},{128,192},{192,0},{1,65},{65,129},{129,193},{193,1... | collective-permute-start | bytes 589832 | tf_op jit(solution)/shard_map/ppermute | solution.py:30
  123.2 8.7 %collective-permute-start.30 = (bf16[192,512]{1,0:T(8,128)(2,1)S(1)}, bf16[192,512]{1,0:T(8,128)(2,1)S(1)}, u32[]{:S(2)}, u32[]{:S(2)}) collective-permute-start(bf16[192,512]{1,0:T(8,128)(2,1)S(1)} %get-tuple-element.91), channel_id=1, source_target_pairs={{0,192},{64,0},{128,64},{192,128},{1,193},{65,1},{129,65},{193,129... | collective-permute-start | bytes 589832 | tf_op jit(solution)/shard_map/ppermute | solution.py:30
  132.0 10.5 %collective-permute-start.31 = (bf16[128,512]{1,0:T(8,128)(2,1)S(1)}, bf16[128,512]{1,0:T(8,128)(2,1)S(1)}, u32[]{:S(2)}, u32[]{:S(2)}) collective-permute-start(bf16[128,512]{1,0:T(8,128)(2,1)S(1)} %get-tuple-element.93), channel_id=1, source_target_pairs={{0,16},{16,32},{32,48},{48,0},{1,17},{17,33},{33,49},{49,1},{2,18}... | collective-permute-start | bytes 393224 | tf_op jit(solution)/shard_map/ppermute | solution.py:30
  132.1 10.4 %collective-permute-start.32 = (bf16[128,512]{1,0:T(8,128)(2,1)S(1)}, bf16[128,512]{1,0:T(8,128)(2,1)S(1)}, u32[]{:S(2)}, u32[]{:S(2)}) collective-permute-start(bf16[128,512]{1,0:T(8,128)(2,1)S(1)} %get-tuple-element.94), channel_id=1, source_target_pairs={{0,48},{16,0},{32,16},{48,32},{1,49},{17,1},{33,17},{49,33},{2,50}... | collective-permute-start | bytes 393224 | tf_op jit(solution)/shard_map/ppermute | solution.py:30
  135.3 6.7 %collective-permute-start.33 = (bf16[96,512]{1,0:T(8,128)(2,1)S(1)}, bf16[96,512]{1,0:T(8,128)(2,1)S(1)}, u32[]{:S(2)}, u32[]{:S(2)}) collective-permute-start(bf16[96,512]{1,0:T(8,128)(2,1)S(1)} %get-tuple-element.92.rest_0_), channel_id=1, source_target_pairs={{0,64},{64,128},{128,192},{192,0},{1,65},{65,129},{129,193},{193,1... | collective-permute-start | bytes 294920 | tf_op jit(solution)/shard_map/ppermute | solution.py:30
  (11 other events, 96.6 us)

commit v2 on v1

--- a/solution.py
+++ b/solution.py
@@ -195,39 +195,44 @@
 
 
 def gathered_logits(head, hidden, at, sibling_at):
-    zb, za = move(head[:PR], "zh", 1), move(head[:PR], "zh", -1)
-    xb, xa = move(head, "x", 1), move(head, "x", -1)
+    def split(h, *outs):
+        for out, start in zip(outs, (0, PH, PR)):
+            out[...] = h[start : start + out.shape[0], :]
+
+    over_zh, over_x, far_x = local_call(
+        split, [jax.ShapeDtypeStruct((r, WIDE), BF16) for r in (PR, ROWS - PH, QR)], head
+    )
+    zb, za, zf = (move(over_zh, "zh", by) for by in (1, -1, 2))
+    xb, xa = move(over_x, "x", 1), move(over_x, "x", -1)
+    xf = move(far_x, "x", 2)
     picked = pick(hidden, sibling_at, 50)
-    zb, za, xb, xa, picked = lax.optimization_barrier((zb, za, xb, xa, picked))
+    zb, za, zf, xb, xa, xf, picked = lax.optimization_barrier((zb, za, zf, xb, xa, xf, picked))
     theirs = move(picked, "c", 1)
-    zf1, zf2 = move(zb[:PH], "zh", 1), move(za[PH:], "zh", -1)
-    xf1, xf2 = move(xb[PR : PR + QH], "x", 1), move(xa[PR + QH :], "x", -1)
-    p = jnp.concatenate([za, zb, zf1, zf2], axis=0)
-    q = jnp.concatenate([head[PR:], xa[PR:], xb[PR:], xf1, xf2], axis=0)
+    p = jnp.concatenate([za, zb, zf, head[:PH]], axis=0)
+    q = jnp.concatenate([head[PR:], xa[PH:], xb[PH:], xf], axis=0)
     pb, pa = move(p, "x", 1), move(p, "x", -1)
     qb, qa = move(q, "zh", 1), move(q, "zh", -1)
-    zf1, zf2, at = lax.optimization_barrier((zf1, zf2, at))
+    zf, at = lax.optimization_barrier((zf, at))
     mine = pick(hidden, at, 40)
+    pb, pa, qb, qa, mine = lax.optimization_barrier((pb, pa, qb, qa, mine))
+    pf1 = jnp.concatenate([pb[: 3 * PH], pb[3 * PR :]], axis=0)
+    pf2 = jnp.concatenate([pa[3 * PH : 3 * PR], xa[:PH]], axis=0)
+    pf1, pf2 = move(pf1, "x", 1), move(pf2, "x", -1)
+    qf1, qf2 = move(qb[: 2 * QR], "zh", 1), move(qa[2 * QR :], "zh", -1)
+
     blocks = (mine, theirs)
 
     def first(add, refs, out):
-        head_ref, xa_ref, xb_ref, xf1_ref, xf2_ref, p_ref = refs
+        head_ref, xa_ref, xb_ref, xf_ref, p_ref = refs
         out[...] = jnp.zeros_like(out)
         add(out, head_ref[...], 0)
-        add(out, xa_ref[...], 1)
-        add(out, xb_ref[...], 3)
-        add(out.at[PR : PR + QH], xf1_ref[...], 2)
-        add(out.at[PR + QH :], xf2_ref[...], 2)
+        add(out.at[PH:], xa_ref[...], 1)
+        add(out.at[PH:], xb_ref[...], 3)
+        add(out.at[PR:], xf_ref[...], 2)
         for k, dz in enumerate(AHEAD):
             add(out.at[:PR], p_ref[k * PR : (k + 1) * PR, :], 4 * dz)
 
-    total = logits_call(first, blocks, [head, xa, xb, xf1, xf2, p])
-    pb, pa, qb, qa, total = lax.optimization_barrier((pb, pa, qb, qa, total))
-    pf1 = jnp.concatenate([pb[: 3 * PH], xb[:PH]], axis=0)
-    pf2 = jnp.concatenate([pa[3 * PH :], xa[PH:PR]], axis=0)
-    pf1, pf2 = move(pf1, "x", 1), move(pf2, "x", -1)
-    qf1, qf2 = move(qb[: 2 * QR], "zh", 1), move(qa[2 * QR :], "zh", -1)
-
+    total = logits_call(first, blocks, [head, xa, xb, xf, p])
     def second(add, refs, out):
         pa_ref, pb_ref, qa_ref, qb_ref, total_ref = refs
         out[...] = total_ref[...]
@@ -235,6 +240,8 @@
             part = slice(k * PR, (k + 1) * PR)
             add(out.at[:PR], pa_ref[part, :], 4 * dz + 1)
             add(out.at[:PR], pb_ref[part, :], 4 * dz + 3)
+        add(out.at[:PH], pa_ref[3 * PR :, :], 1)
+        add(out.at[:PH], pb_ref[3 * PR :, :], 3)
         for j, dx in enumerate((0,) + AHEAD):
             part = slice(j * QR, (j + 1) * QR)
             add(out.at[PR:], qa_ref[part, :], 4 + dx)
@@ -336,9 +343,8 @@
     )
     p_up, p_down, own, q_here = lax.optimization_barrier((p_up, p_down, own, q_here))
 
-    def forward(kept_ahead, kept_behind, up, down, n, half, *after):
-        def body(a, b, u, d, *rest):
-            up_out, down_out = rest[-2:]
+    def forward(kept_ahead, kept_behind, up, down, n, half):
+        def body(a, b, u, d, up_out, down_out):
             for k in range(n):
                 to, first, last = k * half, 2 * k * half, (2 * k + 1) * half
                 up_out[to : to + half, :] = (
@@ -349,7 +355,7 @@
                 ).astype(BF16)
 
         return local_call(
-            body, [array(n * half, BF16)] * 2, kept_ahead, kept_behind, up, down, *after
+            body, [array(n * half, BF16)] * 2, kept_ahead, kept_behind, up, down
         )
 
     def settle(kept, up, down, up2, down2, n, half, k):
@@ -366,26 +372,17 @@
     q_up2, q_down2 = forward(q_ahead, q_behind, q_up, q_down, 4, QH)
     q_up2, q_down2 = move(q_up2, "zh", 1), move(q_down2, "zh", -1)
 
-    def p_body(kept, up, down, up2, down2, up_out, down_out, ahead, behind):
-        for dz in (1, 2, 3):
-            one, two = settle(kept, up, down, up2, down2, 3, PH, dz - 1)
-            if dz == 1:
-                ahead[...] = one
-                up_out[PH:, :] = two.astype(BF16)
-            elif dz == 2:
-                up_out[:PH, :] = one.astype(BF16)
-                down_out[PH:, :] = two.astype(BF16)
-            else:
-                down_out[:PH, :] = one.astype(BF16)
-                behind[...] = two
-
-    z_up, z_down, z_ahead, z_behind = local_call(
-        p_body,
-        [array(PR, BF16), array(PR, BF16), array(PH, F32), array(PH, F32)],
-        p_here, p_up, p_down, p_up2, p_down2,
-    )
-    p_sent = z_up
-    z_up, z_down = move(z_up, "zh", 1), move(z_down, "zh", -1)
+    def p_body(kept, up, down, up2, down2, *outs):
+        for k in range(3):
+            one, two = settle(kept, up, down, up2, down2, 3, PH, k)
+            outs[k][:PH, :] = one.astype(BF16)
+            outs[k][PH:, :] = two.astype(BF16)
+
+    z1, z2, z3 = local_call(
+        p_body, [array(PR, BF16)] * 3, p_here, p_up, p_down, p_up2, p_down2
+    )
+    p_sent = z1
+    z1, z2, z3 = move(z1, "zh", 1), move(z2, "zh", 2), move(z3, "zh", -1)
 
     def q_body(own, kept, up, down, up2, down2, _, up_out, down_out, ahead, behind, here):
         rest = PR - RH
@@ -412,20 +409,16 @@
     )
     x_up, x_down = move(x_up, "x", 1), move(x_down, "x", -1)
 
-    z_up2, z_down2 = forward(z_ahead, z_behind, z_up, z_down, 1, PH)
-    x_up2, x_down2 = forward(x_ahead, x_behind, x_up, x_down, 1, RH, z_up2)
-    z_up2, z_down2 = move(z_up2, "zh", 1), move(z_down2, "zh", -1)
+    x_up2, x_down2 = forward(x_ahead, x_behind, x_up, x_down, 1, RH)
     x_up2, x_down2 = move(x_up2, "x", 1), move(x_down2, "x", -1)
 
-    def last_body(here, xu, xd, xu2, xd2, zu, zd, zu2, zd2, out):
+    def last_body(here, xu, xd, xu2, xd2, z1, z2, z3, out):
         out[:RH, :] = here[:RH, :] + xd[:RH, :].astype(F32) + xu2[...].astype(F32)
         out[RH:, :] = here[RH:, :] + xu[RH:, :].astype(F32) + xd2[...].astype(F32)
-        out[:PH, :] += zd[:PH, :].astype(F32) + zu2[...].astype(F32)
-        out[PH:PR, :] += zu[PH:, :].astype(F32) + zd2[...].astype(F32)
+        out[:PR, :] += z1[...].astype(F32) + z2[...].astype(F32) + z3[...].astype(F32)
 
     (out,) = local_call(
-        last_body, [array(ROWS, F32)],
-        x_here, x_up, x_down, x_up2, x_down2, z_up, z_down, z_up2, z_down2,
+        last_body, [array(ROWS, F32)], x_here, x_up, x_down, x_up2, x_down2, z1, z2, z3
     )
     return out
 

time: 146 us -> 145 us (level); the launches traced: 143 us -> 145 us
  waiting for transfers between devices: 33 us -> 26.7 us
  starting transfers between devices: 61.1 us -> 65.4 us
  blocking collectives: 10.1 us -> 13.1 us
    ppermute x35 -> x32, waiting for transfers between devices: 33 us -> 26.7 us  [move(): return lax.ppermute(value, axis, [(i, (i + by) % n) for i in range(n)])]
    ppermute x35 -> x32, starting transfers between devices: 61.1 us -> 65.4 us  [move(): return lax.ppermute(value, axis, [(i, (i + by) % n) for i in range(n)])]
    all_to_all x1, blocking collectives: 10.1 us -> 13.1 us  [shards(): lax.all_to_all(jnp.broadcast_to(stats[None], (8,) + stats.shape), TENSOR,...]
  transfers between devices with their start and end apart: 35 -> 32, of which waited for: 15 -> 10; matrix products, arithmetic and copies ran while one was open for 1% -> 1% of each run, Pallas kernels for 16% -> 16%
where the time goes in v2:
time: 145 us
  starting transfers between devices  65.4 us (45%)
  Pallas kernels  36.4 us (25%)
  waiting for transfers between devices  26.7 us (18%)
  blocking collectives  13.1 us (9%)
  local copies, waits for them, and re-layouts  1.75 us (1%)
    ppermute x32, starting transfers between devices, move(): return lax.ppermute(value, axis, [(i, (i + by) % n) for i in range(n)])  65.4 us
    ppermute x32, waiting for transfers between devices, move(): return lax.ppermute(value, axis, [(i, (i + by) % n) for i in range(n)])  26.7 us
    pallas_call x12, Pallas kernels, local_call(): pl.pallas_call(body, out_shape=outs, in_specs=[whole(a.shape) for a in ar...  13.5 us
    all_to_all x1, blocking collectives, shards(): lax.all_to_all(jnp.broadcast_to(stats[None], (8,) + stats.shape), TENSOR,...  13.1 us
    pallas_call x2, Pallas kernels, pick(): pl.pallas_call(body, out_shape=jax.ShapeDtypeStruct((n, TOK, WIDE), BF16)...  11.7 us
    pallas_call x2, Pallas kernels, block_call(): pl.pallas_call(body, out_shape=outs, in_specs=[pl.BlockSpec(memory_space=...  11.2 us
  transfers between devices with their start and end apart: 32, of which 10 were waited for; matrix products, arithmetic and copies ran while one was open for 1% of the time, Pallas kernels for 16%

profile of v2, /device:TPU:8, one launch (start us, length us, event | category | flops | bytes accessed | tf_op | source)
XLA Modules:
  0.0 145.0 jit_solution(14293761590355448198)
XLA Ops:
  1.6 3.1 %collective-permute-start.5 = (bf16[64,512]{1,0:T(8,128)(2,1)S(1)}, bf16[64,512]{1,0:T(8,128)(2,1)S(1)}, u32[]{:S(2)}, u32[]{:S(2)}) collective-permute-start(bf16[64,512]{1,0:T(8,128)(2,1)S(1)} %get-tuple-element.53), channel_id=1, source_target_pairs={{0,32},{16,48},{32,0},{48,16},{1,33},{17,49},{33,1},{49,17},{2,34}... | collective-permute-start | bytes 196616 | tf_op jit(solution)/shard_map/ppermute | solution.py:30
  4.7 3.3 %collective-permute-start = (bf16[192,512]{1,0:T(8,128)(2,1)S(1)}, bf16[192,512]{1,0:T(8,128)(2,1)S(1)}, u32[]{:S(2)}, u32[]{:S(2)}) collective-permute-start(bf16[192,512]{1,0:T(8,128)(2,1)S(1)} %get-tuple-element.51), channel_id=1, source_target_pairs={{0,64},{64,128},{128,192},{192,0},{1,65},{65,129},{129,193},{193,1... | collective-permute-start | bytes 589832 | tf_op jit(solution)/shard_map/ppermute | solution.py:30
  8.0 3.0 %collective-permute-start.1 = (bf16[192,512]{1,0:T(8,128)(2,1)S(1)}, bf16[192,512]{1,0:T(8,128)(2,1)S(1)}, u32[]{:S(2)}, u32[]{:S(2)}) collective-permute-start(bf16[192,512]{1,0:T(8,128)(2,1)S(1)} %get-tuple-element.51), channel_id=1, source_target_pairs={{0,192},{64,0},{128,64},{192,128},{1,193},{65,1},{129,65},{193,129... | collective-permute-start | bytes 589832 | tf_op jit(solution)/shard_map/ppermute | solution.py:30
  11.0 5.0 %collective-permute-start.2 = (bf16[192,512]{1,0:T(8,128)(2,1)S(1)}, bf16[192,512]{1,0:T(8,128)(2,1)S(1)}, u32[]{:S(2)}, u32[]{:S(2)}) collective-permute-start(bf16[192,512]{1,0:T(8,128)(2,1)S(1)} %get-tuple-element.51), channel_id=1, source_target_pairs={{0,128},{64,192},{128,0},{192,64},{1,129},{65,193},{129,1},{193,65... | collective-permute-start | bytes 589832 | tf_op jit(solution)/shard_map/ppermute | solution.py:30
  16.6 2.6 %collective-permute-start.4 = (bf16[160,512]{1,0:T(8,128)(2,1)S(1)}, bf16[160,512]{1,0:T(8,128)(2,1)S(1)}, u32[]{:S(2)}, u32[]{:S(2)}) collective-permute-start(bf16[160,512]{1,0:T(8,128)(2,1)S(1)} %get-tuple-element.52), channel_id=1, source_target_pairs={{0,48},{16,0},{32,16},{48,32},{1,49},{17,1},{33,17},{49,33},{2,50}... | collective-permute-start | bytes 491528 | tf_op jit(solution)/shard_map/ppermute | solution.py:30
  19.3 7.5 %shard_map.78 = bf16[16,512,512]{2,1,0:T(8,128)(2,1)} custom-call(s32[16]{0:T(128)S(1)} %broadcast_add_fusion.1.at_ref, bf16[512,16384]{1,0:T(8,128)(2,1)} %h_ref.3), custom_call_target="tpu_custom_call" | custom-call | bytes 16777216 | tf_op jit(solution)/shard_map/pallas_call | solution.py:72
  28.0 2.6 %collective-permute-start.7 = (bf16[672,512]{1,0:T(8,128)(2,1)S(1)}, bf16[672,512]{1,0:T(8,128)(2,1)S(1)}, u32[]{:S(2)}, u32[]{:S(2)}) collective-permute-start(bf16[672,512]{1,0:T(8,128)(2,1)S(1)} %pad_maximum_fusion.refs_4_), channel_id=1, source_target_pairs={{0,48},{16,0},{32,16},{48,32},{1,49},{17,1},{33,17},{49,33},{2,50}... | collective-permute-start | bytes 2064392 | tf_op jit(solution)/shard_map/ppermute | solution.py:30
  30.7 6.1 %collective-permute-start.8 = (bf16[256,512]{1,0:T(8,128)(2,1)S(1)}, bf16[256,512]{1,0:T(8,128)(2,1)S(1)}, u32[]{:S(2)}, u32[]{:S(2)}) collective-permute-start(bf16[256,512]{1,0:T(8,128)(2,1)S(1)} %pad_maximum_fusion.3), channel_id=1, source_target_pairs={{0,64},{64,128},{128,192},{192,0},{1,65},{65,129},{129,193},{193,1... | collective-permute-start | bytes 786440 | tf_op jit(solution)/shard_map/ppermute | solution.py:30
  36.8 4.2 %shard_map.79.m_ref = bf16[16,512,512]{2,1,0:T(8,128)(2,1)S(1)} custom-call(s32[16]{0:T(128)S(1)} %broadcast_add_fusion.at_ref, bf16[512,16384]{1,0:T(8,128)(2,1)} %h_ref.3), custom_call_target="tpu_custom_call" | custom-call | bytes 16777216 | tf_op jit(solution)/shard_map/pallas_call | solution.py:72
  41.1 4.9 %collective-permute-done.8.refs_3_ = bf16[256,512]{1,0:T(8,128)(2,1)S(1)} collective-permute-done((bf16[256,512]{1,0:T(8,128)(2,1)S(1)}, bf16[256,512]{1,0:T(8,128)(2,1)S(1)}, u32[]{:S(2)}, u32[]{:S(2)}) %collective-permute-start.8) | collective-permute-done | bytes 262176 | tf_op jit(solution)/shard_map/ppermute | solution.py:30
  47.2 2.4 %collective-permute-start.12 = (bf16[384,512]{1,0:T(8,128)(2,1)S(1)}, bf16[384,512]{1,0:T(8,128)(2,1)S(1)}, u32[]{:S(2)}, u32[]{:S(2)}) collective-permute-start(bf16[384,512]{1,0:T(8,128)(2,1)S(1)} %pad_maximum_fusion.2), channel_id=1, source_target_pairs={{0,48},{16,0},{32,16},{48,32},{1,49},{17,1},{33,17},{49,33},{2,50}... | collective-permute-start | bytes 1179656 | tf_op jit(solution)/shard_map/ppermute | solution.py:30
  49.8 6.1 %collective-permute-start.13 = (bf16[128,512]{1,0:T(8,128)(2,1)S(1)}, bf16[128,512]{1,0:T(8,128)(2,1)S(1)}, u32[]{:S(2)}, u32[]{:S(2)}) collective-permute-start(bf16[128,512]{1,0:T(8,128)(2,1)S(1)} %slice.50), channel_id=1, source_target_pairs={{0,64},{64,128},{128,192},{192,0},{1,65},{65,129},{129,193},{193,1... | collective-permute-start | bytes 393224 | tf_op jit(solution)/shard_map/ppermute | solution.py:30
  56.2 2.4 %shard_map.80.refs_4_ = f32[256,1024]{1,0:T(8,128)S(1)} custom-call(bf16[16,512,512]{2,1,0:T(8,128)(2,1)S(1)} %shard_map.79.m_ref, bf16[16,512,512]{2,1,0:T(8,128)(2,1)S(1)} %collective-permute-done.10.t_ref, bf16[256,512]{1,0:T(8,128)(2,1)S(1)} %copy-done.3, bf16[160,512]{1,0:T(8,128)(2,1)S(1)} %copy-done.6, ...), custom_call_target="tpu_custom_call" | custom-call | bytes 19169280 | tf_op jit(solution)/shard_map/pallas_call | solution.py:45
  58.7 5.3 %shard_map.81.refs_4_ = f32[256,1024]{1,0:T(8,128)S(1)} custom-call(bf16[16,512,512]{2,1,0:T(8,128)(2,1)S(1)} %shard_map.79.m_ref, bf16[16,512,512]{2,1,0:T(8,128)(2,1)S(1)} %collective-permute-done.10.t_ref, bf16[672,512]{1,0:T(8,128)(2,1)S(1)} %collective-permute-done.7.refs_0_, bf16[672,512]{1,0:T(8,128)(2,1)S(1)} %collective-permute-done.6.refs_1_, ...), custom_call_target="tpu_custom_call" | custom-call | bytes 20774912 | tf_op jit(solution)/shard_map/pallas_call | solution.py:45
  64.2 3.3 %shard_map.82.mine = f32[256,1024]{1,0:T(8,128)S(1)} custom-call(bf16[16,512,512]{2,1,0:T(8,128)(2,1)S(1)} %shard_map.79.m_ref, bf16[16,512,512]{2,1,0:T(8,128)(2,1)S(1)} %collective-permute-done.10.t_ref, bf16[384,512]{1,0:T(8,128)(2,1)S(1)} %collective-permute-done.11.refs_0_, bf16[384,512]{1,0:T(8,128)(2,1)S(1)} %collective-permute-done.12.refs_1_, ...), custom_call_target="tpu_custom_call" | custom-call | bytes 19922944 | tf_op jit(solution)/shard_map/pallas_call | solution.py:45
  68.3 1.9 %collective-permute-done.16 = f32[3,512]{1,0:T(4,128)S(1)} collective-permute-done((f32[3,512]{1,0:T(4,128)S(1)}, f32[3,512]{1,0:T(4,128)S(1)}, u32[]{:S(2)}, u32[]{:S(2)}) %collective-permute-start.16) | collective-permute-done | bytes 6176 | tf_op jit(solution)/shard_map/ppermute | solution.py:30
  71.1 13.1 %all_to_all.5 = f32[8,3,1024]{2,1,0:T(4,128)S(1)} all-to-all(f32[8,3,1024]{2,1,0:T(4,128)S(1)} %broadcast_in_dim.2), channel_id=1, replica_groups=mesh['zh'=4,'x'=4,'c'=2,'zl'=2,'y'=4] {'zl','y'}, dimensions={0} | all-to-all | bytes 196608 | tf_op jit(solution)/shard_map/all_to_all | solution.py:446
  84.5 8.1 %shard_map.85 = (bf16[576,512]{1,0:T(8,128)(2,1)S(1)}, bf16[576,512]{1,0:T(8,128)(2,1)S(1)}, bf16[256,512]{1,0:T(8,128)(2,1)S(1)}, bf16[256,512]{1,0:T(8,128)(2,...) custom-call(bf16[16,512,512]{2,1,0:T(8,128)(2,1)} %copy-done, ...), custom_call_target="tpu_custom_call" | custom-call | flops 3221225472 | bytes 12582912 | tf_op jit(solution)/shard_map/pallas_call | solution.py:113
  92.7 3.3 %collective-permute-start.18 = (bf16[576,512]{1,0:T(8,128)(2,1)S(1)}, bf16[576,512]{1,0:T(8,128)(2,1)S(1)}, u32[]{:S(2)}, u32[]{:S(2)}) collective-permute-start(bf16[576,512]{1,0:T(8,128)(2,1)S(1)} %get-tuple-element.72), channel_id=1, source_target_pairs={{0,48},{16,0},{32,16},{48,32},{1,49},{17,1},{33,17},{49,33},{2,50}... | collective-permute-start | bytes 1769480 | tf_op jit(solution)/shard_map/ppermute | solution.py:30
  96.0 4.1 %collective-permute-start.20 = (bf16[256,512]{1,0:T(8,128)(2,1)S(1)}, bf16[256,512]{1,0:T(8,128)(2,1)S(1)}, u32[]{:S(2)}, u32[]{:S(2)}) collective-permute-start(bf16[256,512]{1,0:T(8,128)(2,1)S(1)} %get-tuple-element.78), channel_id=1, source_target_pairs={{0,192},{64,0},{128,64},{192,128},{1,193},{65,1},{129,65},{193,129... | collective-permute-start | bytes 786440 | tf_op jit(solution)/shard_map/ppermute | solution.py:30
  100.2 3.1 %shard_map.86 = (f32[768,512]{1,0:T(8,128)S(1)}, f32[256,512]{1,0:T(8,128)S(1)}) custom-call(bf16[16,512,512]{2,1,0:T(8,128)(2,1)} %copy-done, bf16[16,512,512]{2,1,0:T(8,128)(2,1)} %copy-done.1, bf16[256,1024]{1,0:T(8,128)(2,1)S(1)} %get-tuple-element.70.refs_0_), custom_call_target="tpu_custom_call" | custom-call | flops 1073741824 | bytes 4194304 | tf_op jit(solution)/shard_map/pallas_call | solution.py:113
  103.3 4.9 %collective-permute-done.17.u.up = bf16[576,512]{1,0:T(8,128)(2,1)S(1)} collective-permute-done((bf16[576,512]{1,0:T(8,128)(2,1)S(1)}, bf16[576,512]{1,0:T(8,128)(2,1)S(1)}, u32[]{:S(2)}, u32[]{:S(2)}) %collective-permute-start.17) | collective-permute-done | bytes 589856 | tf_op jit(solution)/shard_map/ppermute | solution.py:30
  108.3 1.4 collective-permute-start.23
  109.7 2.1 %collective-permute-start.24 = (bf16[288,512]{1,0:T(8,128)(2,1)S(1)}, bf16[288,512]{1,0:T(8,128)(2,1)S(1)}, u32[]{:S(2)}, u32[]{:S(2)}) collective-permute-start(bf16[288,512]{1,0:T(8,128)(2,1)S(1)} %get-tuple-element.89), channel_id=1, source_target_pairs={{0,48},{16,0},{32,16},{48,32},{1,49},{17,1},{33,17},{49,33},{2,50}... | collective-permute-start | bytes 884744 | tf_op jit(solution)/shard_map/ppermute | solution.py:30
  112.6 3.5 %collective-permute-start.22 = (bf16[128,512]{1,0:T(8,128)(2,1)S(1)}, bf16[128,512]{1,0:T(8,128)(2,1)S(1)}, u32[]{:S(2)}, u32[]{:S(2)}) collective-permute-start(bf16[128,512]{1,0:T(8,128)(2,1)S(1)} %get-tuple-element.82), channel_id=1, source_target_pairs={{0,192},{64,0},{128,64},{192,128},{1,193},{65,1},{129,65},{193,129... | collective-permute-start | bytes 393224 | tf_op jit(solution)/shard_map/ppermute | solution.py:30
  116.9 3.5 %collective-permute-done.21.up2 = bf16[128,512]{1,0:T(8,128)(2,1)S(1)} collective-permute-done((bf16[128,512]{1,0:T(8,128)(2,1)S(1)}, bf16[128,512]{1,0:T(8,128)(2,1)S(1)}, u32[]{:S(2)}, u32[]{:S(2)}) %collective-permute-start.21) | collective-permute-done | bytes 131104 | tf_op jit(solution)/shard_map/ppermute | solution.py:30
  120.6 3.2 %collective-permute-start.26 = (bf16[256,512]{1,0:T(8,128)(2,1)S(1)}, bf16[256,512]{1,0:T(8,128)(2,1)S(1)}, u32[]{:S(2)}, u32[]{:S(2)}) collective-permute-start(bf16[256,512]{1,0:T(8,128)(2,1)S(1)} %get-tuple-element.93), channel_id=1, source_target_pairs={{0,48},{16,0},{32,16},{48,32},{1,49},{17,1},{33,17},{49,33},{2,50}... | collective-permute-start | bytes 786440 | tf_op jit(solution)/shard_map/ppermute | solution.py:30
  125.0 4.1 %collective-permute-start.30 = (bf16[192,512]{1,0:T(8,128)(2,1)S(1)}, bf16[192,512]{1,0:T(8,128)(2,1)S(1)}, u32[]{:S(2)}, u32[]{:S(2)}) collective-permute-start(bf16[192,512]{1,0:T(8,128)(2,1)S(1)} %get-tuple-element.98), channel_id=1, source_target_pairs={{0,128},{64,192},{128,0},{192,64},{1,129},{65,193},{129,1},{193,65... | collective-permute-start | bytes 589832 | tf_op jit(solution)/shard_map/ppermute | solution.py:30
  129.1 1.6 %collective-permute-start.31 = (bf16[192,512]{1,0:T(8,128)(2,1)S(1)}, bf16[192,512]{1,0:T(8,128)(2,1)S(1)}, u32[]{:S(2)}, u32[]{:S(2)}) collective-permute-start(bf16[192,512]{1,0:T(8,128)(2,1)S(1)} %get-tuple-element.99), channel_id=1, source_target_pairs={{0,192},{64,0},{128,64},{192,128},{1,193},{65,1},{129,65},{193,129... | collective-permute-start | bytes 589832 | tf_op jit(solution)/shard_map/ppermute | solution.py:30
  130.8 3.2 %collective-permute-start.28 = (bf16[128,512]{1,0:T(8,128)(2,1)S(1)}, bf16[128,512]{1,0:T(8,128)(2,1)S(1)}, u32[]{:S(2)}, u32[]{:S(2)}) collective-permute-start(bf16[128,512]{1,0:T(8,128)(2,1)S(1)} %get-tuple-element.97), channel_id=1, source_target_pairs={{0,48},{16,0},{32,16},{48,32},{1,49},{17,1},{33,17},{49,33},{2,50}... | collective-permute-start | bytes 393224 | tf_op jit(solution)/shard_map/ppermute | solution.py:30
  134.7 6.4 %collective-permute-done.30.z2 = bf16[192,512]{1,0:T(8,128)(2,1)S(1)} collective-permute-done((bf16[192,512]{1,0:T(8,128)(2,1)S(1)}, bf16[192,512]{1,0:T(8,128)(2,1)S(1)}, u32[]{:S(2)}, u32[]{:S(2)}) %collective-permute-start.30) | collective-permute-done | bytes 196640 | tf_op jit(solution)/shard_map/ppermute | solution.py:30
  141.1 2.9 %collective-permute-done.31.z3 = bf16[192,512]{1,0:T(8,128)(2,1)S(1)} collective-permute-done((bf16[192,512]{1,0:T(8,128)(2,1)S(1)}, bf16[192,512]{1,0:T(8,128)(2,1)S(1)}, u32[]{:S(2)}, u32[]{:S(2)}) %collective-permute-start.31) | collective-permute-done | bytes 196640 | tf_op jit(solution)/shard_map/ppermute | solution.py:30
  (100 shorter events, 11.3 us)
Async XLA Ops:
  1.6 15.0 %collective-permute-start.5 = (bf16[64,512]{1,0:T(8,128)(2,1)S(1)}, bf16[64,512]{1,0:T(8,128)(2,1)S(1)}, u32[]{:S(2)}, u32[]{:S(2)}) collective-permute-start(bf16[64,512]{1,0:T(8,128)(2,1)S(1)} %get-tuple-element.53), channel_id=1, source_target_pairs={{0,32},{16,48},{32,0},{48,16},{1,33},{17,49},{33,1},{49,17},{2,34}... | collective-permute-start | bytes 196616 | tf_op jit(solution)/shard_map/ppermute | solution.py:30
  4.7 22.2 %collective-permute-start = (bf16[192,512]{1,0:T(8,128)(2,1)S(1)}, bf16[192,512]{1,0:T(8,128)(2,1)S(1)}, u32[]{:S(2)}, u32[]{:S(2)}) collective-permute-start(bf16[192,512]{1,0:T(8,128)(2,1)S(1)} %get-tuple-element.51), channel_id=1, source_target_pairs={{0,64},{64,128},{128,192},{192,0},{1,65},{65,129},{129,193},{193,1... | collective-permute-start | bytes 589832 | tf_op jit(solution)/shard_map/ppermute | solution.py:30
  8.0 18.9 %collective-permute-start.1 = (bf16[192,512]{1,0:T(8,128)(2,1)S(1)}, bf16[192,512]{1,0:T(8,128)(2,1)S(1)}, u32[]{:S(2)}, u32[]{:S(2)}) collective-permute-start(bf16[192,512]{1,0:T(8,128)(2,1)S(1)} %get-tuple-element.51), channel_id=1, source_target_pairs={{0,192},{64,0},{128,64},{192,128},{1,193},{65,1},{129,65},{193,129... | collective-permute-start | bytes 589832 | tf_op jit(solution)/shard_map/ppermute | solution.py:30
  11.0 16.2 %collective-permute-start.2 = (bf16[192,512]{1,0:T(8,128)(2,1)S(1)}, bf16[192,512]{1,0:T(8,128)(2,1)S(1)}, u32[]{:S(2)}, u32[]{:S(2)}) collective-permute-start(bf16[192,512]{1,0:T(8,128)(2,1)S(1)} %get-tuple-element.51), channel_id=1, source_target_pairs={{0,128},{64,192},{128,0},{192,64},{1,129},{65,193},{129,1},{193,65... | collective-permute-start | bytes 589832 | tf_op jit(solution)/shard_map/ppermute | solution.py:30
  16.1 10.8 %collective-permute-start.3 = (bf16[160,512]{1,0:T(8,128)(2,1)S(1)}, bf16[160,512]{1,0:T(8,128)(2,1)S(1)}, u32[]{:S(2)}, u32[]{:S(2)}) collective-permute-start(bf16[160,512]{1,0:T(8,128)(2,1)S(1)} %get-tuple-element.52), channel_id=1, source_target_pairs={{0,16},{16,32},{32,48},{48,0},{1,17},{17,33},{33,49},{49,1},{2,18}... | collective-permute-start | bytes 491528 | tf_op jit(solution)/shard_map/ppermute | solution.py:30
  16.6 10.2 %collective-permute-start.4 = (bf16[160,512]{1,0:T(8,128)(2,1)S(1)}, bf16[160,512]{1,0:T(8,128)(2,1)S(1)}, u32[]{:S(2)}, u32[]{:S(2)}) collective-permute-start(bf16[160,512]{1,0:T(8,128)(2,1)S(1)} %get-tuple-element.52), channel_id=1, source_target_pairs={{0,48},{16,0},{32,16},{48,32},{1,49},{17,1},{33,17},{49,33},{2,50}... | collective-permute-start | bytes 491528 | tf_op jit(solution)/shard_map/ppermute | solution.py:30
  27.3 28.9 %collective-permute-start.10 = (bf16[16,512,512]{2,1,0:T(8,128)(2,1)}, bf16[16,512,512]{2,1,0:T(8,128)(2,1)S(1)}, u32[]{:S(2)}, u32[]{:S(2)}) collective-permute-start(bf16[16,512,512]{2,1,0:T(8,128)(2,1)} %shard_map.78), channel_id=1, source_target_pairs={{0,8},{8,0},{1,9},{9,1},{2,10},{10,2},{3,11},{11,3},{4,12},{12,4},... | collective-permute-start | bytes 25165832 | tf_op jit(solution)/shard_map/ppermute | solution.py:30
  27.3 19.7 %collective-permute-start.6 = (bf16[672,512]{1,0:T(8,128)(2,1)S(1)}, bf16[672,512]{1,0:T(8,128)(2,1)S(1)}, u32[]{:S(2)}, u32[]{:S(2)}) collective-permute-start(bf16[672,512]{1,0:T(8,128)(2,1)S(1)} %pad_maximum_fusion.refs_4_), channel_id=1, source_target_pairs={{0,16},{16,32},{32,48},{48,0},{1,17},{17,33},{33,49},{49,1},{2,18}... | collective-permute-start | bytes 2064392 | tf_op jit(solution)/shard_map/ppermute | solution.py:30
  28.0 19.1 %collective-permute-start.7 = (bf16[672,512]{1,0:T(8,128)(2,1)S(1)}, bf16[672,512]{1,0:T(8,128)(2,1)S(1)}, u32[]{:S(2)}, u32[]{:S(2)}) collective-permute-start(bf16[672,512]{1,0:T(8,128)(2,1)S(1)} %pad_maximum_fusion.refs_4_), channel_id=1, source_target_pairs={{0,48},{16,0},{32,16},{48,32},{1,49},{17,1},{33,17},{49,33},{2,50}... | collective-permute-start | bytes 2064392 | tf_op jit(solution)/shard_map/ppermute | solution.py:30
  30.7 15.3 %collective-permute-start.8 = (bf16[256,512]{1,0:T(8,128)(2,1)S(1)}, bf16[256,512]{1,0:T(8,128)(2,1)S(1)}, u32[]{:S(2)}, u32[]{:S(2)}) collective-permute-start(bf16[256,512]{1,0:T(8,128)(2,1)S(1)} %pad_maximum_fusion.3), channel_id=1, source_target_pairs={{0,64},{64,128},{128,192},{192,0},{1,65},{65,129},{129,193},{193,1... | collective-permute-start | bytes 786440 | tf_op jit(solution)/shard_map/ppermute | solution.py:30
  36.8 10.2 %collective-permute-start.9 = (bf16[256,512]{1,0:T(8,128)(2,1)S(1)}, bf16[256,512]{1,0:T(8,128)(2,1)S(1)}, u32[]{:S(2)}, u32[]{:S(2)}) collective-permute-start(bf16[256,512]{1,0:T(8,128)(2,1)S(1)} %pad_maximum_fusion.3), channel_id=1, source_target_pairs={{0,192},{64,0},{128,64},{192,128},{1,193},{65,1},{129,65},{193,129... | collective-permute-start | bytes 786440 | tf_op jit(solution)/shard_map/ppermute | solution.py:30
  47.2 16.9 %collective-permute-start.12 = (bf16[384,512]{1,0:T(8,128)(2,1)S(1)}, bf16[384,512]{1,0:T(8,128)(2,1)S(1)}, u32[]{:S(2)}, u32[]{:S(2)}) collective-permute-start(bf16[384,512]{1,0:T(8,128)(2,1)S(1)} %pad_maximum_fusion.2), channel_id=1, source_target_pairs={{0,48},{16,0},{32,16},{48,32},{1,49},{17,1},{33,17},{49,33},{2,50}... | collective-permute-start | bytes 1179656 | tf_op jit(solution)/shard_map/ppermute | solution.py:30
  49.6 14.5 %collective-permute-start.11 = (bf16[384,512]{1,0:T(8,128)(2,1)S(1)}, bf16[384,512]{1,0:T(8,128)(2,1)S(1)}, u32[]{:S(2)}, u32[]{:S(2)}) collective-permute-start(bf16[384,512]{1,0:T(8,128)(2,1)S(1)} %pad_maximum_fusion.1), channel_id=1, source_target_pairs={{0,16},{16,32},{32,48},{48,0},{1,17},{17,33},{33,49},{49,1},{2,18}... | collective-permute-start | bytes 1179656 | tf_op jit(solution)/shard_map/ppermute | solution.py:30
  49.8 14.2 %collective-permute-start.13 = (bf16[128,512]{1,0:T(8,128)(2,1)S(1)}, bf16[128,512]{1,0:T(8,128)(2,1)S(1)}, u32[]{:S(2)}, u32[]{:S(2)}) collective-permute-start(bf16[128,512]{1,0:T(8,128)(2,1)S(1)} %slice.50), channel_id=1, source_target_pairs={{0,64},{64,128},{128,192},{192,0},{1,65},{65,129},{129,193},{193,1... | collective-permute-start | bytes 393224 | tf_op jit(solution)/shard_map/ppermute | solution.py:30
  55.9 8.2 %collective-permute-start.14 = (bf16[128,512]{1,0:T(8,128)(2,1)S(1)}, bf16[128,512]{1,0:T(8,128)(2,1)S(1)}, u32[]{:S(2)}, u32[]{:S(2)}) collective-permute-start(bf16[128,512]{1,0:T(8,128)(2,1)S(1)} %slice.51), channel_id=1, source_target_pairs={{0,192},{64,0},{128,64},{192,128},{1,193},{65,1},{129,65},{193,129... | collective-permute-start | bytes 393224 | tf_op jit(solution)/shard_map/ppermute | solution.py:30
  67.5 2.9 %collective-permute-start.15 = (f32[256,1024]{1,0:T(8,128)S(1)}, f32[256,1024]{1,0:T(8,128)S(1)}, u32[]{:S(2)}, u32[]{:S(2)}) collective-permute-start(f32[256,1024]{1,0:T(8,128)S(1)} %shard_map.82.mine), channel_id=1, source_target_pairs={{0,8},{8,0},{1,9},{9,1},{2,10},{10,2},{3,11},{11,3},{4,12},{12,4},... | collective-permute-start | bytes 3145736 | tf_op jit(solution)/shard_map/ppermute | solution.py:30
  67.6 2.6 %collective-permute-start.16 = (f32[3,512]{1,0:T(4,128)S(1)}, f32[3,512]{1,0:T(4,128)S(1)}, u32[]{:S(2)}, u32[]{:S(2)}) collective-permute-start(f32[3,512]{1,0:T(4,128)S(1)} %pad_maximum_fusion.4), channel_id=1, source_target_pairs={{0,8},{8,0},{1,9},{9,1},{2,10},{10,2},{3,11},{11,3},{4,12},{12,4},... | collective-permute-start | bytes 18440 | tf_op jit(solution)/shard_map/ppermute | solution.py:30
  92.7 15.5 %collective-permute-start.17 = (bf16[576,512]{1,0:T(8,128)(2,1)S(1)}, bf16[576,512]{1,0:T(8,128)(2,1)S(1)}, u32[]{:S(2)}, u32[]{:S(2)}) collective-permute-start(bf16[576,512]{1,0:T(8,128)(2,1)S(1)} %get-tuple-element.71), channel_id=1, source_target_pairs={{0,16},{16,32},{32,48},{48,0},{1,17},{17,33},{33,49},{49,1},{2,18}... | collective-permute-start | bytes 1769480 | tf_op jit(solution)/shard_map/ppermute | solution.py:30
  92.7 15.4 %collective-permute-start.18 = (bf16[576,512]{1,0:T(8,128)(2,1)S(1)}, bf16[576,512]{1,0:T(8,128)(2,1)S(1)}, u32[]{:S(2)}, u32[]{:S(2)}) collective-permute-start(bf16[576,512]{1,0:T(8,128)(2,1)S(1)} %get-tuple-element.72), channel_id=1, source_target_pairs={{0,48},{16,0},{32,16},{48,32},{1,49},{17,1},{33,17},{49,33},{2,50}... | collective-permute-start | bytes 1769480 | tf_op jit(solution)/shard_map/ppermute | solution.py:30
  96.0 15.8 %collective-permute-start.19 = (bf16[256,512]{1,0:T(8,128)(2,1)S(1)}, bf16[256,512]{1,0:T(8,128)(2,1)S(1)}, u32[]{:S(2)}, u32[]{:S(2)}) collective-permute-start(bf16[256,512]{1,0:T(8,128)(2,1)S(1)} %get-tuple-element.77), channel_id=1, source_target_pairs={{0,64},{64,128},{128,192},{192,0},{1,65},{65,129},{129,193},{193,1... | collective-permute-start | bytes 786440 | tf_op jit(solution)/shard_map/ppermute | solution.py:30
  96.0 15.8 %collective-permute-start.20 = (bf16[256,512]{1,0:T(8,128)(2,1)S(1)}, bf16[256,512]{1,0:T(8,128)(2,1)S(1)}, u32[]{:S(2)}, u32[]{:S(2)}) collective-permute-start(bf16[256,512]{1,0:T(8,128)(2,1)S(1)} %get-tuple-element.78), channel_id=1, source_target_pairs={{0,192},{64,0},{128,64},{192,128},{1,193},{65,1},{129,65},{193,129... | collective-permute-start | bytes 786440 | tf_op jit(solution)/shard_map/ppermute | solution.py:30
  108.3 8.5 %collective-permute-start.23 = (bf16[288,512]{1,0:T(8,128)(2,1)S(1)}, bf16[288,512]{1,0:T(8,128)(2,1)S(1)}, u32[]{:S(2)}, u32[]{:S(2)}) collective-permute-start(bf16[288,512]{1,0:T(8,128)(2,1)S(1)} %get-tuple-element.88), channel_id=1, source_target_pairs={{0,16},{16,32},{32,48},{48,0},{1,17},{17,33},{33,49},{49,1},{2,18}... | collective-permute-start | bytes 884744 | tf_op jit(solution)/shard_map/ppermute | solution.py:30
  109.7 7.0 %collective-permute-start.24 = (bf16[288,512]{1,0:T(8,128)(2,1)S(1)}, bf16[288,512]{1,0:T(8,128)(2,1)S(1)}, u32[]{:S(2)}, u32[]{:S(2)}) collective-permute-start(bf16[288,512]{1,0:T(8,128)(2,1)S(1)} %get-tuple-element.89), channel_id=1, source_target_pairs={{0,48},{16,0},{32,16},{48,32},{1,49},{17,1},{33,17},{49,33},{2,50}... | collective-permute-start | bytes 884744 | tf_op jit(solution)/shard_map/ppermute | solution.py:30
  111.9 8.5 %collective-permute-start.21 = (bf16[128,512]{1,0:T(8,128)(2,1)S(1)}, bf16[128,512]{1,0:T(8,128)(2,1)S(1)}, u32[]{:S(2)}, u32[]{:S(2)}) collective-permute-start(bf16[128,512]{1,0:T(8,128)(2,1)S(1)} %get-tuple-element.81), channel_id=1, source_target_pairs={{0,64},{64,128},{128,192},{192,0},{1,65},{65,129},{129,193},{193,1... | collective-permute-start | bytes 393224 | tf_op jit(solution)/shard_map/ppermute | solution.py:30
  112.6 7.8 %collective-permute-start.22 = (bf16[128,512]{1,0:T(8,128)(2,1)S(1)}, bf16[128,512]{1,0:T(8,128)(2,1)S(1)}, u32[]{:S(2)}, u32[]{:S(2)}) collective-permute-start(bf16[128,512]{1,0:T(8,128)(2,1)S(1)} %get-tuple-element.82), channel_id=1, source_target_pairs={{0,192},{64,0},{128,64},{192,128},{1,193},{65,1},{129,65},{193,129... | collective-permute-start | bytes 393224 | tf_op jit(solution)/shard_map/ppermute | solution.py:30
  120.6 10.2 %collective-permute-start.25 = (bf16[256,512]{1,0:T(8,128)(2,1)S(1)}, bf16[256,512]{1,0:T(8,128)(2,1)S(1)}, u32[]{:S(2)}, u32[]{:S(2)}) collective-permute-start(bf16[256,512]{1,0:T(8,128)(2,1)S(1)} %get-tuple-element.92), channel_id=1, source_target_pairs={{0,16},{16,32},{32,48},{48,0},{1,17},{17,33},{33,49},{49,1},{2,18}... | collective-permute-start | bytes 786440 | tf_op jit(solution)/shard_map/ppermute | solution.py:30
  120.6 10.1 %collective-permute-start.26 = (bf16[256,512]{1,0:T(8,128)(2,1)S(1)}, bf16[256,512]{1,0:T(8,128)(2,1)S(1)}, u32[]{:S(2)}, u32[]{:S(2)}) collective-permute-start(bf16[256,512]{1,0:T(8,128)(2,1)S(1)} %get-tuple-element.93), channel_id=1, source_target_pairs={{0,48},{16,0},{32,16},{48,32},{1,49},{17,1},{33,17},{49,33},{2,50}... | collective-permute-start | bytes 786440 | tf_op jit(solution)/shard_map/ppermute | solution.py:30
  123.9 10.8 %collective-permute-start.29 = (bf16[192,512]{1,0:T(8,128)(2,1)S(1)}, bf16[192,512]{1,0:T(8,128)(2,1)S(1)}, u32[]{:S(2)}, u32[]{:S(2)}) collective-permute-start(bf16[192,512]{1,0:T(8,128)(2,1)S(1)} %get-tuple-element.90._), channel_id=1, source_target_pairs={{0,64},{64,128},{128,192},{192,0},{1,65},{65,129},{129,193},{193,1... | collective-permute-start | bytes 589832 | tf_op jit(solution)/shard_map/ppermute | solution.py:30
  125.0 16.1 %collective-permute-start.30 = (bf16[192,512]{1,0:T(8,128)(2,1)S(1)}, bf16[192,512]{1,0:T(8,128)(2,1)S(1)}, u32[]{:S(2)}, u32[]{:S(2)}) collective-permute-start(bf16[192,512]{1,0:T(8,128)(2,1)S(1)} %get-tuple-element.98), channel_id=1, source_target_pairs={{0,128},{64,192},{128,0},{192,64},{1,129},{65,193},{129,1},{193,65... | collective-permute-start | bytes 589832 | tf_op jit(solution)/shard_map/ppermute | solution.py:30
  129.1 14.9 %collective-permute-start.31 = (bf16[192,512]{1,0:T(8,128)(2,1)S(1)}, bf16[192,512]{1,0:T(8,128)(2,1)S(1)}, u32[]{:S(2)}, u32[]{:S(2)}) collective-permute-start(bf16[192,512]{1,0:T(8,128)(2,1)S(1)} %get-tuple-element.99), channel_id=1, source_target_pairs={{0,192},{64,0},{128,64},{192,128},{1,193},{65,1},{129,65},{193,129... | collective-permute-start | bytes 589832 | tf_op jit(solution)/shard_map/ppermute | solution.py:30
  130.8 13.2 %collective-permute-start.27 = (bf16[128,512]{1,0:T(8,128)(2,1)S(1)}, bf16[128,512]{1,0:T(8,128)(2,1)S(1)}, u32[]{:S(2)}, u32[]{:S(2)}) collective-permute-start(bf16[128,512]{1,0:T(8,128)(2,1)S(1)} %get-tuple-element.96), channel_id=1, source_target_pairs={{0,16},{16,32},{32,48},{48,0},{1,17},{17,33},{33,49},{49,1},{2,18}... | collective-permute-start | bytes 393224 | tf_op jit(solution)/shard_map/ppermute | solution.py:30
  130.8 13.1 %collective-permute-start.28 = (bf16[128,512]{1,0:T(8,128)(2,1)S(1)}, bf16[128,512]{1,0:T(8,128)(2,1)S(1)}, u32[]{:S(2)}, u32[]{:S(2)}) collective-permute-start(bf16[128,512]{1,0:T(8,128)(2,1)S(1)} %get-tuple-element.97), channel_id=1, source_target_pairs={{0,48},{16,0},{32,16},{48,32},{1,49},{17,1},{33,17},{49,33},{2,50}... | collective-permute-start | bytes 393224 | tf_op jit(solution)/shard_map/ppermute | solution.py:30
  (14 other events, 100.9 us)

commit v3 on v2

--- a/solution.py
+++ b/solution.py
@@ -151,7 +151,6 @@
 
 
 LOGITS = jax.ShapeDtypeStruct((ROWS, 2 * TOK), F32)
-AHEAD = (1, 3, 2)
 
 
 def statistics(partial, other, hit):
@@ -170,12 +169,23 @@
     return local_call(body, outs, partial, other, hit)
 
 
-def gradient(logits, hit, stats, lse_rest, cotangent):
-    def body(logits_ref, hit_ref, s, rest, cot, loss, grad):
-        top = s[0]
-        row_max = jnp.max(top, axis=0, keepdims=True)
-        row_total = jnp.sum(s[1] * jnp.exp(top - row_max), axis=0, keepdims=True)
-        target_logit = jnp.sum(s[2], axis=0, keepdims=True)
+def merged(one, two):
+    top = jnp.maximum(one[0:1, :], two[0:1, :])
+    total = one[1:2, :] * jnp.exp(one[0:1, :] - top) + two[1:2, :] * jnp.exp(two[0:1, :] - top)
+    return jnp.concatenate([top, total, one[2:3, :] + two[2:3, :]], axis=0)
+
+
+def merge_four(mine, one, two, three):
+    def body(a, b, c, d, out):
+        out[...] = merged(merged(a[...], c[...]), merged(b[...], d[...]))
+
+    return local_call(body, [jax.ShapeDtypeStruct(mine.shape, F32)], mine, one, two, three)[0]
+
+
+def gradient(logits, hit, stats, other, lse_rest, cotangent):
+    def body(logits_ref, hit_ref, s, o, rest, cot, loss, grad):
+        whole_stats = merged(s[...], o[...])
+        row_max, row_total, target_logit = (whole_stats[k : k + 1, :] for k in range(3))
         lse_window = row_max + jnp.log(row_total)
         larger = jnp.maximum(lse_window, rest[...])
         log_total = larger + jnp.log(
@@ -191,59 +201,56 @@
         jax.ShapeDtypeStruct((1, 2 * TOK), F32),
         jax.ShapeDtypeStruct((ROWS, 2 * TOK), BF16),
     ]
-    return local_call(body, outs, logits, hit, stats, lse_rest, cotangent)
+    return local_call(body, outs, logits, hit, stats, other, lse_rest, cotangent)
 
 
 def gathered_logits(head, hidden, at, sibling_at):
-    def split(h, *outs):
-        for out, start in zip(outs, (0, PH, PR)):
-            out[...] = h[start : start + out.shape[0], :]
-
-    over_zh, over_x, far_x = local_call(
-        split, [jax.ShapeDtypeStruct((r, WIDE), BF16) for r in (PR, ROWS - PH, QR)], head
-    )
-    zb, za, zf = (move(over_zh, "zh", by) for by in (1, -1, 2))
-    xb, xa = move(over_x, "x", 1), move(over_x, "x", -1)
-    xf = move(far_x, "x", 2)
+    zb, za = move(head[:PR], "zh", 1), move(head[:PR], "zh", -1)
+    xb, xa = move(head, "x", 1), move(head, "x", -1)
     picked = pick(hidden, sibling_at, 50)
-    zb, za, zf, xb, xa, xf, picked = lax.optimization_barrier((zb, za, zf, xb, xa, xf, picked))
+    zb, za, xb, xa, picked = lax.optimization_barrier((zb, za, xb, xa, picked))
     theirs = move(picked, "c", 1)
-    p = jnp.concatenate([za, zb, zf, head[:PH]], axis=0)
-    q = jnp.concatenate([head[PR:], xa[PH:], xb[PH:], xf], axis=0)
+    zf1, zf2 = move(zb[:PH], "zh", 1), move(za[PH:], "zh", -1)
+    xf1, xf2 = move(xb[PR : PR + QH], "x", 1), move(xa[PR + QH :], "x", -1)
+    p = jnp.concatenate([za, zf1, zf2, zb], axis=0)
+    q = jnp.concatenate([head[PR:], xa[PR:], xf1, xf2, xb[PR:]], axis=0)
     pb, pa = move(p, "x", 1), move(p, "x", -1)
     qb, qa = move(q, "zh", 1), move(q, "zh", -1)
-    zf, at = lax.optimization_barrier((zf, at))
+    zf1, zf2, at = lax.optimization_barrier((zf1, zf2, at))
     mine = pick(hidden, at, 40)
-    pb, pa, qb, qa, mine = lax.optimization_barrier((pb, pa, qb, qa, mine))
-    pf1 = jnp.concatenate([pb[: 3 * PH], pb[3 * PR :]], axis=0)
-    pf2 = jnp.concatenate([pa[3 * PH : 3 * PR], xa[:PH]], axis=0)
+    blocks = (mine, theirs)
+
+    def first(add, refs, out):
+        head_ref, xa_ref, xb_ref, xf1_ref, xf2_ref, p_ref = refs
+        out[...] = jnp.zeros_like(out)
+        add(out, head_ref[...], 0)
+        add(out, xa_ref[...], 1)
+        add(out, xb_ref[...], 3)
+        add(out.at[PR : PR + QH], xf1_ref[...], 2)
+        add(out.at[PR + QH :], xf2_ref[...], 2)
+        for dz in (1, 2, 3):
+            add(out.at[:PR], p_ref[(dz - 1) * PR : dz * PR, :], 4 * dz)
+
+    total = logits_call(first, blocks, [head, xa, xb, xf1, xf2, p])
+    pb, pa, qb, qa, total = lax.optimization_barrier((pb, pa, qb, qa, total))
+    pf1 = jnp.concatenate([pb[: 3 * PH], xb[:PH]], axis=0)
+    pf2 = jnp.concatenate([pa[3 * PH :], xa[PH:PR]], axis=0)
     pf1, pf2 = move(pf1, "x", 1), move(pf2, "x", -1)
     qf1, qf2 = move(qb[: 2 * QR], "zh", 1), move(qa[2 * QR :], "zh", -1)
 
-    blocks = (mine, theirs)
-
-    def first(add, refs, out):
-        head_ref, xa_ref, xb_ref, xf_ref, p_ref = refs
-        out[...] = jnp.zeros_like(out)
-        add(out, head_ref[...], 0)
-        add(out.at[PH:], xa_ref[...], 1)
-        add(out.at[PH:], xb_ref[...], 3)
-        add(out.at[PR:], xf_ref[...], 2)
-        for k, dz in enumerate(AHEAD):
-            add(out.at[:PR], p_ref[k * PR : (k + 1) * PR, :], 4 * dz)
-
-    total = logits_call(first, blocks, [head, xa, xb, xf, p])
     def second(add, refs, out):
         pa_ref, pb_ref, qa_ref, qb_ref, total_ref = refs
         out[...] = total_ref[...]
-        for k, dz in enumerate(AHEAD):
-            part = slice(k * PR, (k + 1) * PR)
-            add(out.at[:PR], pa_ref[part, :], 4 * dz + 1)
-            add(out.at[:PR], pb_ref[part, :], 4 * dz + 3)
-        add(out.at[:PH], pa_ref[3 * PR :, :], 1)
-        add(out.at[:PH], pb_ref[3 * PR :, :], 3)
-        for j, dx in enumerate((0,) + AHEAD):
-            part = slice(j * QR, (j + 1) * QR)
+
+        @pl.loop(0, 3)
+        def _(k):
+            part = rows_at(k, PR)
+            add(out.at[:PR], pa_ref[part, :], 4 * k + 5)
+            add(out.at[:PR], pb_ref[part, :], 4 * k + 7)
+
+        @pl.loop(0, 4)
+        def _(dx):
+            part = rows_at(dx, QR)
             add(out.at[PR:], qa_ref[part, :], 4 + dx)
             add(out.at[PR:], qb_ref[part, :], 12 + dx)
 
@@ -253,15 +260,15 @@
         pf1_ref, pf2_ref, qf1_ref, qf2_ref, total_ref = refs
         out[...] = total_ref[...]
         add(out.at[:PR], pf1_ref[:PR, :], 4 + 2)
-        add(out.at[:PH], pf1_ref[PR : 3 * PH, :], 12 + 2)
-        add(out.at[PH:PR], pf2_ref[:PH, :], 12 + 2)
-        add(out.at[:PR], pf2_ref[PH : 3 * PH, :], 8 + 2)
+        add(out.at[:PH], pf1_ref[PR : 3 * PH, :], 8 + 2)
+        add(out.at[PH:PR], pf2_ref[:PH, :], 8 + 2)
+        add(out.at[:PR], pf2_ref[PH : 3 * PH, :], 12 + 2)
         add(out.at[:PH], pf1_ref[3 * PH :, :], 2)
         add(out.at[PH:PR], pf2_ref[3 * PH :, :], 2)
         add(out.at[PR:], qf1_ref[:QR, :], 8)
         add(out.at[PR:], qf1_ref[QR:, :], 8 + 1)
-        add(out.at[PR:], qf2_ref[:QR, :], 8 + 3)
-        add(out.at[PR:], qf2_ref[QR:, :], 8 + 2)
+        add(out.at[PR:], qf2_ref[:QR, :], 8 + 2)
+        add(out.at[PR:], qf2_ref[QR:, :], 8 + 3)
 
     total = logits_call(third, blocks, [pf1, pf2, qf1, qf2, total])
     return total, blocks
@@ -443,11 +450,9 @@
 
     partial, blocks = gathered_logits(head, hidden, at, sibling_at)
     logits, stats = statistics(partial, move(partial, "c", 1), hit)
-    stats = lax.all_to_all(
-        jnp.broadcast_to(stats[None], (8,) + stats.shape), TENSOR, split_axis=0, concat_axis=0, tiled=True
-    )
+    stats = merge_four(stats, *(move(stats, "y", by) for by in (1, 2, 3)))
     loss, grad = gradient(
-        logits, hit, jnp.swapaxes(stats, 0, 1), facts[1:2], facts[2:3]
+        logits, hit, stats, move(stats, "zl", 1), facts[1:2], facts[2:3]
     )
     return loss[0, :TOK], scattered_gradient(grad, blocks)
 

time: 145 us -> 140 us (0.966); the launches traced: 145 us -> 138 us
  blocking collectives: 13.1 us -> 0 us
  waiting for transfers between devices: 26.7 us -> 31.9 us
    all_to_all x1 -> x0, blocking collectives: 13.1 us -> none  [shards(): lax.all_to_all(jnp.broadcast_to(stats[None], (8,) + stats.shape), TENSOR,...]
    ppermute x32 -> x38, waiting for transfers between devices: 26.7 us -> 31.9 us  [move(): return lax.ppermute(value, axis, [(i, (i + by) % n) for i in range(n)])]
    ppermute x32 -> x38, starting transfers between devices: 65.4 us -> 66 us  [move(): return lax.ppermute(value, axis, [(i, (i + by) % n) for i in range(n)])]
  transfers between devices with their start and end apart: 32 -> 38, of which waited for: 10 -> 14; matrix products, arithmetic and copies ran while one was open for 1% -> 1% of each run, Pallas kernels for 16% -> 17%
where the time goes in v3:
time: 140 us; the launch traced here: 138 us
  starting transfers between devices  66 us (47%)
  Pallas kernels  37 us (26%)
  waiting for transfers between devices  31.9 us (23%)
  local copies, waits for them, and re-layouts  1.76 us (1%)
    ppermute x38, starting transfers between devices, move(): return lax.ppermute(value, axis, [(i, (i + by) % n) for i in range(n)])  66 us
    ppermute x38, waiting for transfers between devices, move(): return lax.ppermute(value, axis, [(i, (i + by) % n) for i in range(n)])  31.9 us
    pallas_call x12, Pallas kernels, local_call(): pl.pallas_call(body, out_shape=outs, in_specs=[whole(a.shape) for a in ar...  14.1 us
    pallas_call x2, Pallas kernels, pick(): pl.pallas_call(body, out_shape=jax.ShapeDtypeStruct((n, TOK, WIDE), BF16)...  11.7 us
    pallas_call x2, Pallas kernels, block_call(): pl.pallas_call(body, out_shape=outs, in_specs=[pl.BlockSpec(memory_space=...  11.2 us
  transfers between devices with their start and end apart: 38, of which 14 were waited for; matrix products, arithmetic and copies ran while one was open for 1% of the time, Pallas kernels for 17%

profile of v3, /device:TPU:8, one launch (start us, length us, event | category | flops | bytes accessed | tf_op | source)
XLA Modules:
  0.0 138.0 jit_solution(5955829597620145070)
XLA Ops:
  4.9 3.3 %collective-permute-start = (bf16[192,512]{1,0:T(8,128)(2,1)S(1)}, bf16[192,512]{1,0:T(8,128)(2,1)S(1)}, u32[]{:S(2)}, u32[]{:S(2)}) collective-permute-start(bf16[192,512]{1,0:T(8,128)(2,1)S(1)} %slice.55), channel_id=1, source_target_pairs={{0,64},{64,128},{128,192},{192,0},{1,65},{65,129},{129,193},{193,1... | collective-permute-start | bytes 589832 | tf_op jit(solution)/shard_map/ppermute | solution.py:30
  8.3 3.1 %collective-permute-start.1 = (bf16[192,512]{1,0:T(8,128)(2,1)S(1)}, bf16[192,512]{1,0:T(8,128)(2,1)S(1)}, u32[]{:S(2)}, u32[]{:S(2)}) collective-permute-start(bf16[192,512]{1,0:T(8,128)(2,1)S(1)} %slice.55), channel_id=1, source_target_pairs={{0,192},{64,0},{128,64},{192,128},{1,193},{65,1},{129,65},{193,129... | collective-permute-start | bytes 589832 | tf_op jit(solution)/shard_map/ppermute | solution.py:30
  11.4 7.5 %shard_map.77 = bf16[16,512,512]{2,1,0:T(8,128)(2,1)} custom-call(s32[16]{0:T(128)S(1)} %broadcast_add_fusion.1.at_ref, bf16[512,16384]{1,0:T(8,128)(2,1)} %h_ref.3), custom_call_target="tpu_custom_call" | custom-call | bytes 16777216 | tf_op jit(solution)/shard_map/pallas_call | solution.py:72
  18.9 2.1 %collective-permute-done.1 = bf16[192,512]{1,0:T(8,128)(2,1)S(1)} collective-permute-done((bf16[192,512]{1,0:T(8,128)(2,1)S(1)}, bf16[192,512]{1,0:T(8,128)(2,1)S(1)}, u32[]{:S(2)}, u32[]{:S(2)}) %collective-permute-start.1) | collective-permute-done | bytes 196640 | tf_op jit(solution)/shard_map/ppermute | solution.py:30
  21.1 3.7 %collective-permute-start.4 = (bf16[96,512]{1,0:T(8,128)(2,1)S(1)}, bf16[96,512]{1,0:T(8,128)(2,1)S(1)}, u32[]{:S(2)}, u32[]{:S(2)}) collective-permute-start(bf16[96,512]{1,0:T(8,128)(2,1)S(1)} %slice.56), channel_id=1, source_target_pairs={{0,64},{64,128},{128,192},{192,0},{1,65},{65,129},{129,193},{193,1... | collective-permute-start | bytes 294920 | tf_op jit(solution)/shard_map/ppermute | solution.py:30
  27.4 4.6 %collective-permute-done.9.refs_3_ = bf16[32,512]{1,0:T(8,128)(2,1)S(1)} collective-permute-done((bf16[32,512]{1,0:T(8,128)(2,1)S(1)}, bf16[32,512]{1,0:T(8,128)(2,1)S(1)}, u32[]{:S(2)}, u32[]{:S(2)}) %collective-permute-start.9) | collective-permute-done | bytes 32800 | tf_op jit(solution)/shard_map/ppermute | solution.py:30
  32.8 3.0 %collective-permute-start.8 = (bf16[576,512]{1,0:T(8,128)(2,1)S(1)}, bf16[576,512]{1,0:T(8,128)(2,1)S(1)}, u32[]{:S(2)}, u32[]{:S(2)}) collective-permute-start(bf16[576,512]{1,0:T(8,128)(2,1)S(1)} %constant_dynamic-update-slice_fusion.refs_5_), channel_id=1, source_target_pairs={{0,48},{16,0},{32,16},{48,32},{1,49},{17,1},{33,17},{49,33},{2,50}... | collective-permute-start | bytes 1769480 | tf_op jit(solution)/shard_map/ppermute | solution.py:30
  35.8 2.2 %collective-permute-start.11 = (bf16[256,512]{1,0:T(8,128)(2,1)S(1)}, bf16[256,512]{1,0:T(8,128)(2,1)S(1)}, u32[]{:S(2)}, u32[]{:S(2)}) collective-permute-start(bf16[256,512]{1,0:T(8,128)(2,1)S(1)} %slice_dynamic-update-slice_fusion), channel_id=1, source_target_pairs={{0,64},{64,128},{128,192},{192,0},{1,65},{65,129},{129,193},{193,1... | collective-permute-start | bytes 786440 | tf_op jit(solution)/shard_map/ppermute | solution.py:30
  38.0 2.0 %collective-permute-start.12 = (bf16[256,512]{1,0:T(8,128)(2,1)S(1)}, bf16[256,512]{1,0:T(8,128)(2,1)S(1)}, u32[]{:S(2)}, u32[]{:S(2)}) collective-permute-start(bf16[256,512]{1,0:T(8,128)(2,1)S(1)} %slice_dynamic-update-slice_fusion), channel_id=1, source_target_pairs={{0,192},{64,0},{128,64},{192,128},{1,193},{65,1},{129,65},{193,129... | collective-permute-start | bytes 786440 | tf_op jit(solution)/shard_map/ppermute | solution.py:30
  40.1 4.2 %shard_map.78.m_ref = bf16[16,512,512]{2,1,0:T(8,128)(2,1)S(1)} custom-call(s32[16]{0:T(128)S(1)} %broadcast_add_fusion.at_ref, bf16[512,16384]{1,0:T(8,128)(2,1)} %h_ref.3), custom_call_target="tpu_custom_call" | custom-call | bytes 16777216 | tf_op jit(solution)/shard_map/pallas_call | solution.py:72
  44.3 2.6 %shard_map.79.refs_4_ = f32[256,1024]{1,0:T(8,128)S(1)} custom-call(bf16[16,512,512]{2,1,0:T(8,128)(2,1)S(1)} %shard_map.78.m_ref, bf16[16,512,512]{2,1,0:T(8,128)(2,1)S(1)} %collective-permute-done.6.t_ref, bf16[256,512]{1,0:T(8,128)(2,1)S(1)} %copy-done.3, bf16[256,512]{1,0:T(8,128)(2,1)S(1)} %collective-permute-done.3.refs_1_, ...), custom_call_target="tpu_custom_call" | custom-call | bytes 19267584 | tf_op jit(solution)/shard_map/pallas_call | solution.py:45
  48.4 2.3 %collective-permute-done.12.refs_2_ = bf16[256,512]{1,0:T(8,128)(2,1)S(1)} collective-permute-done((bf16[256,512]{1,0:T(8,128)(2,1)S(1)}, bf16[256,512]{1,0:T(8,128)(2,1)S(1)}, u32[]{:S(2)}, u32[]{:S(2)}) %collective-permute-start.12) | collective-permute-done | bytes 262176 | tf_op jit(solution)/shard_map/ppermute | solution.py:30
  54.7 2.8 %collective-permute-start.16 = (bf16[128,512]{1,0:T(8,128)(2,1)S(1)}, bf16[128,512]{1,0:T(8,128)(2,1)S(1)}, u32[]{:S(2)}, u32[]{:S(2)}) collective-permute-start(bf16[128,512]{1,0:T(8,128)(2,1)S(1)} %slice.68), channel_id=1, source_target_pairs={{0,192},{64,0},{128,64},{192,128},{1,193},{65,1},{129,65},{193,129... | collective-permute-start | bytes 393224 | tf_op jit(solution)/shard_map/ppermute | solution.py:30
  57.5 5.6 %shard_map.80.refs_4_ = f32[256,1024]{1,0:T(8,128)S(1)} custom-call(bf16[16,512,512]{2,1,0:T(8,128)(2,1)S(1)} %shard_map.78.m_ref, bf16[16,512,512]{2,1,0:T(8,128)(2,1)S(1)} %collective-permute-done.6.t_ref, bf16[576,512]{1,0:T(8,128)(2,1)S(1)} %collective-permute-done.8.refs_0_, bf16[576,512]{1,0:T(8,128)(2,1)S(1)} %collective-permute-done.7.refs_1_, ...), custom_call_target="tpu_custom_call" | custom-call | bytes 20578304 | tf_op jit(solution)/shard_map/pallas_call | solution.py:45
  63.2 3.3 %shard_map.81.mine = f32[256,1024]{1,0:T(8,128)S(1)} custom-call(bf16[16,512,512]{2,1,0:T(8,128)(2,1)S(1)} %shard_map.78.m_ref, bf16[16,512,512]{2,1,0:T(8,128)(2,1)S(1)} %collective-permute-done.6.t_ref, bf16[384,512]{1,0:T(8,128)(2,1)S(1)} %collective-permute-done.13.refs_0_, bf16[384,512]{1,0:T(8,128)(2,1)S(1)} %collective-permute-done.14.refs_1_, ...), custom_call_target="tpu_custom_call" | custom-call | bytes 19922944 | tf_op jit(solution)/shard_map/pallas_call | solution.py:45
  67.3 1.9 %collective-permute-done.18 = f32[3,512]{1,0:T(4,128)S(1)} collective-permute-done((f32[3,512]{1,0:T(4,128)S(1)}, f32[3,512]{1,0:T(4,128)S(1)}, u32[]{:S(2)}, u32[]{:S(2)}) %collective-permute-start.18) | collective-permute-done | bytes 6176 | tf_op jit(solution)/shard_map/ppermute | solution.py:30
  72.7 2.4 %collective-permute-start.21 = (f32[3,1024]{1,0:T(4,128)S(1)}, f32[3,1024]{1,0:T(4,128)S(1)}, u32[]{:S(2)}, u32[]{:S(2)}) collective-permute-start(f32[3,1024]{1,0:T(4,128)S(1)} %get-tuple-element.58.a), channel_id=1, source_target_pairs={{0,3},{1,0},{2,1},{3,2},{4,7},{5,4},{6,5},{7,6},{8,11},{9,8},{10,9... | collective-permute-start | bytes 36872 | tf_op jit(solution)/shard_map/ppermute | solution.py:30
  75.1 1.9 %collective-permute-done.20.c = f32[3,1024]{1,0:T(4,128)S(1)} collective-permute-done((f32[3,1024]{1,0:T(4,128)S(1)}, f32[3,1024]{1,0:T(4,128)S(1)}, u32[]{:S(2)}, u32[]{:S(2)}) %collective-permute-start.20) | collective-permute-done | bytes 12320 | tf_op jit(solution)/shard_map/ppermute | solution.py:30
  77.7 3.1 %collective-permute-done.22.o = f32[3,1024]{1,0:T(4,128)S(1)} collective-permute-done((f32[3,1024]{1,0:T(4,128)S(1)}, f32[3,1024]{1,0:T(4,128)S(1)}, u32[]{:S(2)}, u32[]{:S(2)}) %collective-permute-start.22) | collective-permute-done | bytes 12320 | tf_op jit(solution)/shard_map/ppermute | solution.py:30
  81.2 8.1 %shard_map.85 = (bf16[576,512]{1,0:T(8,128)(2,1)S(1)}, bf16[576,512]{1,0:T(8,128)(2,1)S(1)}, bf16[256,512]{1,0:T(8,128)(2,1)S(1)}, bf16[256,512]{1,0:T(8,128)(2,...) custom-call(bf16[16,512,512]{2,1,0:T(8,128)(2,1)} %copy-done, ...), custom_call_target="tpu_custom_call" | custom-call | flops 3221225472 | bytes 12582912 | tf_op jit(solution)/shard_map/pallas_call | solution.py:113
  89.4 3.2 %collective-permute-start.24 = (bf16[576,512]{1,0:T(8,128)(2,1)S(1)}, bf16[576,512]{1,0:T(8,128)(2,1)S(1)}, u32[]{:S(2)}, u32[]{:S(2)}) collective-permute-start(bf16[576,512]{1,0:T(8,128)(2,1)S(1)} %get-tuple-element.62), channel_id=1, source_target_pairs={{0,48},{16,0},{32,16},{48,32},{1,49},{17,1},{33,17},{49,33},{2,50}... | collective-permute-start | bytes 1769480 | tf_op jit(solution)/shard_map/ppermute | solution.py:30
  94.1 2.7 %collective-permute-start.26 = (bf16[256,512]{1,0:T(8,128)(2,1)S(1)}, bf16[256,512]{1,0:T(8,128)(2,1)S(1)}, u32[]{:S(2)}, u32[]{:S(2)}) collective-permute-start(bf16[256,512]{1,0:T(8,128)(2,1)S(1)} %get-tuple-element.68), channel_id=1, source_target_pairs={{0,192},{64,0},{128,64},{192,128},{1,193},{65,1},{129,65},{193,129... | collective-permute-start | bytes 786440 | tf_op jit(solution)/shard_map/ppermute | solution.py:30
  96.7 3.1 %shard_map.86 = (f32[768,512]{1,0:T(8,128)S(1)}, f32[256,512]{1,0:T(8,128)S(1)}) custom-call(bf16[16,512,512]{2,1,0:T(8,128)(2,1)} %copy-done, bf16[16,512,512]{2,1,0:T(8,128)(2,1)} %copy-done.1, bf16[256,1024]{1,0:T(8,128)(2,1)S(1)} %get-tuple-element.60.refs_0_), custom_call_target="tpu_custom_call" | custom-call | flops 1073741824 | bytes 4194304 | tf_op jit(solution)/shard_map/pallas_call | solution.py:113
  99.8 3.5 %collective-permute-done.23.u.up = bf16[576,512]{1,0:T(8,128)(2,1)S(1)} collective-permute-done((bf16[576,512]{1,0:T(8,128)(2,1)S(1)}, bf16[576,512]{1,0:T(8,128)(2,1)S(1)}, u32[]{:S(2)}, u32[]{:S(2)}) %collective-permute-start.23) | collective-permute-done | bytes 589856 | tf_op jit(solution)/shard_map/ppermute | solution.py:30
  104.1 2.7 %collective-permute-start.30 = (bf16[288,512]{1,0:T(8,128)(2,1)S(1)}, bf16[288,512]{1,0:T(8,128)(2,1)S(1)}, u32[]{:S(2)}, u32[]{:S(2)}) collective-permute-start(bf16[288,512]{1,0:T(8,128)(2,1)S(1)} %get-tuple-element.79), channel_id=1, source_target_pairs={{0,48},{16,0},{32,16},{48,32},{1,49},{17,1},{33,17},{49,33},{2,50}... | collective-permute-start | bytes 884744 | tf_op jit(solution)/shard_map/ppermute | solution.py:30
  108.7 2.4 %collective-permute-start.28 = (bf16[128,512]{1,0:T(8,128)(2,1)S(1)}, bf16[128,512]{1,0:T(8,128)(2,1)S(1)}, u32[]{:S(2)}, u32[]{:S(2)}) collective-permute-start(bf16[128,512]{1,0:T(8,128)(2,1)S(1)} %get-tuple-element.72), channel_id=1, source_target_pairs={{0,192},{64,0},{128,64},{192,128},{1,193},{65,1},{129,65},{193,129... | collective-permute-start | bytes 393224 | tf_op jit(solution)/shard_map/ppermute | solution.py:30
  111.7 3.7 %collective-permute-done.27.up2 = bf16[128,512]{1,0:T(8,128)(2,1)S(1)} collective-permute-done((bf16[128,512]{1,0:T(8,128)(2,1)S(1)}, bf16[128,512]{1,0:T(8,128)(2,1)S(1)}, u32[]{:S(2)}, u32[]{:S(2)}) %collective-permute-start.27) | collective-permute-done | bytes 131104 | tf_op jit(solution)/shard_map/ppermute | solution.py:30
  116.2 3.2 %collective-permute-start.32 = (bf16[256,512]{1,0:T(8,128)(2,1)S(1)}, bf16[256,512]{1,0:T(8,128)(2,1)S(1)}, u32[]{:S(2)}, u32[]{:S(2)}) collective-permute-start(bf16[256,512]{1,0:T(8,128)(2,1)S(1)} %get-tuple-element.83), channel_id=1, source_target_pairs={{0,48},{16,0},{32,16},{48,32},{1,49},{17,1},{33,17},{49,33},{2,50}... | collective-permute-start | bytes 786440 | tf_op jit(solution)/shard_map/ppermute | solution.py:30
  119.5 2.4 %collective-permute-start.35 = (bf16[192,512]{1,0:T(8,128)(2,1)S(1)}, bf16[192,512]{1,0:T(8,128)(2,1)S(1)}, u32[]{:S(2)}, u32[]{:S(2)}) collective-permute-start(bf16[192,512]{1,0:T(8,128)(2,1)S(1)} %get-tuple-element.80._), channel_id=1, source_target_pairs={{0,64},{64,128},{128,192},{192,0},{1,65},{65,129},{129,193},{193,1... | collective-permute-start | bytes 589832 | tf_op jit(solution)/shard_map/ppermute | solution.py:30
  121.9 3.5 %collective-permute-start.36 = (bf16[192,512]{1,0:T(8,128)(2,1)S(1)}, bf16[192,512]{1,0:T(8,128)(2,1)S(1)}, u32[]{:S(2)}, u32[]{:S(2)}) collective-permute-start(bf16[192,512]{1,0:T(8,128)(2,1)S(1)} %get-tuple-element.88), channel_id=1, source_target_pairs={{0,128},{64,192},{128,0},{192,64},{1,129},{65,193},{129,1},{193,65... | collective-permute-start | bytes 589832 | tf_op jit(solution)/shard_map/ppermute | solution.py:30
  127.4 3.2 %collective-permute-start.34 = (bf16[128,512]{1,0:T(8,128)(2,1)S(1)}, bf16[128,512]{1,0:T(8,128)(2,1)S(1)}, u32[]{:S(2)}, u32[]{:S(2)}) collective-permute-start(bf16[128,512]{1,0:T(8,128)(2,1)S(1)} %get-tuple-element.87), channel_id=1, source_target_pairs={{0,48},{16,0},{32,16},{48,32},{1,49},{17,1},{33,17},{49,33},{2,50}... | collective-permute-start | bytes 393224 | tf_op jit(solution)/shard_map/ppermute | solution.py:30
  131.2 4.7 %collective-permute-done.36.z2 = bf16[192,512]{1,0:T(8,128)(2,1)S(1)} collective-permute-done((bf16[192,512]{1,0:T(8,128)(2,1)S(1)}, bf16[192,512]{1,0:T(8,128)(2,1)S(1)}, u32[]{:S(2)}, u32[]{:S(2)}) %collective-permute-start.36) | collective-permute-done | bytes 196640 | tf_op jit(solution)/shard_map/ppermute | solution.py:30
  (108 shorter events, 28.9 us)
Async XLA Ops:
  0.6 20.4 %collective-permute-start.2 = (bf16[256,512]{1,0:T(8,128)(2,1)}, bf16[256,512]{1,0:T(8,128)(2,1)S(1)}, u32[]{:S(2)}, u32[]{:S(2)}) collective-permute-start(bf16[256,512]{1,0:T(8,128)(2,1)} %refs_0_.1), channel_id=1, source_target_pairs={{0,16},{16,32},{32,48},{48,0},{1,17},{17,33},{33,49},{49,1},{2,18}... | collective-permute-start | bytes 786440 | tf_op jit(solution)/shard_map/ppermute | solution.py:30
  2.2 18.8 %collective-permute-start.3 = (bf16[256,512]{1,0:T(8,128)(2,1)}, bf16[256,512]{1,0:T(8,128)(2,1)S(1)}, u32[]{:S(2)}, u32[]{:S(2)}) collective-permute-start(bf16[256,512]{1,0:T(8,128)(2,1)} %refs_0_.1), channel_id=1, source_target_pairs={{0,48},{16,0},{32,16},{48,32},{1,49},{17,1},{33,17},{49,33},{2,50}... | collective-permute-start | bytes 786440 | tf_op jit(solution)/shard_map/ppermute | solution.py:30
  4.9 14.0 %collective-permute-start = (bf16[192,512]{1,0:T(8,128)(2,1)S(1)}, bf16[192,512]{1,0:T(8,128)(2,1)S(1)}, u32[]{:S(2)}, u32[]{:S(2)}) collective-permute-start(bf16[192,512]{1,0:T(8,128)(2,1)S(1)} %slice.55), channel_id=1, source_target_pairs={{0,64},{64,128},{128,192},{192,0},{1,65},{65,129},{129,193},{193,1... | collective-permute-start | bytes 589832 | tf_op jit(solution)/shard_map/ppermute | solution.py:30
  8.3 12.8 %collective-permute-start.1 = (bf16[192,512]{1,0:T(8,128)(2,1)S(1)}, bf16[192,512]{1,0:T(8,128)(2,1)S(1)}, u32[]{:S(2)}, u32[]{:S(2)}) collective-permute-start(bf16[192,512]{1,0:T(8,128)(2,1)S(1)} %slice.55), channel_id=1, source_target_pairs={{0,192},{64,0},{128,64},{192,128},{1,193},{65,1},{129,65},{193,129... | collective-permute-start | bytes 589832 | tf_op jit(solution)/shard_map/ppermute | solution.py:30
  21.0 23.3 %collective-permute-start.6 = (bf16[16,512,512]{2,1,0:T(8,128)(2,1)}, bf16[16,512,512]{2,1,0:T(8,128)(2,1)S(1)}, u32[]{:S(2)}, u32[]{:S(2)}) collective-permute-start(bf16[16,512,512]{2,1,0:T(8,128)(2,1)} %shard_map.77), channel_id=1, source_target_pairs={{0,8},{8,0},{1,9},{9,1},{2,10},{10,2},{3,11},{11,3},{4,12},{12,4},... | collective-permute-start | bytes 25165832 | tf_op jit(solution)/shard_map/ppermute | solution.py:30
  21.1 11.0 %collective-permute-start.4 = (bf16[96,512]{1,0:T(8,128)(2,1)S(1)}, bf16[96,512]{1,0:T(8,128)(2,1)S(1)}, u32[]{:S(2)}, u32[]{:S(2)}) collective-permute-start(bf16[96,512]{1,0:T(8,128)(2,1)S(1)} %slice.56), channel_id=1, source_target_pairs={{0,64},{64,128},{128,192},{192,0},{1,65},{65,129},{129,193},{193,1... | collective-permute-start | bytes 294920 | tf_op jit(solution)/shard_map/ppermute | solution.py:30
  24.8 7.6 %collective-permute-start.5 = (bf16[96,512]{1,0:T(8,128)(2,1)S(1)}, bf16[96,512]{1,0:T(8,128)(2,1)S(1)}, u32[]{:S(2)}, u32[]{:S(2)}) collective-permute-start(bf16[96,512]{1,0:T(8,128)(2,1)S(1)} %slice.57), channel_id=1, source_target_pairs={{0,192},{64,0},{128,64},{192,128},{1,193},{65,1},{129,65},{193,129... | collective-permute-start | bytes 294920 | tf_op jit(solution)/shard_map/ppermute | solution.py:30
  25.4 10.4 %collective-permute-start.10 = (bf16[32,512]{1,0:T(8,128)(2,1)S(1)}, bf16[32,512]{1,0:T(8,128)(2,1)S(1)}, u32[]{:S(2)}, u32[]{:S(2)}) collective-permute-start(bf16[32,512]{1,0:T(8,128)(2,1)S(1)} %slice.61), channel_id=1, source_target_pairs={{0,48},{16,0},{32,16},{48,32},{1,49},{17,1},{33,17},{49,33},{2,50}... | collective-permute-start | bytes 98312 | tf_op jit(solution)/shard_map/ppermute | solution.py:30
  32.5 18.2 %collective-permute-start.7 = (bf16[576,512]{1,0:T(8,128)(2,1)S(1)}, bf16[576,512]{1,0:T(8,128)(2,1)S(1)}, u32[]{:S(2)}, u32[]{:S(2)}) collective-permute-start(bf16[576,512]{1,0:T(8,128)(2,1)S(1)} %constant_dynamic-update-slice_fusion.refs_5_), channel_id=1, source_target_pairs={{0,16},{16,32},{32,48},{48,0},{1,17},{17,33},{33,49},{49,1},{2,18}... | collective-permute-start | bytes 1769480 | tf_op jit(solution)/shard_map/ppermute | solution.py:30
  32.8 17.8 %collective-permute-start.8 = (bf16[576,512]{1,0:T(8,128)(2,1)S(1)}, bf16[576,512]{1,0:T(8,128)(2,1)S(1)}, u32[]{:S(2)}, u32[]{:S(2)}) collective-permute-start(bf16[576,512]{1,0:T(8,128)(2,1)S(1)} %constant_dynamic-update-slice_fusion.refs_5_), channel_id=1, source_target_pairs={{0,48},{16,0},{32,16},{48,32},{1,49},{17,1},{33,17},{49,33},{2,50}... | collective-permute-start | bytes 1769480 | tf_op jit(solution)/shard_map/ppermute | solution.py:30
  35.8 12.6 %collective-permute-start.11 = (bf16[256,512]{1,0:T(8,128)(2,1)S(1)}, bf16[256,512]{1,0:T(8,128)(2,1)S(1)}, u32[]{:S(2)}, u32[]{:S(2)}) collective-permute-start(bf16[256,512]{1,0:T(8,128)(2,1)S(1)} %slice_dynamic-update-slice_fusion), channel_id=1, source_target_pairs={{0,64},{64,128},{128,192},{192,0},{1,65},{65,129},{129,193},{193,1... | collective-permute-start | bytes 786440 | tf_op jit(solution)/shard_map/ppermute | solution.py:30
  38.0 12.7 %collective-permute-start.12 = (bf16[256,512]{1,0:T(8,128)(2,1)S(1)}, bf16[256,512]{1,0:T(8,128)(2,1)S(1)}, u32[]{:S(2)}, u32[]{:S(2)}) collective-permute-start(bf16[256,512]{1,0:T(8,128)(2,1)S(1)} %slice_dynamic-update-slice_fusion), channel_id=1, source_target_pairs={{0,192},{64,0},{128,64},{192,128},{1,193},{65,1},{129,65},{193,129... | collective-permute-start | bytes 786440 | tf_op jit(solution)/shard_map/ppermute | solution.py:30
  50.7 12.4 %collective-permute-start.14 = (bf16[384,512]{1,0:T(8,128)(2,1)S(1)}, bf16[384,512]{1,0:T(8,128)(2,1)S(1)}, u32[]{:S(2)}, u32[]{:S(2)}) collective-permute-start(bf16[384,512]{1,0:T(8,128)(2,1)S(1)} %pad_maximum_fusion.1), channel_id=1, source_target_pairs={{0,48},{16,0},{32,16},{48,32},{1,49},{17,1},{33,17},{49,33},{2,50}... | collective-permute-start | bytes 1179656 | tf_op jit(solution)/shard_map/ppermute | solution.py:30
  52.2 11.0 %collective-permute-start.13 = (bf16[384,512]{1,0:T(8,128)(2,1)S(1)}, bf16[384,512]{1,0:T(8,128)(2,1)S(1)}, u32[]{:S(2)}, u32[]{:S(2)}) collective-permute-start(bf16[384,512]{1,0:T(8,128)(2,1)S(1)} %pad_maximum_fusion), channel_id=1, source_target_pairs={{0,16},{16,32},{32,48},{48,0},{1,17},{17,33},{33,49},{49,1},{2,18}... | collective-permute-start | bytes 1179656 | tf_op jit(solution)/shard_map/ppermute | solution.py:30
  53.2 10.0 %collective-permute-start.15 = (bf16[128,512]{1,0:T(8,128)(2,1)S(1)}, bf16[128,512]{1,0:T(8,128)(2,1)S(1)}, u32[]{:S(2)}, u32[]{:S(2)}) collective-permute-start(bf16[128,512]{1,0:T(8,128)(2,1)S(1)} %slice.67), channel_id=1, source_target_pairs={{0,64},{64,128},{128,192},{192,0},{1,65},{65,129},{129,193},{193,1... | collective-permute-start | bytes 393224 | tf_op jit(solution)/shard_map/ppermute | solution.py:30
  54.7 8.4 %collective-permute-start.16 = (bf16[128,512]{1,0:T(8,128)(2,1)S(1)}, bf16[128,512]{1,0:T(8,128)(2,1)S(1)}, u32[]{:S(2)}, u32[]{:S(2)}) collective-permute-start(bf16[128,512]{1,0:T(8,128)(2,1)S(1)} %slice.68), channel_id=1, source_target_pairs={{0,192},{64,0},{128,64},{192,128},{1,193},{65,1},{129,65},{193,129... | collective-permute-start | bytes 393224 | tf_op jit(solution)/shard_map/ppermute | solution.py:30
  71.7 5.2 %collective-permute-start.20 = (f32[3,1024]{1,0:T(4,128)S(1)}, f32[3,1024]{1,0:T(4,128)S(1)}, u32[]{:S(2)}, u32[]{:S(2)}) collective-permute-start(f32[3,1024]{1,0:T(4,128)S(1)} %get-tuple-element.58.a), channel_id=1, source_target_pairs={{0,2},{1,3},{2,0},{3,1},{4,6},{5,7},{6,4},{7,5},{8,10},{9,11},{10,... | collective-permute-start | bytes 36872 | tf_op jit(solution)/shard_map/ppermute | solution.py:30
  89.3 14.1 %collective-permute-start.23 = (bf16[576,512]{1,0:T(8,128)(2,1)S(1)}, bf16[576,512]{1,0:T(8,128)(2,1)S(1)}, u32[]{:S(2)}, u32[]{:S(2)}) collective-permute-start(bf16[576,512]{1,0:T(8,128)(2,1)S(1)} %get-tuple-element.61), channel_id=1, source_target_pairs={{0,16},{16,32},{32,48},{48,0},{1,17},{17,33},{33,49},{49,1},{2,18}... | collective-permute-start | bytes 1769480 | tf_op jit(solution)/shard_map/ppermute | solution.py:30
  89.4 14.0 %collective-permute-start.24 = (bf16[576,512]{1,0:T(8,128)(2,1)S(1)}, bf16[576,512]{1,0:T(8,128)(2,1)S(1)}, u32[]{:S(2)}, u32[]{:S(2)}) collective-permute-start(bf16[576,512]{1,0:T(8,128)(2,1)S(1)} %get-tuple-element.62), channel_id=1, source_target_pairs={{0,48},{16,0},{32,16},{48,32},{1,49},{17,1},{33,17},{49,33},{2,50}... | collective-permute-start | bytes 1769480 | tf_op jit(solution)/shard_map/ppermute | solution.py:30
  92.6 14.2 %collective-permute-start.25 = (bf16[256,512]{1,0:T(8,128)(2,1)S(1)}, bf16[256,512]{1,0:T(8,128)(2,1)S(1)}, u32[]{:S(2)}, u32[]{:S(2)}) collective-permute-start(bf16[256,512]{1,0:T(8,128)(2,1)S(1)} %get-tuple-element.67), channel_id=1, source_target_pairs={{0,64},{64,128},{128,192},{192,0},{1,65},{65,129},{129,193},{193,1... | collective-permute-start | bytes 786440 | tf_op jit(solution)/shard_map/ppermute | solution.py:30
  94.1 12.7 %collective-permute-start.26 = (bf16[256,512]{1,0:T(8,128)(2,1)S(1)}, bf16[256,512]{1,0:T(8,128)(2,1)S(1)}, u32[]{:S(2)}, u32[]{:S(2)}) collective-permute-start(bf16[256,512]{1,0:T(8,128)(2,1)S(1)} %get-tuple-element.68), channel_id=1, source_target_pairs={{0,192},{64,0},{128,64},{192,128},{1,193},{65,1},{129,65},{193,129... | collective-permute-start | bytes 786440 | tf_op jit(solution)/shard_map/ppermute | solution.py:30
  103.5 8.0 %collective-permute-start.29 = (bf16[288,512]{1,0:T(8,128)(2,1)S(1)}, bf16[288,512]{1,0:T(8,128)(2,1)S(1)}, u32[]{:S(2)}, u32[]{:S(2)}) collective-permute-start(bf16[288,512]{1,0:T(8,128)(2,1)S(1)} %get-tuple-element.78), channel_id=1, source_target_pairs={{0,16},{16,32},{32,48},{48,0},{1,17},{17,33},{33,49},{49,1},{2,18}... | collective-permute-start | bytes 884744 | tf_op jit(solution)/shard_map/ppermute | solution.py:30
  104.1 7.4 %collective-permute-start.30 = (bf16[288,512]{1,0:T(8,128)(2,1)S(1)}, bf16[288,512]{1,0:T(8,128)(2,1)S(1)}, u32[]{:S(2)}, u32[]{:S(2)}) collective-permute-start(bf16[288,512]{1,0:T(8,128)(2,1)S(1)} %get-tuple-element.79), channel_id=1, source_target_pairs={{0,48},{16,0},{32,16},{48,32},{1,49},{17,1},{33,17},{49,33},{2,50}... | collective-permute-start | bytes 884744 | tf_op jit(solution)/shard_map/ppermute | solution.py:30
  106.8 8.6 %collective-permute-start.27 = (bf16[128,512]{1,0:T(8,128)(2,1)S(1)}, bf16[128,512]{1,0:T(8,128)(2,1)S(1)}, u32[]{:S(2)}, u32[]{:S(2)}) collective-permute-start(bf16[128,512]{1,0:T(8,128)(2,1)S(1)} %get-tuple-element.71), channel_id=1, source_target_pairs={{0,64},{64,128},{128,192},{192,0},{1,65},{65,129},{129,193},{193,1... | collective-permute-start | bytes 393224 | tf_op jit(solution)/shard_map/ppermute | solution.py:30
  108.7 7.3 %collective-permute-start.28 = (bf16[128,512]{1,0:T(8,128)(2,1)S(1)}, bf16[128,512]{1,0:T(8,128)(2,1)S(1)}, u32[]{:S(2)}, u32[]{:S(2)}) collective-permute-start(bf16[128,512]{1,0:T(8,128)(2,1)S(1)} %get-tuple-element.72), channel_id=1, source_target_pairs={{0,192},{64,0},{128,64},{192,128},{1,193},{65,1},{129,65},{193,129... | collective-permute-start | bytes 393224 | tf_op jit(solution)/shard_map/ppermute | solution.py:30
  116.2 11.1 %collective-permute-start.31 = (bf16[256,512]{1,0:T(8,128)(2,1)S(1)}, bf16[256,512]{1,0:T(8,128)(2,1)S(1)}, u32[]{:S(2)}, u32[]{:S(2)}) collective-permute-start(bf16[256,512]{1,0:T(8,128)(2,1)S(1)} %get-tuple-element.82), channel_id=1, source_target_pairs={{0,16},{16,32},{32,48},{48,0},{1,17},{17,33},{33,49},{49,1},{2,18}... | collective-permute-start | bytes 786440 | tf_op jit(solution)/shard_map/ppermute | solution.py:30
  116.2 11.0 %collective-permute-start.32 = (bf16[256,512]{1,0:T(8,128)(2,1)S(1)}, bf16[256,512]{1,0:T(8,128)(2,1)S(1)}, u32[]{:S(2)}, u32[]{:S(2)}) collective-permute-start(bf16[256,512]{1,0:T(8,128)(2,1)S(1)} %get-tuple-element.83), channel_id=1, source_target_pairs={{0,48},{16,0},{32,16},{48,32},{1,49},{17,1},{33,17},{49,33},{2,50}... | collective-permute-start | bytes 786440 | tf_op jit(solution)/shard_map/ppermute | solution.py:30
  119.5 11.7 %collective-permute-start.35 = (bf16[192,512]{1,0:T(8,128)(2,1)S(1)}, bf16[192,512]{1,0:T(8,128)(2,1)S(1)}, u32[]{:S(2)}, u32[]{:S(2)}) collective-permute-start(bf16[192,512]{1,0:T(8,128)(2,1)S(1)} %get-tuple-element.80._), channel_id=1, source_target_pairs={{0,64},{64,128},{128,192},{192,0},{1,65},{65,129},{129,193},{193,1... | collective-permute-start | bytes 589832 | tf_op jit(solution)/shard_map/ppermute | solution.py:30
  121.9 14.0 %collective-permute-start.36 = (bf16[192,512]{1,0:T(8,128)(2,1)S(1)}, bf16[192,512]{1,0:T(8,128)(2,1)S(1)}, u32[]{:S(2)}, u32[]{:S(2)}) collective-permute-start(bf16[192,512]{1,0:T(8,128)(2,1)S(1)} %get-tuple-element.88), channel_id=1, source_target_pairs={{0,128},{64,192},{128,0},{192,64},{1,129},{65,193},{129,1},{193,65... | collective-permute-start | bytes 589832 | tf_op jit(solution)/shard_map/ppermute | solution.py:30
  125.4 11.6 %collective-permute-start.37 = (bf16[192,512]{1,0:T(8,128)(2,1)S(1)}, bf16[192,512]{1,0:T(8,128)(2,1)S(1)}, u32[]{:S(2)}, u32[]{:S(2)}) collective-permute-start(bf16[192,512]{1,0:T(8,128)(2,1)S(1)} %get-tuple-element.89), channel_id=1, source_target_pairs={{0,192},{64,0},{128,64},{192,128},{1,193},{65,1},{129,65},{193,129... | collective-permute-start | bytes 589832 | tf_op jit(solution)/shard_map/ppermute | solution.py:30
  127.3 9.7 %collective-permute-start.33 = (bf16[128,512]{1,0:T(8,128)(2,1)S(1)}, bf16[128,512]{1,0:T(8,128)(2,1)S(1)}, u32[]{:S(2)}, u32[]{:S(2)}) collective-permute-start(bf16[128,512]{1,0:T(8,128)(2,1)S(1)} %get-tuple-element.86), channel_id=1, source_target_pairs={{0,16},{16,32},{32,48},{48,0},{1,17},{17,33},{33,49},{49,1},{2,18}... | collective-permute-start | bytes 393224 | tf_op jit(solution)/shard_map/ppermute | solution.py:30
  127.4 9.6 %collective-permute-start.34 = (bf16[128,512]{1,0:T(8,128)(2,1)S(1)}, bf16[128,512]{1,0:T(8,128)(2,1)S(1)}, u32[]{:S(2)}, u32[]{:S(2)}) collective-permute-start(bf16[128,512]{1,0:T(8,128)(2,1)S(1)} %get-tuple-element.87), channel_id=1, source_target_pairs={{0,48},{16,0},{32,16},{48,32},{1,49},{17,1},{33,17},{49,33},{2,50}... | collective-permute-start | bytes 393224 | tf_op jit(solution)/shard_map/ppermute | solution.py:30
  (14 other events, 103.2 us)

commit v4 on v3

--- a/solution.py
+++ b/solution.py
@@ -120,7 +120,7 @@
             pltpu.VMEM((places, 2 * TOK, WIDE), BF16),
             pltpu.SemaphoreType.DMA((places, 2)),
         ],
-        compiler_params=params(50),
+        compiler_params=params(46),
         cost_estimate=pl.CostEstimate(
             flops=4 * rows * WIDE * TOK,
             bytes_accessed=2 * len(slots) * TOK * WIDE * 2,
@@ -207,7 +207,7 @@
 def gathered_logits(head, hidden, at, sibling_at):
     zb, za = move(head[:PR], "zh", 1), move(head[:PR], "zh", -1)
     xb, xa = move(head, "x", 1), move(head, "x", -1)
-    picked = pick(hidden, sibling_at, 50)
+    picked = pick(hidden, sibling_at, 44)
     zb, za, xb, xa, picked = lax.optimization_barrier((zb, za, xb, xa, picked))
     theirs = move(picked, "c", 1)
     zf1, zf2 = move(zb[:PH], "zh", 1), move(za[PH:], "zh", -1)
@@ -217,7 +217,7 @@
     pb, pa = move(p, "x", 1), move(p, "x", -1)
     qb, qa = move(q, "zh", 1), move(q, "zh", -1)
     zf1, zf2, at = lax.optimization_barrier((zf1, zf2, at))
-    mine = pick(hidden, at, 40)
+    mine = pick(hidden, at, 30)
     blocks = (mine, theirs)
 
     def first(add, refs, out):
@@ -291,15 +291,17 @@
     ]
     def others_terms(block, refs, outs):
         (g_ref,) = refs
-        p_up, p_down, q_up, q_down, p_ahead, p_behind, p_here, q_ahead, q_behind = outs
+        p_up, p_down, q_up, q_down, p_ahead, p_behind, p_here, q_ahead, q_behind, q_scratch = outs
 
         @pl.loop(0, 3)
         def _(k):
             first, last = pl.ds(pl.multiple_of(k * PR, PR), PH), pl.ds(pl.multiple_of(k * PR + PH, PH), PH)
             kept = rows_at(k, PH)
-            for dx in range(4):
-                term = jnp.dot(g_ref[...], block(4 * k + dx), preferred_element_type=F32)
-                one, two, three, four = term[:PH], term[PH:PR], term[PR : PR + QH], term[PR + QH :]
+            held = [block(4 * k + dx) for dx in range(4)]
+            for dx in (2, 1, 3, 0):
+                term = jnp.dot(g_ref[:, :TOK], held[dx][:TOK], preferred_element_type=F32)
+                term += jnp.dot(g_ref[:, TOK:], held[dx][TOK:], preferred_element_type=F32)
+                one, two = term[:PH], term[PH:PR]
                 if dx == 0:
                     p_here[rows_at(k, PR), :] = term[:PR]
                 elif dx == 1:
@@ -311,7 +313,11 @@
                 else:
                     p_down[first, :] = one.astype(BF16)
                     p_behind[kept, :] = two
+                q_scratch[dx] = term[PR:]
+
+            for dx in range(4):
                 start, middle = dx * QR, dx * QR + QH
+                three, four = q_scratch[dx, :QH], q_scratch[dx, QH:]
 
                 @pl.when(k == 0)
                 def _():
@@ -329,8 +335,9 @@
                     q_behind[dx * QH : (dx + 1) * QH, :] = four
 
     slots = {place: 4 + place for place in range(12)}
-    p_up, p_down, q_up, q_down, p_ahead, p_behind, p_here, q_ahead, q_behind = block_call(
-        others_terms, slots, outs, blocks, [grad], 12 * ROWS
+    q_rows = jax.ShapeDtypeStruct((4, QR, WIDE), F32)
+    p_up, p_down, q_up, q_down, p_ahead, p_behind, p_here, q_ahead, q_behind, _ = block_call(
+        others_terms, slots, outs + [q_rows], blocks, [grad], 12 * ROWS
     )
     p_up, p_down = move(p_up, "x", 1), move(p_down, "x", -1)
     q_up, q_down = move(q_up, "zh", 1), move(q_down, "zh", -1)

time: 140 us -> 139 us (level)
  Pallas kernels: 37 us -> 33 us
  waiting for transfers between devices: 31.9 us -> 35.2 us
    ppermute x38, waiting for transfers between devices: 31.9 us -> 35.2 us  [move(): return lax.ppermute(value, axis, [(i, (i + by) % n) for i in range(n)])]
    pallas_call x2, Pallas kernels: 11.7 us -> 8.43 us  [pick(): pl.pallas_call(body, out_shape=jax.ShapeDtypeStruct((n, TOK, WIDE), BF16)...]
  transfers between devices with their start and end apart: 38 -> 38, of which waited for: 14 -> 15; matrix products, arithmetic and copies ran while one was open for 1% -> 1% of each run, Pallas kernels for 17% -> 15%
where the time goes in v4:
time: 139 us; the launch traced here: 138 us
  starting transfers between devices  66.8 us (48%)
  waiting for transfers between devices  35.2 us (25%)
  Pallas kernels  33 us (24%)
  local copies, waits for them, and re-layouts  1.75 us (1%)
    ppermute x38, starting transfers between devices, move(): return lax.ppermute(value, axis, [(i, (i + by) % n) for i in range(n)])  66.8 us
    ppermute x38, waiting for transfers between devices, move(): return lax.ppermute(value, axis, [(i, (i + by) % n) for i in range(n)])  35.2 us
    pallas_call x12, Pallas kernels, local_call(): pl.pallas_call(body, out_shape=outs, in_specs=[whole(a.shape) for a in ar...  14 us
    pallas_call x2, Pallas kernels, block_call(): pl.pallas_call(body, out_shape=outs, in_specs=[pl.BlockSpec(memory_space=...  10.6 us
    pallas_call x2, Pallas kernels, pick(): pl.pallas_call(body, out_shape=jax.ShapeDtypeStruct((n, TOK, WIDE), BF16)...  8.43 us
  transfers between devices with their start and end apart: 38, of which 15 were waited for; matrix products, arithmetic and copies ran while one was open for 1% of the time, Pallas kernels for 15%

profile of v4, /device:TPU:8, one launch (start us, length us, event | category | flops | bytes accessed | tf_op | source)
XLA Modules:
  0.0 138.2 jit_solution(11376703676451782426)
XLA Ops:
  4.9 3.3 %collective-permute-start = (bf16[192,512]{1,0:T(8,128)(2,1)S(1)}, bf16[192,512]{1,0:T(8,128)(2,1)S(1)}, u32[]{:S(2)}, u32[]{:S(2)}) collective-permute-start(bf16[192,512]{1,0:T(8,128)(2,1)S(1)} %slice.55), channel_id=1, source_target_pairs={{0,64},{64,128},{128,192},{192,0},{1,65},{65,129},{129,193},{193,1... | collective-permute-start | bytes 589832 | tf_op jit(solution)/shard_map/ppermute | solution.py:30
  8.3 3.1 %collective-permute-start.1 = (bf16[192,512]{1,0:T(8,128)(2,1)S(1)}, bf16[192,512]{1,0:T(8,128)(2,1)S(1)}, u32[]{:S(2)}, u32[]{:S(2)}) collective-permute-start(bf16[192,512]{1,0:T(8,128)(2,1)S(1)} %slice.55), channel_id=1, source_target_pairs={{0,192},{64,0},{128,64},{192,128},{1,193},{65,1},{129,65},{193,129... | collective-permute-start | bytes 589832 | tf_op jit(solution)/shard_map/ppermute | solution.py:30
  11.4 4.2 %shard_map.77 = bf16[16,512,512]{2,1,0:T(8,128)(2,1)S(1)} custom-call(s32[16]{0:T(128)S(1)} %broadcast_add_fusion.1.at_ref, bf16[512,16384]{1,0:T(8,128)(2,1)} %h_ref.3), custom_call_target="tpu_custom_call" | custom-call | bytes 16777216 | tf_op jit(solution)/shard_map/pallas_call | solution.py:72
  17.2 3.8 %collective-permute-done.1 = bf16[192,512]{1,0:T(8,128)(2,1)S(1)} collective-permute-done((bf16[192,512]{1,0:T(8,128)(2,1)S(1)}, bf16[192,512]{1,0:T(8,128)(2,1)S(1)}, u32[]{:S(2)}, u32[]{:S(2)}) %collective-permute-start.1) | collective-permute-done | bytes 196640 | tf_op jit(solution)/shard_map/ppermute | solution.py:30
  21.1 3.7 %collective-permute-start.4 = (bf16[96,512]{1,0:T(8,128)(2,1)S(1)}, bf16[96,512]{1,0:T(8,128)(2,1)S(1)}, u32[]{:S(2)}, u32[]{:S(2)}) collective-permute-start(bf16[96,512]{1,0:T(8,128)(2,1)S(1)} %slice.56), channel_id=1, source_target_pairs={{0,64},{64,128},{128,192},{192,0},{1,65},{65,129},{129,193},{193,1... | collective-permute-start | bytes 294920 | tf_op jit(solution)/shard_map/ppermute | solution.py:30
  27.4 4.6 %collective-permute-done.9.refs_3_ = bf16[32,512]{1,0:T(8,128)(2,1)S(1)} collective-permute-done((bf16[32,512]{1,0:T(8,128)(2,1)S(1)}, bf16[32,512]{1,0:T(8,128)(2,1)S(1)}, u32[]{:S(2)}, u32[]{:S(2)}) %collective-permute-start.9) | collective-permute-done | bytes 32800 | tf_op jit(solution)/shard_map/ppermute | solution.py:30
  32.8 3.0 %collective-permute-start.8 = (bf16[576,512]{1,0:T(8,128)(2,1)S(1)}, bf16[576,512]{1,0:T(8,128)(2,1)S(1)}, u32[]{:S(2)}, u32[]{:S(2)}) collective-permute-start(bf16[576,512]{1,0:T(8,128)(2,1)S(1)} %constant_dynamic-update-slice_fusion.refs_5_), channel_id=1, source_target_pairs={{0,48},{16,0},{32,16},{48,32},{1,49},{17,1},{33,17},{49,33},{2,50}... | collective-permute-start | bytes 1769480 | tf_op jit(solution)/shard_map/ppermute | solution.py:30
  35.8 2.2 %collective-permute-start.11 = (bf16[256,512]{1,0:T(8,128)(2,1)S(1)}, bf16[256,512]{1,0:T(8,128)(2,1)S(1)}, u32[]{:S(2)}, u32[]{:S(2)}) collective-permute-start(bf16[256,512]{1,0:T(8,128)(2,1)S(1)} %slice_dynamic-update-slice_fusion), channel_id=1, source_target_pairs={{0,64},{64,128},{128,192},{192,0},{1,65},{65,129},{129,193},{193,1... | collective-permute-start | bytes 786440 | tf_op jit(solution)/shard_map/ppermute | solution.py:30
  38.0 2.0 %collective-permute-start.12 = (bf16[256,512]{1,0:T(8,128)(2,1)S(1)}, bf16[256,512]{1,0:T(8,128)(2,1)S(1)}, u32[]{:S(2)}, u32[]{:S(2)}) collective-permute-start(bf16[256,512]{1,0:T(8,128)(2,1)S(1)} %slice_dynamic-update-slice_fusion), channel_id=1, source_target_pairs={{0,192},{64,0},{128,64},{192,128},{1,193},{65,1},{129,65},{193,129... | collective-permute-start | bytes 786440 | tf_op jit(solution)/shard_map/ppermute | solution.py:30
  40.1 4.2 %shard_map.78.m_ref = bf16[16,512,512]{2,1,0:T(8,128)(2,1)S(1)} custom-call(s32[16]{0:T(128)S(1)} %broadcast_add_fusion.at_ref, bf16[512,16384]{1,0:T(8,128)(2,1)} %h_ref.3), custom_call_target="tpu_custom_call" | custom-call | bytes 16777216 | tf_op jit(solution)/shard_map/pallas_call | solution.py:72
  44.3 2.6 %shard_map.79.refs_4_ = f32[256,1024]{1,0:T(8,128)S(1)} custom-call(bf16[16,512,512]{2,1,0:T(8,128)(2,1)S(1)} %shard_map.78.m_ref, bf16[16,512,512]{2,1,0:T(8,128)(2,1)S(1)} %collective-permute-done.6.t_ref, bf16[256,512]{1,0:T(8,128)(2,1)S(1)} %copy-done.2, bf16[256,512]{1,0:T(8,128)(2,1)S(1)} %collective-permute-done.3.refs_1_, ...), custom_call_target="tpu_custom_call" | custom-call | bytes 19267584 | tf_op jit(solution)/shard_map/pallas_call | solution.py:45
  48.4 2.2 %collective-permute-done.12.refs_2_ = bf16[256,512]{1,0:T(8,128)(2,1)S(1)} collective-permute-done((bf16[256,512]{1,0:T(8,128)(2,1)S(1)}, bf16[256,512]{1,0:T(8,128)(2,1)S(1)}, u32[]{:S(2)}, u32[]{:S(2)}) %collective-permute-start.12) | collective-permute-done | bytes 262176 | tf_op jit(solution)/shard_map/ppermute | solution.py:30
  54.7 2.7 %collective-permute-start.16 = (bf16[128,512]{1,0:T(8,128)(2,1)S(1)}, bf16[128,512]{1,0:T(8,128)(2,1)S(1)}, u32[]{:S(2)}, u32[]{:S(2)}) collective-permute-start(bf16[128,512]{1,0:T(8,128)(2,1)S(1)} %slice.68), channel_id=1, source_target_pairs={{0,192},{64,0},{128,64},{192,128},{1,193},{65,1},{129,65},{193,129... | collective-permute-start | bytes 393224 | tf_op jit(solution)/shard_map/ppermute | solution.py:30
  57.4 5.6 %shard_map.80.refs_4_ = f32[256,1024]{1,0:T(8,128)S(1)} custom-call(bf16[16,512,512]{2,1,0:T(8,128)(2,1)S(1)} %shard_map.78.m_ref, bf16[16,512,512]{2,1,0:T(8,128)(2,1)S(1)} %collective-permute-done.6.t_ref, bf16[576,512]{1,0:T(8,128)(2,1)S(1)} %collective-permute-done.8.refs_0_, bf16[576,512]{1,0:T(8,128)(2,1)S(1)} %collective-permute-done.7.refs_1_, ...), custom_call_target="tpu_custom_call" | custom-call | bytes 20578304 | tf_op jit(solution)/shard_map/pallas_call | solution.py:45
  63.1 3.3 %shard_map.81.mine = f32[256,1024]{1,0:T(8,128)S(1)} custom-call(bf16[16,512,512]{2,1,0:T(8,128)(2,1)S(1)} %shard_map.78.m_ref, bf16[16,512,512]{2,1,0:T(8,128)(2,1)S(1)} %collective-permute-done.6.t_ref, bf16[384,512]{1,0:T(8,128)(2,1)S(1)} %collective-permute-done.13.refs_0_, bf16[384,512]{1,0:T(8,128)(2,1)S(1)} %collective-permute-done.14.refs_1_, ...), custom_call_target="tpu_custom_call" | custom-call | bytes 19922944 | tf_op jit(solution)/shard_map/pallas_call | solution.py:45
  72.6 2.4 %collective-permute-start.21 = (f32[3,1024]{1,0:T(4,128)S(1)}, f32[3,1024]{1,0:T(4,128)S(1)}, u32[]{:S(2)}, u32[]{:S(2)}) collective-permute-start(f32[3,1024]{1,0:T(4,128)S(1)} %get-tuple-element.58.a), channel_id=1, source_target_pairs={{0,3},{1,0},{2,1},{3,2},{4,7},{5,4},{6,5},{7,6},{8,11},{9,8},{10,9... | collective-permute-start | bytes 36872 | tf_op jit(solution)/shard_map/ppermute | solution.py:30
  78.6 2.1 %collective-permute-done.22.o = f32[3,1024]{1,0:T(4,128)S(1)} collective-permute-done((f32[3,1024]{1,0:T(4,128)S(1)}, f32[3,1024]{1,0:T(4,128)S(1)}, u32[]{:S(2)}, u32[]{:S(2)}) %collective-permute-start.22) | collective-permute-done | bytes 12320 | tf_op jit(solution)/shard_map/ppermute | solution.py:30
  81.1 7.5 %shard_map.85 = (bf16[576,512]{1,0:T(8,128)(2,1)S(1)}, bf16[576,512]{1,0:T(8,128)(2,1)S(1)}, bf16[256,512]{1,0:T(8,128)(2,1)S(1)}, bf16[256,512]{1,0:T(8,128)(2,...) custom-call(bf16[16,512,512]{2,1,0:T(8,128)(2,1)} %copy-done, ...), custom_call_target="tpu_custom_call" | custom-call | flops 3221225472 | bytes 12582912 | tf_op jit(solution)/shard_map/pallas_call | solution.py:113
  88.7 3.2 %collective-permute-start.24 = (bf16[576,512]{1,0:T(8,128)(2,1)S(1)}, bf16[576,512]{1,0:T(8,128)(2,1)S(1)}, u32[]{:S(2)}, u32[]{:S(2)}) collective-permute-start(bf16[576,512]{1,0:T(8,128)(2,1)S(1)} %get-tuple-element.62), channel_id=1, source_target_pairs={{0,48},{16,0},{32,16},{48,32},{1,49},{17,1},{33,17},{49,33},{2,50}... | collective-permute-start | bytes 1769480 | tf_op jit(solution)/shard_map/ppermute | solution.py:30
  92.6 3.4 %collective-permute-start.26 = (bf16[256,512]{1,0:T(8,128)(2,1)S(1)}, bf16[256,512]{1,0:T(8,128)(2,1)S(1)}, u32[]{:S(2)}, u32[]{:S(2)}) collective-permute-start(bf16[256,512]{1,0:T(8,128)(2,1)S(1)} %get-tuple-element.68), channel_id=1, source_target_pairs={{0,192},{64,0},{128,64},{192,128},{1,193},{65,1},{129,65},{193,129... | collective-permute-start | bytes 786440 | tf_op jit(solution)/shard_map/ppermute | solution.py:30
  96.0 3.1 %shard_map.86 = (f32[768,512]{1,0:T(8,128)S(1)}, f32[256,512]{1,0:T(8,128)S(1)}) custom-call(bf16[16,512,512]{2,1,0:T(8,128)(2,1)} %copy-done, bf16[16,512,512]{2,1,0:T(8,128)(2,1)} %copy-done.1, bf16[256,1024]{1,0:T(8,128)(2,1)S(1)} %get-tuple-element.60.refs_0_), custom_call_target="tpu_custom_call" | custom-call | flops 1073741824 | bytes 4194304 | tf_op jit(solution)/shard_map/pallas_call | solution.py:113
  99.1 3.5 %collective-permute-done.23.u.up = bf16[576,512]{1,0:T(8,128)(2,1)S(1)} collective-permute-done((bf16[576,512]{1,0:T(8,128)(2,1)S(1)}, bf16[576,512]{1,0:T(8,128)(2,1)S(1)}, u32[]{:S(2)}, u32[]{:S(2)}) %collective-permute-start.23) | collective-permute-done | bytes 589856 | tf_op jit(solution)/shard_map/ppermute | solution.py:30
  103.4 2.6 %collective-permute-start.30 = (bf16[288,512]{1,0:T(8,128)(2,1)S(1)}, bf16[288,512]{1,0:T(8,128)(2,1)S(1)}, u32[]{:S(2)}, u32[]{:S(2)}) collective-permute-start(bf16[288,512]{1,0:T(8,128)(2,1)S(1)} %get-tuple-element.79), channel_id=1, source_target_pairs={{0,48},{16,0},{32,16},{48,32},{1,49},{17,1},{33,17},{49,33},{2,50}... | collective-permute-start | bytes 884744 | tf_op jit(solution)/shard_map/ppermute | solution.py:30
  106.1 2.2 %collective-permute-start.27 = (bf16[128,512]{1,0:T(8,128)(2,1)S(1)}, bf16[128,512]{1,0:T(8,128)(2,1)S(1)}, u32[]{:S(2)}, u32[]{:S(2)}) collective-permute-start(bf16[128,512]{1,0:T(8,128)(2,1)S(1)} %get-tuple-element.71), channel_id=1, source_target_pairs={{0,64},{64,128},{128,192},{192,0},{1,65},{65,129},{129,193},{193,1... | collective-permute-start | bytes 393224 | tf_op jit(solution)/shard_map/ppermute | solution.py:30
  108.3 2.0 %collective-permute-start.28 = (bf16[128,512]{1,0:T(8,128)(2,1)S(1)}, bf16[128,512]{1,0:T(8,128)(2,1)S(1)}, u32[]{:S(2)}, u32[]{:S(2)}) collective-permute-start(bf16[128,512]{1,0:T(8,128)(2,1)S(1)} %get-tuple-element.72), channel_id=1, source_target_pairs={{0,192},{64,0},{128,64},{192,128},{1,193},{65,1},{129,65},{193,129... | collective-permute-start | bytes 393224 | tf_op jit(solution)/shard_map/ppermute | solution.py:30
  110.9 3.7 %collective-permute-done.27.up2 = bf16[128,512]{1,0:T(8,128)(2,1)S(1)} collective-permute-done((bf16[128,512]{1,0:T(8,128)(2,1)S(1)}, bf16[128,512]{1,0:T(8,128)(2,1)S(1)}, u32[]{:S(2)}, u32[]{:S(2)}) %collective-permute-start.27) | collective-permute-done | bytes 131104 | tf_op jit(solution)/shard_map/ppermute | solution.py:30
  115.7 3.2 %collective-permute-start.32 = (bf16[256,512]{1,0:T(8,128)(2,1)S(1)}, bf16[256,512]{1,0:T(8,128)(2,1)S(1)}, u32[]{:S(2)}, u32[]{:S(2)}) collective-permute-start(bf16[256,512]{1,0:T(8,128)(2,1)S(1)} %get-tuple-element.83), channel_id=1, source_target_pairs={{0,48},{16,0},{32,16},{48,32},{1,49},{17,1},{33,17},{49,33},{2,50}... | collective-permute-start | bytes 786440 | tf_op jit(solution)/shard_map/ppermute | solution.py:30
  119.0 2.8 %collective-permute-start.35 = (bf16[192,512]{1,0:T(8,128)(2,1)S(1)}, bf16[192,512]{1,0:T(8,128)(2,1)S(1)}, u32[]{:S(2)}, u32[]{:S(2)}) collective-permute-start(bf16[192,512]{1,0:T(8,128)(2,1)S(1)} %get-tuple-element.80._), channel_id=1, source_target_pairs={{0,64},{64,128},{128,192},{192,0},{1,65},{65,129},{129,193},{193,1... | collective-permute-start | bytes 589832 | tf_op jit(solution)/shard_map/ppermute | solution.py:30
  123.3 3.3 %collective-permute-start.37 = (bf16[192,512]{1,0:T(8,128)(2,1)S(1)}, bf16[192,512]{1,0:T(8,128)(2,1)S(1)}, u32[]{:S(2)}, u32[]{:S(2)}) collective-permute-start(bf16[192,512]{1,0:T(8,128)(2,1)S(1)} %get-tuple-element.89), channel_id=1, source_target_pairs={{0,192},{64,0},{128,64},{192,128},{1,193},{65,1},{129,65},{193,129... | collective-permute-start | bytes 589832 | tf_op jit(solution)/shard_map/ppermute | solution.py:30
  126.7 3.2 %collective-permute-start.34 = (bf16[128,512]{1,0:T(8,128)(2,1)S(1)}, bf16[128,512]{1,0:T(8,128)(2,1)S(1)}, u32[]{:S(2)}, u32[]{:S(2)}) collective-permute-start(bf16[128,512]{1,0:T(8,128)(2,1)S(1)} %get-tuple-element.87), channel_id=1, source_target_pairs={{0,48},{16,0},{32,16},{48,32},{1,49},{17,1},{33,17},{49,33},{2,50}... | collective-permute-start | bytes 393224 | tf_op jit(solution)/shard_map/ppermute | solution.py:30
  130.5 4.3 %collective-permute-done.36.z2 = bf16[192,512]{1,0:T(8,128)(2,1)S(1)} collective-permute-done((bf16[192,512]{1,0:T(8,128)(2,1)S(1)}, bf16[192,512]{1,0:T(8,128)(2,1)S(1)}, u32[]{:S(2)}, u32[]{:S(2)}) %collective-permute-start.36) | collective-permute-done | bytes 196640 | tf_op jit(solution)/shard_map/ppermute | solution.py:30
  134.8 2.4 %collective-permute-done.37.z3 = bf16[192,512]{1,0:T(8,128)(2,1)S(1)} collective-permute-done((bf16[192,512]{1,0:T(8,128)(2,1)S(1)}, bf16[192,512]{1,0:T(8,128)(2,1)S(1)}, u32[]{:S(2)}, u32[]{:S(2)}) %collective-permute-start.37) | collective-permute-done | bytes 196640 | tf_op jit(solution)/shard_map/ppermute | solution.py:30
  (106 shorter events, 31.4 us)
Async XLA Ops:
  0.6 20.4 %collective-permute-start.2 = (bf16[256,512]{1,0:T(8,128)(2,1)}, bf16[256,512]{1,0:T(8,128)(2,1)S(1)}, u32[]{:S(2)}, u32[]{:S(2)}) collective-permute-start(bf16[256,512]{1,0:T(8,128)(2,1)} %refs_0_.1), channel_id=1, source_target_pairs={{0,16},{16,32},{32,48},{48,0},{1,17},{17,33},{33,49},{49,1},{2,18}... | collective-permute-start | bytes 786440 | tf_op jit(solution)/shard_map/ppermute | solution.py:30
  2.2 18.8 %collective-permute-start.3 = (bf16[256,512]{1,0:T(8,128)(2,1)}, bf16[256,512]{1,0:T(8,128)(2,1)S(1)}, u32[]{:S(2)}, u32[]{:S(2)}) collective-permute-start(bf16[256,512]{1,0:T(8,128)(2,1)} %refs_0_.1), channel_id=1, source_target_pairs={{0,48},{16,0},{32,16},{48,32},{1,49},{17,1},{33,17},{49,33},{2,50}... | collective-permute-start | bytes 786440 | tf_op jit(solution)/shard_map/ppermute | solution.py:30
  4.9 12.3 %collective-permute-start = (bf16[192,512]{1,0:T(8,128)(2,1)S(1)}, bf16[192,512]{1,0:T(8,128)(2,1)S(1)}, u32[]{:S(2)}, u32[]{:S(2)}) collective-permute-start(bf16[192,512]{1,0:T(8,128)(2,1)S(1)} %slice.55), channel_id=1, source_target_pairs={{0,64},{64,128},{128,192},{192,0},{1,65},{65,129},{129,193},{193,1... | collective-permute-start | bytes 589832 | tf_op jit(solution)/shard_map/ppermute | solution.py:30
  8.3 12.8 %collective-permute-start.1 = (bf16[192,512]{1,0:T(8,128)(2,1)S(1)}, bf16[192,512]{1,0:T(8,128)(2,1)S(1)}, u32[]{:S(2)}, u32[]{:S(2)}) collective-permute-start(bf16[192,512]{1,0:T(8,128)(2,1)S(1)} %slice.55), channel_id=1, source_target_pairs={{0,192},{64,0},{128,64},{192,128},{1,193},{65,1},{129,65},{193,129... | collective-permute-start | bytes 589832 | tf_op jit(solution)/shard_map/ppermute | solution.py:30
  21.0 23.3 %collective-permute-start.6 = (bf16[16,512,512]{2,1,0:T(8,128)(2,1)S(1)}, bf16[16,512,512]{2,1,0:T(8,128)(2,1)S(1)}, u32[]{:S(2)}, u32[]{:S(2)}) collective-permute-start(bf16[16,512,512]{2,1,0:T(8,128)(2,1)S(1)} %shard_map.77), channel_id=1, source_target_pairs={{0,8},{8,0},{1,9},{9,1},{2,10},{10,2},{3,11},{11,3},{4,12},{12,4},... | collective-permute-start | bytes 25165832 | tf_op jit(solution)/shard_map/ppermute | solution.py:30
  21.1 11.0 %collective-permute-start.4 = (bf16[96,512]{1,0:T(8,128)(2,1)S(1)}, bf16[96,512]{1,0:T(8,128)(2,1)S(1)}, u32[]{:S(2)}, u32[]{:S(2)}) collective-permute-start(bf16[96,512]{1,0:T(8,128)(2,1)S(1)} %slice.56), channel_id=1, source_target_pairs={{0,64},{64,128},{128,192},{192,0},{1,65},{65,129},{129,193},{193,1... | collective-permute-start | bytes 294920 | tf_op jit(solution)/shard_map/ppermute | solution.py:30
  24.8 7.6 %collective-permute-start.5 = (bf16[96,512]{1,0:T(8,128)(2,1)S(1)}, bf16[96,512]{1,0:T(8,128)(2,1)S(1)}, u32[]{:S(2)}, u32[]{:S(2)}) collective-permute-start(bf16[96,512]{1,0:T(8,128)(2,1)S(1)} %slice.57), channel_id=1, source_target_pairs={{0,192},{64,0},{128,64},{192,128},{1,193},{65,1},{129,65},{193,129... | collective-permute-start | bytes 294920 | tf_op jit(solution)/shard_map/ppermute | solution.py:30
  25.4 10.4 %collective-permute-start.10 = (bf16[32,512]{1,0:T(8,128)(2,1)S(1)}, bf16[32,512]{1,0:T(8,128)(2,1)S(1)}, u32[]{:S(2)}, u32[]{:S(2)}) collective-permute-start(bf16[32,512]{1,0:T(8,128)(2,1)S(1)} %slice.61), channel_id=1, source_target_pairs={{0,48},{16,0},{32,16},{48,32},{1,49},{17,1},{33,17},{49,33},{2,50}... | collective-permute-start | bytes 98312 | tf_op jit(solution)/shard_map/ppermute | solution.py:30
  32.5 18.1 %collective-permute-start.7 = (bf16[576,512]{1,0:T(8,128)(2,1)S(1)}, bf16[576,512]{1,0:T(8,128)(2,1)S(1)}, u32[]{:S(2)}, u32[]{:S(2)}) collective-permute-start(bf16[576,512]{1,0:T(8,128)(2,1)S(1)} %constant_dynamic-update-slice_fusion.refs_5_), channel_id=1, source_target_pairs={{0,16},{16,32},{32,48},{48,0},{1,17},{17,33},{33,49},{49,1},{2,18}... | collective-permute-start | bytes 1769480 | tf_op jit(solution)/shard_map/ppermute | solution.py:30
  32.8 17.7 %collective-permute-start.8 = (bf16[576,512]{1,0:T(8,128)(2,1)S(1)}, bf16[576,512]{1,0:T(8,128)(2,1)S(1)}, u32[]{:S(2)}, u32[]{:S(2)}) collective-permute-start(bf16[576,512]{1,0:T(8,128)(2,1)S(1)} %constant_dynamic-update-slice_fusion.refs_5_), channel_id=1, source_target_pairs={{0,48},{16,0},{32,16},{48,32},{1,49},{17,1},{33,17},{49,33},{2,50}... | collective-permute-start | bytes 1769480 | tf_op jit(solution)/shard_map/ppermute | solution.py:30
  35.8 12.6 %collective-permute-start.11 = (bf16[256,512]{1,0:T(8,128)(2,1)S(1)}, bf16[256,512]{1,0:T(8,128)(2,1)S(1)}, u32[]{:S(2)}, u32[]{:S(2)}) collective-permute-start(bf16[256,512]{1,0:T(8,128)(2,1)S(1)} %slice_dynamic-update-slice_fusion), channel_id=1, source_target_pairs={{0,64},{64,128},{128,192},{192,0},{1,65},{65,129},{129,193},{193,1... | collective-permute-start | bytes 786440 | tf_op jit(solution)/shard_map/ppermute | solution.py:30
  38.0 12.6 %collective-permute-start.12 = (bf16[256,512]{1,0:T(8,128)(2,1)S(1)}, bf16[256,512]{1,0:T(8,128)(2,1)S(1)}, u32[]{:S(2)}, u32[]{:S(2)}) collective-permute-start(bf16[256,512]{1,0:T(8,128)(2,1)S(1)} %slice_dynamic-update-slice_fusion), channel_id=1, source_target_pairs={{0,192},{64,0},{128,64},{192,128},{1,193},{65,1},{129,65},{193,129... | collective-permute-start | bytes 786440 | tf_op jit(solution)/shard_map/ppermute | solution.py:30
  50.7 12.4 %collective-permute-start.14 = (bf16[384,512]{1,0:T(8,128)(2,1)S(1)}, bf16[384,512]{1,0:T(8,128)(2,1)S(1)}, u32[]{:S(2)}, u32[]{:S(2)}) collective-permute-start(bf16[384,512]{1,0:T(8,128)(2,1)S(1)} %pad_maximum_fusion.1), channel_id=1, source_target_pairs={{0,48},{16,0},{32,16},{48,32},{1,49},{17,1},{33,17},{49,33},{2,50}... | collective-permute-start | bytes 1179656 | tf_op jit(solution)/shard_map/ppermute | solution.py:30
  52.2 10.9 %collective-permute-start.13 = (bf16[384,512]{1,0:T(8,128)(2,1)S(1)}, bf16[384,512]{1,0:T(8,128)(2,1)S(1)}, u32[]{:S(2)}, u32[]{:S(2)}) collective-permute-start(bf16[384,512]{1,0:T(8,128)(2,1)S(1)} %pad_maximum_fusion), channel_id=1, source_target_pairs={{0,16},{16,32},{32,48},{48,0},{1,17},{17,33},{33,49},{49,1},{2,18}... | collective-permute-start | bytes 1179656 | tf_op jit(solution)/shard_map/ppermute | solution.py:30
  53.1 10.0 %collective-permute-start.15 = (bf16[128,512]{1,0:T(8,128)(2,1)S(1)}, bf16[128,512]{1,0:T(8,128)(2,1)S(1)}, u32[]{:S(2)}, u32[]{:S(2)}) collective-permute-start(bf16[128,512]{1,0:T(8,128)(2,1)S(1)} %slice.67), channel_id=1, source_target_pairs={{0,64},{64,128},{128,192},{192,0},{1,65},{65,129},{129,193},{193,1... | collective-permute-start | bytes 393224 | tf_op jit(solution)/shard_map/ppermute | solution.py:30
  54.7 8.4 %collective-permute-start.16 = (bf16[128,512]{1,0:T(8,128)(2,1)S(1)}, bf16[128,512]{1,0:T(8,128)(2,1)S(1)}, u32[]{:S(2)}, u32[]{:S(2)}) collective-permute-start(bf16[128,512]{1,0:T(8,128)(2,1)S(1)} %slice.68), channel_id=1, source_target_pairs={{0,192},{64,0},{128,64},{192,128},{1,193},{65,1},{129,65},{193,129... | collective-permute-start | bytes 393224 | tf_op jit(solution)/shard_map/ppermute | solution.py:30
  71.6 5.2 %collective-permute-start.20 = (f32[3,1024]{1,0:T(4,128)S(1)}, f32[3,1024]{1,0:T(4,128)S(1)}, u32[]{:S(2)}, u32[]{:S(2)}) collective-permute-start(f32[3,1024]{1,0:T(4,128)S(1)} %get-tuple-element.58.a), channel_id=1, source_target_pairs={{0,2},{1,3},{2,0},{3,1},{4,6},{5,7},{6,4},{7,5},{8,10},{9,11},{10,... | collective-permute-start | bytes 36872 | tf_op jit(solution)/shard_map/ppermute | solution.py:30
  88.6 14.1 %collective-permute-start.23 = (bf16[576,512]{1,0:T(8,128)(2,1)S(1)}, bf16[576,512]{1,0:T(8,128)(2,1)S(1)}, u32[]{:S(2)}, u32[]{:S(2)}) collective-permute-start(bf16[576,512]{1,0:T(8,128)(2,1)S(1)} %get-tuple-element.61), channel_id=1, source_target_pairs={{0,16},{16,32},{32,48},{48,0},{1,17},{17,33},{33,49},{49,1},{2,18}... | collective-permute-start | bytes 1769480 | tf_op jit(solution)/shard_map/ppermute | solution.py:30
  88.7 14.0 %collective-permute-start.24 = (bf16[576,512]{1,0:T(8,128)(2,1)S(1)}, bf16[576,512]{1,0:T(8,128)(2,1)S(1)}, u32[]{:S(2)}, u32[]{:S(2)}) collective-permute-start(bf16[576,512]{1,0:T(8,128)(2,1)S(1)} %get-tuple-element.62), channel_id=1, source_target_pairs={{0,48},{16,0},{32,16},{48,32},{1,49},{17,1},{33,17},{49,33},{2,50}... | collective-permute-start | bytes 1769480 | tf_op jit(solution)/shard_map/ppermute | solution.py:30
  91.9 14.2 %collective-permute-start.25 = (bf16[256,512]{1,0:T(8,128)(2,1)S(1)}, bf16[256,512]{1,0:T(8,128)(2,1)S(1)}, u32[]{:S(2)}, u32[]{:S(2)}) collective-permute-start(bf16[256,512]{1,0:T(8,128)(2,1)S(1)} %get-tuple-element.67), channel_id=1, source_target_pairs={{0,64},{64,128},{128,192},{192,0},{1,65},{65,129},{129,193},{193,1... | collective-permute-start | bytes 786440 | tf_op jit(solution)/shard_map/ppermute | solution.py:30
  92.6 13.5 %collective-permute-start.26 = (bf16[256,512]{1,0:T(8,128)(2,1)S(1)}, bf16[256,512]{1,0:T(8,128)(2,1)S(1)}, u32[]{:S(2)}, u32[]{:S(2)}) collective-permute-start(bf16[256,512]{1,0:T(8,128)(2,1)S(1)} %get-tuple-element.68), channel_id=1, source_target_pairs={{0,192},{64,0},{128,64},{192,128},{1,193},{65,1},{129,65},{193,129... | collective-permute-start | bytes 786440 | tf_op jit(solution)/shard_map/ppermute | solution.py:30
  102.7 8.0 %collective-permute-start.29 = (bf16[288,512]{1,0:T(8,128)(2,1)S(1)}, bf16[288,512]{1,0:T(8,128)(2,1)S(1)}, u32[]{:S(2)}, u32[]{:S(2)}) collective-permute-start(bf16[288,512]{1,0:T(8,128)(2,1)S(1)} %get-tuple-element.78), channel_id=1, source_target_pairs={{0,16},{16,32},{32,48},{48,0},{1,17},{17,33},{33,49},{49,1},{2,18}... | collective-permute-start | bytes 884744 | tf_op jit(solution)/shard_map/ppermute | solution.py:30
  103.4 7.3 %collective-permute-start.30 = (bf16[288,512]{1,0:T(8,128)(2,1)S(1)}, bf16[288,512]{1,0:T(8,128)(2,1)S(1)}, u32[]{:S(2)}, u32[]{:S(2)}) collective-permute-start(bf16[288,512]{1,0:T(8,128)(2,1)S(1)} %get-tuple-element.79), channel_id=1, source_target_pairs={{0,48},{16,0},{32,16},{48,32},{1,49},{17,1},{33,17},{49,33},{2,50}... | collective-permute-start | bytes 884744 | tf_op jit(solution)/shard_map/ppermute | solution.py:30
  106.1 8.6 %collective-permute-start.27 = (bf16[128,512]{1,0:T(8,128)(2,1)S(1)}, bf16[128,512]{1,0:T(8,128)(2,1)S(1)}, u32[]{:S(2)}, u32[]{:S(2)}) collective-permute-start(bf16[128,512]{1,0:T(8,128)(2,1)S(1)} %get-tuple-element.71), channel_id=1, source_target_pairs={{0,64},{64,128},{128,192},{192,0},{1,65},{65,129},{129,193},{193,1... | collective-permute-start | bytes 393224 | tf_op jit(solution)/shard_map/ppermute | solution.py:30
  108.3 7.2 %collective-permute-start.28 = (bf16[128,512]{1,0:T(8,128)(2,1)S(1)}, bf16[128,512]{1,0:T(8,128)(2,1)S(1)}, u32[]{:S(2)}, u32[]{:S(2)}) collective-permute-start(bf16[128,512]{1,0:T(8,128)(2,1)S(1)} %get-tuple-element.72), channel_id=1, source_target_pairs={{0,192},{64,0},{128,64},{192,128},{1,193},{65,1},{129,65},{193,129... | collective-permute-start | bytes 393224 | tf_op jit(solution)/shard_map/ppermute | solution.py:30
  115.7 10.9 %collective-permute-start.31 = (bf16[256,512]{1,0:T(8,128)(2,1)S(1)}, bf16[256,512]{1,0:T(8,128)(2,1)S(1)}, u32[]{:S(2)}, u32[]{:S(2)}) collective-permute-start(bf16[256,512]{1,0:T(8,128)(2,1)S(1)} %get-tuple-element.82), channel_id=1, source_target_pairs={{0,16},{16,32},{32,48},{48,0},{1,17},{17,33},{33,49},{49,1},{2,18}... | collective-permute-start | bytes 786440 | tf_op jit(solution)/shard_map/ppermute | solution.py:30
  115.7 10.8 %collective-permute-start.32 = (bf16[256,512]{1,0:T(8,128)(2,1)S(1)}, bf16[256,512]{1,0:T(8,128)(2,1)S(1)}, u32[]{:S(2)}, u32[]{:S(2)}) collective-permute-start(bf16[256,512]{1,0:T(8,128)(2,1)S(1)} %get-tuple-element.83), channel_id=1, source_target_pairs={{0,48},{16,0},{32,16},{48,32},{1,49},{17,1},{33,17},{49,33},{2,50}... | collective-permute-start | bytes 786440 | tf_op jit(solution)/shard_map/ppermute | solution.py:30
  119.0 11.5 %collective-permute-start.35 = (bf16[192,512]{1,0:T(8,128)(2,1)S(1)}, bf16[192,512]{1,0:T(8,128)(2,1)S(1)}, u32[]{:S(2)}, u32[]{:S(2)}) collective-permute-start(bf16[192,512]{1,0:T(8,128)(2,1)S(1)} %get-tuple-element.80._), channel_id=1, source_target_pairs={{0,64},{64,128},{128,192},{192,0},{1,65},{65,129},{129,193},{193,1... | collective-permute-start | bytes 589832 | tf_op jit(solution)/shard_map/ppermute | solution.py:30
  121.8 13.0 %collective-permute-start.36 = (bf16[192,512]{1,0:T(8,128)(2,1)S(1)}, bf16[192,512]{1,0:T(8,128)(2,1)S(1)}, u32[]{:S(2)}, u32[]{:S(2)}) collective-permute-start(bf16[192,512]{1,0:T(8,128)(2,1)S(1)} %get-tuple-element.88), channel_id=1, source_target_pairs={{0,128},{64,192},{128,0},{192,64},{1,129},{65,193},{129,1},{193,65... | collective-permute-start | bytes 589832 | tf_op jit(solution)/shard_map/ppermute | solution.py:30
  123.3 13.9 %collective-permute-start.37 = (bf16[192,512]{1,0:T(8,128)(2,1)S(1)}, bf16[192,512]{1,0:T(8,128)(2,1)S(1)}, u32[]{:S(2)}, u32[]{:S(2)}) collective-permute-start(bf16[192,512]{1,0:T(8,128)(2,1)S(1)} %get-tuple-element.89), channel_id=1, source_target_pairs={{0,192},{64,0},{128,64},{192,128},{1,193},{65,1},{129,65},{193,129... | collective-permute-start | bytes 589832 | tf_op jit(solution)/shard_map/ppermute | solution.py:30
  126.6 10.6 %collective-permute-start.33 = (bf16[128,512]{1,0:T(8,128)(2,1)S(1)}, bf16[128,512]{1,0:T(8,128)(2,1)S(1)}, u32[]{:S(2)}, u32[]{:S(2)}) collective-permute-start(bf16[128,512]{1,0:T(8,128)(2,1)S(1)} %get-tuple-element.86), channel_id=1, source_target_pairs={{0,16},{16,32},{32,48},{48,0},{1,17},{17,33},{33,49},{49,1},{2,18}... | collective-permute-start | bytes 393224 | tf_op jit(solution)/shard_map/ppermute | solution.py:30
  126.7 10.5 %collective-permute-start.34 = (bf16[128,512]{1,0:T(8,128)(2,1)S(1)}, bf16[128,512]{1,0:T(8,128)(2,1)S(1)}, u32[]{:S(2)}, u32[]{:S(2)}) collective-permute-start(bf16[128,512]{1,0:T(8,128)(2,1)S(1)} %get-tuple-element.87), channel_id=1, source_target_pairs={{0,48},{16,0},{32,16},{48,32},{1,49},{17,1},{33,17},{49,33},{2,50}... | collective-permute-start | bytes 393224 | tf_op jit(solution)/shard_map/ppermute | solution.py:30
  (13 other events, 85.7 us)

commit v5 on v4

--- a/solution.py
+++ b/solution.py
@@ -50,6 +50,17 @@
         compiler_params=params(16),
         cost_estimate=pl.CostEstimate(flops=0, bytes_accessed=size, transcendentals=0),
     )(*args)
+
+
+def joined(*parts, after=()):
+    def body(*refs):
+        to = 0
+        for ref, (_, start, rows) in zip(refs, parts):
+            refs[-1][to : to + rows, :] = ref[start : start + rows, :]
+            to += rows
+
+    out = jax.ShapeDtypeStruct((sum(rows for _, _, rows in parts), WIDE), BF16)
+    return local_call(body, [out], *(array for array, _, _ in parts), *after)[0]
 
 
 def pick(hidden, at, mib):
@@ -205,15 +216,22 @@
 
 
 def gathered_logits(head, hidden, at, sibling_at):
-    zb, za = move(head[:PR], "zh", 1), move(head[:PR], "zh", -1)
-    xb, xa = move(head, "x", 1), move(head, "x", -1)
+    def split(h, over_zh, over_x):
+        over_zh[...] = h[:PR, :]
+        over_x[...] = h[PH:, :]
+
+    over_zh, over_x = local_call(
+        split, [jax.ShapeDtypeStruct((r, WIDE), BF16) for r in (PR, ROWS - PH)], head
+    )
+    zb, za = move(over_zh, "zh", 1), move(over_zh, "zh", -1)
+    xb, xa = move(over_x, "x", 1), move(over_x, "x", -1)
     picked = pick(hidden, sibling_at, 44)
     zb, za, xb, xa, picked = lax.optimization_barrier((zb, za, xb, xa, picked))
     theirs = move(picked, "c", 1)
     zf1, zf2 = move(zb[:PH], "zh", 1), move(za[PH:], "zh", -1)
-    xf1, xf2 = move(xb[PR : PR + QH], "x", 1), move(xa[PR + QH :], "x", -1)
-    p = jnp.concatenate([za, zf1, zf2, zb], axis=0)
-    q = jnp.concatenate([head[PR:], xa[PR:], xf1, xf2, xb[PR:]], axis=0)
+    xf1, xf2 = move(xb[PH : PH + QH], "x", 1), move(xa[PH + QH :], "x", -1)
+    q = joined((over_x, PH, QR), (xa, PH, QR), (xf1, 0, QH), (xf2, 0, QH), (xb, PH, QR))
+    p = joined((za, 0, PR), (zf1, 0, PH), (zf2, 0, PH), (zb, 0, PR), (over_zh, 0, PH), after=[q])
     pb, pa = move(p, "x", 1), move(p, "x", -1)
     qb, qa = move(q, "zh", 1), move(q, "zh", -1)
     zf1, zf2, at = lax.optimization_barrier((zf1, zf2, at))
@@ -224,8 +242,8 @@
         head_ref, xa_ref, xb_ref, xf1_ref, xf2_ref, p_ref = refs
         out[...] = jnp.zeros_like(out)
         add(out, head_ref[...], 0)
-        add(out, xa_ref[...], 1)
-        add(out, xb_ref[...], 3)
+        add(out.at[PH:], xa_ref[...], 1)
+        add(out.at[PH:], xb_ref[...], 3)
         add(out.at[PR : PR + QH], xf1_ref[...], 2)
         add(out.at[PR + QH :], xf2_ref[...], 2)
         for dz in (1, 2, 3):
@@ -233,14 +251,17 @@
 
     total = logits_call(first, blocks, [head, xa, xb, xf1, xf2, p])
     pb, pa, qb, qa, total = lax.optimization_barrier((pb, pa, qb, qa, total))
-    pf1 = jnp.concatenate([pb[: 3 * PH], xb[:PH]], axis=0)
-    pf2 = jnp.concatenate([pa[3 * PH :], xa[PH:PR]], axis=0)
+    pf1 = joined((pb, 0, 3 * PH), (pb, 3 * PR, PH))
+    pf2 = joined((pa, 3 * PH, 3 * PH), (xa, 0, PH))
     pf1, pf2 = move(pf1, "x", 1), move(pf2, "x", -1)
     qf1, qf2 = move(qb[: 2 * QR], "zh", 1), move(qa[2 * QR :], "zh", -1)
 
     def second(add, refs, out):
         pa_ref, pb_ref, qa_ref, qb_ref, total_ref = refs
         out[...] = total_ref[...]
+
+        add(out.at[:PH], pa_ref[3 * PR :, :], 1)
+        add(out.at[:PH], pb_ref[3 * PR :, :], 3)
 
         @pl.loop(0, 3)
         def _(k):

time: 139 us -> 140 us (level)
  starting transfers between devices: 66.8 us -> 69 us
    ppermute x38, starting transfers between devices: 66.8 us -> 69 us  [move(): return lax.ppermute(value, axis, [(i, (i + by) % n) for i in range(n)])]
    pallas_call x12 -> x17, Pallas kernels: 14 us -> 15 us  [local_call(): pl.pallas_call(body, out_shape=outs, in_specs=[whole(a.shape) for a in ar...]
where the time goes in v5:
time: 140 us
  starting transfers between devices  69 us (49%)
  waiting for transfers between devices  34.3 us (24%)
  Pallas kernels  34 us (24%)
  local copies, waits for them, and re-layouts  1.6 us (1%)
    ppermute x38, starting transfers between devices, move(): return lax.ppermute(value, axis, [(i, (i + by) % n) for i in range(n)])  69 us
    ppermute x38, waiting for transfers between devices, move(): return lax.ppermute(value, axis, [(i, (i + by) % n) for i in range(n)])  34.3 us
    pallas_call x17, Pallas kernels, local_call(): pl.pallas_call(body, out_shape=outs, in_specs=[whole(a.shape) for a in ar...  15 us
    pallas_call x2, Pallas kernels, block_call(): pl.pallas_call(body, out_shape=outs, in_specs=[pl.BlockSpec(memory_space=...  10.6 us
    pallas_call x2, Pallas kernels, pick(): pl.pallas_call(body, out_shape=jax.ShapeDtypeStruct((n, TOK, WIDE), BF16)...  8.43 us
  transfers between devices with their start and end apart: 38, of which 15 were waited for; matrix products, arithmetic and copies ran while one was open for 1% of the time, Pallas kernels for 15%

profile of v5, /device:TPU:8, one launch (start us, length us, event | category | flops | bytes accessed | tf_op | source)
XLA Modules:
  0.0 140.2 jit_solution(7433272906773631597)
XLA Ops:
  1.6 3.3 %collective-permute-start = (bf16[192,512]{1,0:T(8,128)(2,1)S(1)}, bf16[192,512]{1,0:T(8,128)(2,1)S(1)}, u32[]{:S(2)}, u32[]{:S(2)}) collective-permute-start(bf16[192,512]{1,0:T(8,128)(2,1)S(1)} %get-tuple-element.48.refs_4_), channel_id=1, source_target_pairs={{0,64},{64,128},{128,192},{192,0},{1,65},{65,129},{129,193},{193,1... | collective-permute-start | bytes 589832 | tf_op jit(solution)/shard_map/ppermute | solution.py:30
  5.0 3.1 %collective-permute-start.1 = (bf16[192,512]{1,0:T(8,128)(2,1)S(1)}, bf16[192,512]{1,0:T(8,128)(2,1)S(1)}, u32[]{:S(2)}, u32[]{:S(2)}) collective-permute-start(bf16[192,512]{1,0:T(8,128)(2,1)S(1)} %get-tuple-element.48.refs_4_), channel_id=1, source_target_pairs={{0,192},{64,0},{128,64},{192,128},{1,193},{65,1},{129,65},{193,129... | collective-permute-start | bytes 589832 | tf_op jit(solution)/shard_map/ppermute | solution.py:30
  11.3 4.2 %shard_map.78 = bf16[16,512,512]{2,1,0:T(8,128)(2,1)S(1)} custom-call(s32[16]{0:T(128)S(1)} %broadcast_add_fusion.1.at_ref, bf16[512,16384]{1,0:T(8,128)(2,1)} %h_ref.3), custom_call_target="tpu_custom_call" | custom-call | bytes 16777216 | tf_op jit(solution)/shard_map/pallas_call | solution.py:83
  15.6 2.7 %collective-permute-done.1.refs_0_ = bf16[192,512]{1,0:T(8,128)(2,1)S(1)} collective-permute-done((bf16[192,512]{1,0:T(8,128)(2,1)S(1)}, bf16[192,512]{1,0:T(8,128)(2,1)S(1)}, u32[]{:S(2)}, u32[]{:S(2)}) %collective-permute-start.1) | collective-permute-done | bytes 196640 | tf_op jit(solution)/shard_map/ppermute | solution.py:30
  18.3 3.7 %collective-permute-start.4 = (bf16[96,512]{1,0:T(8,128)(2,1)S(1)}, bf16[96,512]{1,0:T(8,128)(2,1)S(1)}, u32[]{:S(2)}, u32[]{:S(2)}) collective-permute-start(bf16[96,512]{1,0:T(8,128)(2,1)S(1)} %slice.30), channel_id=1, source_target_pairs={{0,64},{64,128},{128,192},{192,0},{1,65},{65,129},{129,193},{193,1... | collective-permute-start | bytes 294920 | tf_op jit(solution)/shard_map/ppermute | solution.py:30
  25.8 1.9 %collective-permute-done.7.refs_2_.refs_3_ = bf16[32,512]{1,0:T(8,128)(2,1)S(1)} collective-permute-done((bf16[32,512]{1,0:T(8,128)(2,1)S(1)}, bf16[32,512]{1,0:T(8,128)(2,1)S(1)}, u32[]{:S(2)}, u32[]{:S(2)}) %collective-permute-start.7) | collective-permute-done | bytes 32800 | tf_op jit(solution)/shard_map/ppermute | solution.py:30
  33.9 3.3 %collective-permute-start.12 = (bf16[256,512]{1,0:T(8,128)(2,1)S(1)}, bf16[256,512]{1,0:T(8,128)(2,1)S(1)}, u32[]{:S(2)}, u32[]{:S(2)}) collective-permute-start(bf16[256,512]{1,0:T(8,128)(2,1)S(1)} %shard_map.80.refs_5_), channel_id=1, source_target_pairs={{0,192},{64,0},{128,64},{192,128},{1,193},{65,1},{129,65},{193,129... | collective-permute-start | bytes 786440 | tf_op jit(solution)/shard_map/ppermute | solution.py:30
  37.2 4.2 %shard_map.79.m_ref = bf16[16,512,512]{2,1,0:T(8,128)(2,1)S(1)} custom-call(s32[16]{0:T(128)S(1)} %broadcast_add_fusion.at_ref, bf16[512,16384]{1,0:T(8,128)(2,1)} %h_ref.3), custom_call_target="tpu_custom_call" | custom-call | bytes 16777216 | tf_op jit(solution)/shard_map/pallas_call | solution.py:83
  41.5 2.7 %shard_map.82.refs_4_ = f32[256,1024]{1,0:T(8,128)S(1)} custom-call(bf16[16,512,512]{2,1,0:T(8,128)(2,1)S(1)} %shard_map.79.m_ref, bf16[16,512,512]{2,1,0:T(8,128)(2,1)S(1)} %collective-permute-done.6.t_ref, bf16[256,512]{1,0:T(8,128)(2,1)S(1)} %copy-done.3, bf16[160,512]{1,0:T(8,128)(2,1)S(1)} %collective-permute-done.3.refs_1_, ...), custom_call_target="tpu_custom_call" | custom-call | bytes 19169280 | tf_op jit(solution)/shard_map/pallas_call | solution.py:45
  48.2 1.7 %collective-permute-start.13 = (bf16[384,512]{1,0:T(8,128)(2,1)S(1)}, bf16[384,512]{1,0:T(8,128)(2,1)S(1)}, u32[]{:S(2)}, u32[]{:S(2)}) collective-permute-start(bf16[384,512]{1,0:T(8,128)(2,1)S(1)} %shard_map.83), channel_id=1, source_target_pairs={{0,16},{16,32},{32,48},{48,0},{1,17},{17,33},{33,49},{49,1},{2,18}... | collective-permute-start | bytes 1179656 | tf_op jit(solution)/shard_map/ppermute | solution.py:30
  50.0 1.8 %collective-permute-start.14 = (bf16[384,512]{1,0:T(8,128)(2,1)S(1)}, bf16[384,512]{1,0:T(8,128)(2,1)S(1)}, u32[]{:S(2)}, u32[]{:S(2)}) collective-permute-start(bf16[384,512]{1,0:T(8,128)(2,1)S(1)} %shard_map.84), channel_id=1, source_target_pairs={{0,48},{16,0},{32,16},{48,32},{1,49},{17,1},{33,17},{49,33},{2,50}... | collective-permute-start | bytes 1179656 | tf_op jit(solution)/shard_map/ppermute | solution.py:30
  52.7 3.4 %collective-permute-start.16 = (bf16[128,512]{1,0:T(8,128)(2,1)S(1)}, bf16[128,512]{1,0:T(8,128)(2,1)S(1)}, u32[]{:S(2)}, u32[]{:S(2)}) collective-permute-start(bf16[128,512]{1,0:T(8,128)(2,1)S(1)} %slice.35), channel_id=1, source_target_pairs={{0,192},{64,0},{128,64},{192,128},{1,193},{65,1},{129,65},{193,129... | collective-permute-start | bytes 393224 | tf_op jit(solution)/shard_map/ppermute | solution.py:30
  56.2 6.3 %shard_map.85.refs_4_ = f32[256,1024]{1,0:T(8,128)S(1)} custom-call(bf16[16,512,512]{2,1,0:T(8,128)(2,1)S(1)} %shard_map.79.m_ref, bf16[16,512,512]{2,1,0:T(8,128)(2,1)S(1)} %collective-permute-done.6.t_ref, bf16[672,512]{1,0:T(8,128)(2,1)S(1)} %collective-permute-done.10.refs_0_, bf16[672,512]{1,0:T(8,128)(2,1)S(1)} %collective-permute-done.9.refs_0_.refs_1_, ...), custom_call_target="tpu_custom_call" | custom-call | bytes 20774912 | tf_op jit(solution)/shard_map/pallas_call | solution.py:45
  62.6 3.3 %shard_map.86.mine = f32[256,1024]{1,0:T(8,128)S(1)} custom-call(bf16[16,512,512]{2,1,0:T(8,128)(2,1)S(1)} %shard_map.79.m_ref, bf16[16,512,512]{2,1,0:T(8,128)(2,1)S(1)} %collective-permute-done.6.t_ref, bf16[384,512]{1,0:T(8,128)(2,1)S(1)} %collective-permute-done.13.refs_0_, bf16[384,512]{1,0:T(8,128)(2,1)S(1)} %collective-permute-done.14.refs_1_, ...), custom_call_target="tpu_custom_call" | custom-call | bytes 19922944 | tf_op jit(solution)/shard_map/pallas_call | solution.py:45
  66.7 1.9 %collective-permute-done.18 = f32[3,512]{1,0:T(4,128)S(1)} collective-permute-done((f32[3,512]{1,0:T(4,128)S(1)}, f32[3,512]{1,0:T(4,128)S(1)}, u32[]{:S(2)}, u32[]{:S(2)}) %collective-permute-start.18) | collective-permute-done | bytes 6176 | tf_op jit(solution)/shard_map/ppermute | solution.py:30
  72.0 2.4 %collective-permute-start.21 = (f32[3,1024]{1,0:T(4,128)S(1)}, f32[3,1024]{1,0:T(4,128)S(1)}, u32[]{:S(2)}, u32[]{:S(2)}) collective-permute-start(f32[3,1024]{1,0:T(4,128)S(1)} %get-tuple-element.62.a), channel_id=1, source_target_pairs={{0,3},{1,0},{2,1},{3,2},{4,7},{5,4},{6,5},{7,6},{8,11},{9,8},{10,9... | collective-permute-start | bytes 36872 | tf_op jit(solution)/shard_map/ppermute | solution.py:30
  74.4 1.9 %collective-permute-done.20.c = f32[3,1024]{1,0:T(4,128)S(1)} collective-permute-done((f32[3,1024]{1,0:T(4,128)S(1)}, f32[3,1024]{1,0:T(4,128)S(1)}, u32[]{:S(2)}, u32[]{:S(2)}) %collective-permute-start.20) | collective-permute-done | bytes 12320 | tf_op jit(solution)/shard_map/ppermute | solution.py:30
  77.7 2.5 %collective-permute-done.22.o = f32[3,1024]{1,0:T(4,128)S(1)} collective-permute-done((f32[3,1024]{1,0:T(4,128)S(1)}, f32[3,1024]{1,0:T(4,128)S(1)}, u32[]{:S(2)}, u32[]{:S(2)}) %collective-permute-start.22) | collective-permute-done | bytes 12320 | tf_op jit(solution)/shard_map/ppermute | solution.py:30
  80.5 7.5 %shard_map.90 = (bf16[576,512]{1,0:T(8,128)(2,1)S(1)}, bf16[576,512]{1,0:T(8,128)(2,1)S(1)}, bf16[256,512]{1,0:T(8,128)(2,1)S(1)}, bf16[256,512]{1,0:T(8,128)(2,...) custom-call(bf16[16,512,512]{2,1,0:T(8,128)(2,1)} %copy-done, ...), custom_call_target="tpu_custom_call" | custom-call | flops 3221225472 | bytes 12582912 | tf_op jit(solution)/shard_map/pallas_call | solution.py:124
  88.4 3.0 %collective-permute-start.24 = (bf16[576,512]{1,0:T(8,128)(2,1)S(1)}, bf16[576,512]{1,0:T(8,128)(2,1)S(1)}, u32[]{:S(2)}, u32[]{:S(2)}) collective-permute-start(bf16[576,512]{1,0:T(8,128)(2,1)S(1)} %get-tuple-element.66), channel_id=1, source_target_pairs={{0,48},{16,0},{32,16},{48,32},{1,49},{17,1},{33,17},{49,33},{2,50}... | collective-permute-start | bytes 1769480 | tf_op jit(solution)/shard_map/ppermute | solution.py:30
  91.3 4.1 %collective-permute-start.26 = (bf16[256,512]{1,0:T(8,128)(2,1)S(1)}, bf16[256,512]{1,0:T(8,128)(2,1)S(1)}, u32[]{:S(2)}, u32[]{:S(2)}) collective-permute-start(bf16[256,512]{1,0:T(8,128)(2,1)S(1)} %get-tuple-element.72), channel_id=1, source_target_pairs={{0,192},{64,0},{128,64},{192,128},{1,193},{65,1},{129,65},{193,129... | collective-permute-start | bytes 786440 | tf_op jit(solution)/shard_map/ppermute | solution.py:30
  95.5 3.1 %shard_map.91 = (f32[768,512]{1,0:T(8,128)S(1)}, f32[256,512]{1,0:T(8,128)S(1)}) custom-call(bf16[16,512,512]{2,1,0:T(8,128)(2,1)} %copy-done, bf16[16,512,512]{2,1,0:T(8,128)(2,1)} %copy-done.1, bf16[256,1024]{1,0:T(8,128)(2,1)S(1)} %get-tuple-element.64.refs_0_), custom_call_target="tpu_custom_call" | custom-call | flops 1073741824 | bytes 4194304 | tf_op jit(solution)/shard_map/pallas_call | solution.py:124
  98.6 3.5 %collective-permute-done.23.u.up = bf16[576,512]{1,0:T(8,128)(2,1)S(1)} collective-permute-done((bf16[576,512]{1,0:T(8,128)(2,1)S(1)}, bf16[576,512]{1,0:T(8,128)(2,1)S(1)}, u32[]{:S(2)}, u32[]{:S(2)}) %collective-permute-start.23) | collective-permute-done | bytes 589856 | tf_op jit(solution)/shard_map/ppermute | solution.py:30
  102.3 3.2 %collective-permute-start.30 = (bf16[288,512]{1,0:T(8,128)(2,1)S(1)}, bf16[288,512]{1,0:T(8,128)(2,1)S(1)}, u32[]{:S(2)}, u32[]{:S(2)}) collective-permute-start(bf16[288,512]{1,0:T(8,128)(2,1)S(1)} %get-tuple-element.83), channel_id=1, source_target_pairs={{0,48},{16,0},{32,16},{48,32},{1,49},{17,1},{33,17},{49,33},{2,50}... | collective-permute-start | bytes 884744 | tf_op jit(solution)/shard_map/ppermute | solution.py:30
  106.3 3.5 %collective-permute-start.28 = (bf16[128,512]{1,0:T(8,128)(2,1)S(1)}, bf16[128,512]{1,0:T(8,128)(2,1)S(1)}, u32[]{:S(2)}, u32[]{:S(2)}) collective-permute-start(bf16[128,512]{1,0:T(8,128)(2,1)S(1)} %get-tuple-element.76), channel_id=1, source_target_pairs={{0,192},{64,0},{128,64},{192,128},{1,193},{65,1},{129,65},{193,129... | collective-permute-start | bytes 393224 | tf_op jit(solution)/shard_map/ppermute | solution.py:30
  110.4 3.6 %collective-permute-done.27.up2 = bf16[128,512]{1,0:T(8,128)(2,1)S(1)} collective-permute-done((bf16[128,512]{1,0:T(8,128)(2,1)S(1)}, bf16[128,512]{1,0:T(8,128)(2,1)S(1)}, u32[]{:S(2)}, u32[]{:S(2)}) %collective-permute-start.27) | collective-permute-done | bytes 131104 | tf_op jit(solution)/shard_map/ppermute | solution.py:30
  114.2 3.2 %collective-permute-start.32 = (bf16[256,512]{1,0:T(8,128)(2,1)S(1)}, bf16[256,512]{1,0:T(8,128)(2,1)S(1)}, u32[]{:S(2)}, u32[]{:S(2)}) collective-permute-start(bf16[256,512]{1,0:T(8,128)(2,1)S(1)} %get-tuple-element.87), channel_id=1, source_target_pairs={{0,48},{16,0},{32,16},{48,32},{1,49},{17,1},{33,17},{49,33},{2,50}... | collective-permute-start | bytes 786440 | tf_op jit(solution)/shard_map/ppermute | solution.py:30
  117.4 2.4 %collective-permute-start.35 = (bf16[192,512]{1,0:T(8,128)(2,1)S(1)}, bf16[192,512]{1,0:T(8,128)(2,1)S(1)}, u32[]{:S(2)}, u32[]{:S(2)}) collective-permute-start(bf16[192,512]{1,0:T(8,128)(2,1)S(1)} %get-tuple-element.84._), channel_id=1, source_target_pairs={{0,64},{64,128},{128,192},{192,0},{1,65},{65,129},{129,193},{193,1... | collective-permute-start | bytes 589832 | tf_op jit(solution)/shard_map/ppermute | solution.py:30
  119.8 4.6 %collective-permute-start.36 = (bf16[192,512]{1,0:T(8,128)(2,1)S(1)}, bf16[192,512]{1,0:T(8,128)(2,1)S(1)}, u32[]{:S(2)}, u32[]{:S(2)}) collective-permute-start(bf16[192,512]{1,0:T(8,128)(2,1)S(1)} %get-tuple-element.92), channel_id=1, source_target_pairs={{0,128},{64,192},{128,0},{192,64},{1,129},{65,193},{129,1},{193,65... | collective-permute-start | bytes 589832 | tf_op jit(solution)/shard_map/ppermute | solution.py:30
  125.5 3.2 %collective-permute-start.34 = (bf16[128,512]{1,0:T(8,128)(2,1)S(1)}, bf16[128,512]{1,0:T(8,128)(2,1)S(1)}, u32[]{:S(2)}, u32[]{:S(2)}) collective-permute-start(bf16[128,512]{1,0:T(8,128)(2,1)S(1)} %get-tuple-element.91), channel_id=1, source_target_pairs={{0,48},{16,0},{32,16},{48,32},{1,49},{17,1},{33,17},{49,33},{2,50}... | collective-permute-start | bytes 393224 | tf_op jit(solution)/shard_map/ppermute | solution.py:30
  129.3 5.1 %collective-permute-done.36.z2 = bf16[192,512]{1,0:T(8,128)(2,1)S(1)} collective-permute-done((bf16[192,512]{1,0:T(8,128)(2,1)S(1)}, bf16[192,512]{1,0:T(8,128)(2,1)S(1)}, u32[]{:S(2)}, u32[]{:S(2)}) %collective-permute-start.36) | collective-permute-done | bytes 196640 | tf_op jit(solution)/shard_map/ppermute | solution.py:30
  134.5 4.8 %collective-permute-done.37.z3 = bf16[192,512]{1,0:T(8,128)(2,1)S(1)} collective-permute-done((bf16[192,512]{1,0:T(8,128)(2,1)S(1)}, bf16[192,512]{1,0:T(8,128)(2,1)S(1)}, u32[]{:S(2)}, u32[]{:S(2)}) %collective-permute-start.37) | collective-permute-done | bytes 196640 | tf_op jit(solution)/shard_map/ppermute | solution.py:30
  (97 shorter events, 29.9 us)
Async XLA Ops:
  1.6 14.0 %collective-permute-start = (bf16[192,512]{1,0:T(8,128)(2,1)S(1)}, bf16[192,512]{1,0:T(8,128)(2,1)S(1)}, u32[]{:S(2)}, u32[]{:S(2)}) collective-permute-start(bf16[192,512]{1,0:T(8,128)(2,1)S(1)} %get-tuple-element.48.refs_4_), channel_id=1, source_target_pairs={{0,64},{64,128},{128,192},{192,0},{1,65},{65,129},{129,193},{193,1... | collective-permute-start | bytes 589832 | tf_op jit(solution)/shard_map/ppermute | solution.py:30
  5.0 13.3 %collective-permute-start.1 = (bf16[192,512]{1,0:T(8,128)(2,1)S(1)}, bf16[192,512]{1,0:T(8,128)(2,1)S(1)}, u32[]{:S(2)}, u32[]{:S(2)}) collective-permute-start(bf16[192,512]{1,0:T(8,128)(2,1)S(1)} %get-tuple-element.48.refs_4_), channel_id=1, source_target_pairs={{0,192},{64,0},{128,64},{192,128},{1,193},{65,1},{129,65},{193,129... | collective-permute-start | bytes 589832 | tf_op jit(solution)/shard_map/ppermute | solution.py:30
  8.1 7.5 %collective-permute-start.2 = (bf16[160,512]{1,0:T(8,128)(2,1)S(1)}, bf16[160,512]{1,0:T(8,128)(2,1)S(1)}, u32[]{:S(2)}, u32[]{:S(2)}) collective-permute-start(bf16[160,512]{1,0:T(8,128)(2,1)S(1)} %get-tuple-element.49.refs_0_), channel_id=1, source_target_pairs={{0,16},{16,32},{32,48},{48,0},{1,17},{17,33},{33,49},{49,1},{2,18}... | collective-permute-start | bytes 491528 | tf_op jit(solution)/shard_map/ppermute | solution.py:30
  9.6 6.0 %collective-permute-start.3 = (bf16[160,512]{1,0:T(8,128)(2,1)S(1)}, bf16[160,512]{1,0:T(8,128)(2,1)S(1)}, u32[]{:S(2)}, u32[]{:S(2)}) collective-permute-start(bf16[160,512]{1,0:T(8,128)(2,1)S(1)} %get-tuple-element.49.refs_0_), channel_id=1, source_target_pairs={{0,48},{16,0},{32,16},{48,32},{1,49},{17,1},{33,17},{49,33},{2,50}... | collective-permute-start | bytes 491528 | tf_op jit(solution)/shard_map/ppermute | solution.py:30
  18.3 23.2 %collective-permute-start.6 = (bf16[16,512,512]{2,1,0:T(8,128)(2,1)S(1)}, bf16[16,512,512]{2,1,0:T(8,128)(2,1)S(1)}, u32[]{:S(2)}, u32[]{:S(2)}) collective-permute-start(bf16[16,512,512]{2,1,0:T(8,128)(2,1)S(1)} %shard_map.78), channel_id=1, source_target_pairs={{0,8},{8,0},{1,9},{9,1},{2,10},{10,2},{3,11},{11,3},{4,12},{12,4},... | collective-permute-start | bytes 25165832 | tf_op jit(solution)/shard_map/ppermute | solution.py:30
  18.3 9.7 %collective-permute-start.4 = (bf16[96,512]{1,0:T(8,128)(2,1)S(1)}, bf16[96,512]{1,0:T(8,128)(2,1)S(1)}, u32[]{:S(2)}, u32[]{:S(2)}) collective-permute-start(bf16[96,512]{1,0:T(8,128)(2,1)S(1)} %slice.30), channel_id=1, source_target_pairs={{0,64},{64,128},{128,192},{192,0},{1,65},{65,129},{129,193},{193,1... | collective-permute-start | bytes 294920 | tf_op jit(solution)/shard_map/ppermute | solution.py:30
  22.0 7.7 %collective-permute-start.5 = (bf16[96,512]{1,0:T(8,128)(2,1)S(1)}, bf16[96,512]{1,0:T(8,128)(2,1)S(1)}, u32[]{:S(2)}, u32[]{:S(2)}) collective-permute-start(bf16[96,512]{1,0:T(8,128)(2,1)S(1)} %slice.31), channel_id=1, source_target_pairs={{0,192},{64,0},{128,64},{192,128},{1,193},{65,1},{129,65},{193,129... | collective-permute-start | bytes 294920 | tf_op jit(solution)/shard_map/ppermute | solution.py:30
  22.6 5.1 %collective-permute-start.7 = (bf16[32,512]{1,0:T(8,128)(2,1)S(1)}, bf16[32,512]{1,0:T(8,128)(2,1)S(1)}, u32[]{:S(2)}, u32[]{:S(2)}) collective-permute-start(bf16[32,512]{1,0:T(8,128)(2,1)S(1)} %slice.32), channel_id=1, source_target_pairs={{0,16},{16,32},{32,48},{48,0},{1,17},{17,33},{33,49},{49,1},{2,18}... | collective-permute-start | bytes 98312 | tf_op jit(solution)/shard_map/ppermute | solution.py:30
  29.7 18.5 %collective-permute-start.9 = (bf16[672,512]{1,0:T(8,128)(2,1)S(1)}, bf16[672,512]{1,0:T(8,128)(2,1)S(1)}, u32[]{:S(2)}, u32[]{:S(2)}) collective-permute-start(bf16[672,512]{1,0:T(8,128)(2,1)S(1)} %shard_map.81.refs_5_), channel_id=1, source_target_pairs={{0,16},{16,32},{32,48},{48,0},{1,17},{17,33},{33,49},{49,1},{2,18}... | collective-permute-start | bytes 2064392 | tf_op jit(solution)/shard_map/ppermute | solution.py:30
  31.3 16.9 %collective-permute-start.10 = (bf16[672,512]{1,0:T(8,128)(2,1)S(1)}, bf16[672,512]{1,0:T(8,128)(2,1)S(1)}, u32[]{:S(2)}, u32[]{:S(2)}) collective-permute-start(bf16[672,512]{1,0:T(8,128)(2,1)S(1)} %shard_map.81.refs_5_), channel_id=1, source_target_pairs={{0,48},{16,0},{32,16},{48,32},{1,49},{17,1},{33,17},{49,33},{2,50}... | collective-permute-start | bytes 2064392 | tf_op jit(solution)/shard_map/ppermute | solution.py:30
  33.1 12.5 %collective-permute-start.11 = (bf16[256,512]{1,0:T(8,128)(2,1)S(1)}, bf16[256,512]{1,0:T(8,128)(2,1)S(1)}, u32[]{:S(2)}, u32[]{:S(2)}) collective-permute-start(bf16[256,512]{1,0:T(8,128)(2,1)S(1)} %shard_map.80.refs_5_), channel_id=1, source_target_pairs={{0,64},{64,128},{128,192},{192,0},{1,65},{65,129},{129,193},{193,1... | collective-permute-start | bytes 786440 | tf_op jit(solution)/shard_map/ppermute | solution.py:30
  33.9 12.8 %collective-permute-start.12 = (bf16[256,512]{1,0:T(8,128)(2,1)S(1)}, bf16[256,512]{1,0:T(8,128)(2,1)S(1)}, u32[]{:S(2)}, u32[]{:S(2)}) collective-permute-start(bf16[256,512]{1,0:T(8,128)(2,1)S(1)} %shard_map.80.refs_5_), channel_id=1, source_target_pairs={{0,192},{64,0},{128,64},{192,128},{1,193},{65,1},{129,65},{193,129... | collective-permute-start | bytes 786440 | tf_op jit(solution)/shard_map/ppermute | solution.py:30
  48.2 14.3 %collective-permute-start.13 = (bf16[384,512]{1,0:T(8,128)(2,1)S(1)}, bf16[384,512]{1,0:T(8,128)(2,1)S(1)}, u32[]{:S(2)}, u32[]{:S(2)}) collective-permute-start(bf16[384,512]{1,0:T(8,128)(2,1)S(1)} %shard_map.83), channel_id=1, source_target_pairs={{0,16},{16,32},{32,48},{48,0},{1,17},{17,33},{33,49},{49,1},{2,18}... | collective-permute-start | bytes 1179656 | tf_op jit(solution)/shard_map/ppermute | solution.py:30
  50.0 12.5 %collective-permute-start.14 = (bf16[384,512]{1,0:T(8,128)(2,1)S(1)}, bf16[384,512]{1,0:T(8,128)(2,1)S(1)}, u32[]{:S(2)}, u32[]{:S(2)}) collective-permute-start(bf16[384,512]{1,0:T(8,128)(2,1)S(1)} %shard_map.84), channel_id=1, source_target_pairs={{0,48},{16,0},{32,16},{48,32},{1,49},{17,1},{33,17},{49,33},{2,50}... | collective-permute-start | bytes 1179656 | tf_op jit(solution)/shard_map/ppermute | solution.py:30
  51.8 10.7 %collective-permute-start.15 = (bf16[128,512]{1,0:T(8,128)(2,1)S(1)}, bf16[128,512]{1,0:T(8,128)(2,1)S(1)}, u32[]{:S(2)}, u32[]{:S(2)}) collective-permute-start(bf16[128,512]{1,0:T(8,128)(2,1)S(1)} %slice.34), channel_id=1, source_target_pairs={{0,64},{64,128},{128,192},{192,0},{1,65},{65,129},{129,193},{193,1... | collective-permute-start | bytes 393224 | tf_op jit(solution)/shard_map/ppermute | solution.py:30
  52.7 9.8 %collective-permute-start.16 = (bf16[128,512]{1,0:T(8,128)(2,1)S(1)}, bf16[128,512]{1,0:T(8,128)(2,1)S(1)}, u32[]{:S(2)}, u32[]{:S(2)}) collective-permute-start(bf16[128,512]{1,0:T(8,128)(2,1)S(1)} %slice.35), channel_id=1, source_target_pairs={{0,192},{64,0},{128,64},{192,128},{1,193},{65,1},{129,65},{193,129... | collective-permute-start | bytes 393224 | tf_op jit(solution)/shard_map/ppermute | solution.py:30
  71.1 5.2 %collective-permute-start.20 = (f32[3,1024]{1,0:T(4,128)S(1)}, f32[3,1024]{1,0:T(4,128)S(1)}, u32[]{:S(2)}, u32[]{:S(2)}) collective-permute-start(f32[3,1024]{1,0:T(4,128)S(1)} %get-tuple-element.62.a), channel_id=1, source_target_pairs={{0,2},{1,3},{2,0},{3,1},{4,6},{5,7},{6,4},{7,5},{8,10},{9,11},{10,... | collective-permute-start | bytes 36872 | tf_op jit(solution)/shard_map/ppermute | solution.py:30
  88.0 14.1 %collective-permute-start.23 = (bf16[576,512]{1,0:T(8,128)(2,1)S(1)}, bf16[576,512]{1,0:T(8,128)(2,1)S(1)}, u32[]{:S(2)}, u32[]{:S(2)}) collective-permute-start(bf16[576,512]{1,0:T(8,128)(2,1)S(1)} %get-tuple-element.65), channel_id=1, source_target_pairs={{0,16},{16,32},{32,48},{48,0},{1,17},{17,33},{33,49},{49,1},{2,18}... | collective-permute-start | bytes 1769480 | tf_op jit(solution)/shard_map/ppermute | solution.py:30
  88.4 13.7 %collective-permute-start.24 = (bf16[576,512]{1,0:T(8,128)(2,1)S(1)}, bf16[576,512]{1,0:T(8,128)(2,1)S(1)}, u32[]{:S(2)}, u32[]{:S(2)}) collective-permute-start(bf16[576,512]{1,0:T(8,128)(2,1)S(1)} %get-tuple-element.66), channel_id=1, source_target_pairs={{0,48},{16,0},{32,16},{48,32},{1,49},{17,1},{33,17},{49,33},{2,50}... | collective-permute-start | bytes 1769480 | tf_op jit(solution)/shard_map/ppermute | solution.py:30
  91.3 14.2 %collective-permute-start.25 = (bf16[256,512]{1,0:T(8,128)(2,1)S(1)}, bf16[256,512]{1,0:T(8,128)(2,1)S(1)}, u32[]{:S(2)}, u32[]{:S(2)}) collective-permute-start(bf16[256,512]{1,0:T(8,128)(2,1)S(1)} %get-tuple-element.71), channel_id=1, source_target_pairs={{0,64},{64,128},{128,192},{192,0},{1,65},{65,129},{129,193},{193,1... | collective-permute-start | bytes 786440 | tf_op jit(solution)/shard_map/ppermute | solution.py:30
  91.3 14.2 %collective-permute-start.26 = (bf16[256,512]{1,0:T(8,128)(2,1)S(1)}, bf16[256,512]{1,0:T(8,128)(2,1)S(1)}, u32[]{:S(2)}, u32[]{:S(2)}) collective-permute-start(bf16[256,512]{1,0:T(8,128)(2,1)S(1)} %get-tuple-element.72), channel_id=1, source_target_pairs={{0,192},{64,0},{128,64},{192,128},{1,193},{65,1},{129,65},{193,129... | collective-permute-start | bytes 786440 | tf_op jit(solution)/shard_map/ppermute | solution.py:30
  102.2 8.0 %collective-permute-start.29 = (bf16[288,512]{1,0:T(8,128)(2,1)S(1)}, bf16[288,512]{1,0:T(8,128)(2,1)S(1)}, u32[]{:S(2)}, u32[]{:S(2)}) collective-permute-start(bf16[288,512]{1,0:T(8,128)(2,1)S(1)} %get-tuple-element.82), channel_id=1, source_target_pairs={{0,16},{16,32},{32,48},{48,0},{1,17},{17,33},{33,49},{49,1},{2,18}... | collective-permute-start | bytes 884744 | tf_op jit(solution)/shard_map/ppermute | solution.py:30
  102.3 7.9 %collective-permute-start.30 = (bf16[288,512]{1,0:T(8,128)(2,1)S(1)}, bf16[288,512]{1,0:T(8,128)(2,1)S(1)}, u32[]{:S(2)}, u32[]{:S(2)}) collective-permute-start(bf16[288,512]{1,0:T(8,128)(2,1)S(1)} %get-tuple-element.83), channel_id=1, source_target_pairs={{0,48},{16,0},{32,16},{48,32},{1,49},{17,1},{33,17},{49,33},{2,50}... | collective-permute-start | bytes 884744 | tf_op jit(solution)/shard_map/ppermute | solution.py:30
  105.6 8.4 %collective-permute-start.27 = (bf16[128,512]{1,0:T(8,128)(2,1)S(1)}, bf16[128,512]{1,0:T(8,128)(2,1)S(1)}, u32[]{:S(2)}, u32[]{:S(2)}) collective-permute-start(bf16[128,512]{1,0:T(8,128)(2,1)S(1)} %get-tuple-element.75), channel_id=1, source_target_pairs={{0,64},{64,128},{128,192},{192,0},{1,65},{65,129},{129,193},{193,1... | collective-permute-start | bytes 393224 | tf_op jit(solution)/shard_map/ppermute | solution.py:30
  106.3 7.7 %collective-permute-start.28 = (bf16[128,512]{1,0:T(8,128)(2,1)S(1)}, bf16[128,512]{1,0:T(8,128)(2,1)S(1)}, u32[]{:S(2)}, u32[]{:S(2)}) collective-permute-start(bf16[128,512]{1,0:T(8,128)(2,1)S(1)} %get-tuple-element.76), channel_id=1, source_target_pairs={{0,192},{64,0},{128,64},{192,128},{1,193},{65,1},{129,65},{193,129... | collective-permute-start | bytes 393224 | tf_op jit(solution)/shard_map/ppermute | solution.py:30
  114.1 11.3 %collective-permute-start.31 = (bf16[256,512]{1,0:T(8,128)(2,1)S(1)}, bf16[256,512]{1,0:T(8,128)(2,1)S(1)}, u32[]{:S(2)}, u32[]{:S(2)}) collective-permute-start(bf16[256,512]{1,0:T(8,128)(2,1)S(1)} %get-tuple-element.86), channel_id=1, source_target_pairs={{0,16},{16,32},{32,48},{48,0},{1,17},{17,33},{33,49},{49,1},{2,18}... | collective-permute-start | bytes 786440 | tf_op jit(solution)/shard_map/ppermute | solution.py:30
  114.2 11.2 %collective-permute-start.32 = (bf16[256,512]{1,0:T(8,128)(2,1)S(1)}, bf16[256,512]{1,0:T(8,128)(2,1)S(1)}, u32[]{:S(2)}, u32[]{:S(2)}) collective-permute-start(bf16[256,512]{1,0:T(8,128)(2,1)S(1)} %get-tuple-element.87), channel_id=1, source_target_pairs={{0,48},{16,0},{32,16},{48,32},{1,49},{17,1},{33,17},{49,33},{2,50}... | collective-permute-start | bytes 786440 | tf_op jit(solution)/shard_map/ppermute | solution.py:30
  117.4 11.9 %collective-permute-start.35 = (bf16[192,512]{1,0:T(8,128)(2,1)S(1)}, bf16[192,512]{1,0:T(8,128)(2,1)S(1)}, u32[]{:S(2)}, u32[]{:S(2)}) collective-permute-start(bf16[192,512]{1,0:T(8,128)(2,1)S(1)} %get-tuple-element.84._), channel_id=1, source_target_pairs={{0,64},{64,128},{128,192},{192,0},{1,65},{65,129},{129,193},{193,1... | collective-permute-start | bytes 589832 | tf_op jit(solution)/shard_map/ppermute | solution.py:30
  119.8 14.7 %collective-permute-start.36 = (bf16[192,512]{1,0:T(8,128)(2,1)S(1)}, bf16[192,512]{1,0:T(8,128)(2,1)S(1)}, u32[]{:S(2)}, u32[]{:S(2)}) collective-permute-start(bf16[192,512]{1,0:T(8,128)(2,1)S(1)} %get-tuple-element.92), channel_id=1, source_target_pairs={{0,128},{64,192},{128,0},{192,64},{1,129},{65,193},{129,1},{193,65... | collective-permute-start | bytes 589832 | tf_op jit(solution)/shard_map/ppermute | solution.py:30
  124.4 14.8 %collective-permute-start.37 = (bf16[192,512]{1,0:T(8,128)(2,1)S(1)}, bf16[192,512]{1,0:T(8,128)(2,1)S(1)}, u32[]{:S(2)}, u32[]{:S(2)}) collective-permute-start(bf16[192,512]{1,0:T(8,128)(2,1)S(1)} %get-tuple-element.93), channel_id=1, source_target_pairs={{0,192},{64,0},{128,64},{192,128},{1,193},{65,1},{129,65},{193,129... | collective-permute-start | bytes 589832 | tf_op jit(solution)/shard_map/ppermute | solution.py:30
  125.4 13.8 %collective-permute-start.33 = (bf16[128,512]{1,0:T(8,128)(2,1)S(1)}, bf16[128,512]{1,0:T(8,128)(2,1)S(1)}, u32[]{:S(2)}, u32[]{:S(2)}) collective-permute-start(bf16[128,512]{1,0:T(8,128)(2,1)S(1)} %get-tuple-element.90), channel_id=1, source_target_pairs={{0,16},{16,32},{32,48},{48,0},{1,17},{17,33},{33,49},{49,1},{2,18}... | collective-permute-start | bytes 393224 | tf_op jit(solution)/shard_map/ppermute | solution.py:30
  125.5 13.7 %collective-permute-start.34 = (bf16[128,512]{1,0:T(8,128)(2,1)S(1)}, bf16[128,512]{1,0:T(8,128)(2,1)S(1)}, u32[]{:S(2)}, u32[]{:S(2)}) collective-permute-start(bf16[128,512]{1,0:T(8,128)(2,1)S(1)} %get-tuple-element.91), channel_id=1, source_target_pairs={{0,48},{16,0},{32,16},{48,32},{1,49},{17,1},{33,17},{49,33},{2,50}... | collective-permute-start | bytes 393224 | tf_op jit(solution)/shard_map/ppermute | solution.py:30
  (14 other events, 84.7 us)

commit v6 on v4

--- a/solution.py
+++ b/solution.py
@@ -50,6 +50,17 @@
         compiler_params=params(16),
         cost_estimate=pl.CostEstimate(flops=0, bytes_accessed=size, transcendentals=0),
     )(*args)
+
+
+def joined(*parts, after=()):
+    def body(*refs):
+        to = 0
+        for ref, (_, start, rows) in zip(refs, parts):
+            refs[-1][to : to + rows, :] = ref[start : start + rows, :]
+            to += rows
+
+    out = jax.ShapeDtypeStruct((sum(rows for _, _, rows in parts), WIDE), BF16)
+    return local_call(body, [out], *(array for array, _, _ in parts), *after)[0]
 
 
 def pick(hidden, at, mib):
@@ -212,8 +223,8 @@
     theirs = move(picked, "c", 1)
     zf1, zf2 = move(zb[:PH], "zh", 1), move(za[PH:], "zh", -1)
     xf1, xf2 = move(xb[PR : PR + QH], "x", 1), move(xa[PR + QH :], "x", -1)
-    p = jnp.concatenate([za, zf1, zf2, zb], axis=0)
-    q = jnp.concatenate([head[PR:], xa[PR:], xf1, xf2, xb[PR:]], axis=0)
+    q = joined((head, PR, QR), (xa, PR, QR), (xf1, 0, QH), (xf2, 0, QH), (xb, PR, QR))
+    p = joined((za, 0, PR), (zf1, 0, PH), (zf2, 0, PH), (zb, 0, PR), after=[q])
     pb, pa = move(p, "x", 1), move(p, "x", -1)
     qb, qa = move(q, "zh", 1), move(q, "zh", -1)
     zf1, zf2, at = lax.optimization_barrier((zf1, zf2, at))
@@ -233,8 +244,8 @@
 
     total = logits_call(first, blocks, [head, xa, xb, xf1, xf2, p])
     pb, pa, qb, qa, total = lax.optimization_barrier((pb, pa, qb, qa, total))
-    pf1 = jnp.concatenate([pb[: 3 * PH], xb[:PH]], axis=0)
-    pf2 = jnp.concatenate([pa[3 * PH :], xa[PH:PR]], axis=0)
+    pf1 = joined((pb, 0, 3 * PH), (xb, 0, PH))
+    pf2 = joined((pa, 3 * PH, 3 * PH), (xa, PH, PH))
     pf1, pf2 = move(pf1, "x", 1), move(pf2, "x", -1)
     qf1, qf2 = move(qb[: 2 * QR], "zh", 1), move(qa[2 * QR :], "zh", -1)
 

time: 139 us -> 141 us (1.014)
  starting transfers between devices: 66.8 us -> 70.8 us
  waiting for transfers between devices: 35.2 us -> 32.6 us
    ppermute x38, starting transfers between devices: 66.8 us -> 70.8 us  [move(): return lax.ppermute(value, axis, [(i, (i + by) % n) for i in range(n)])]
    ppermute x38, waiting for transfers between devices: 35.2 us -> 32.6 us  [move(): return lax.ppermute(value, axis, [(i, (i + by) % n) for i in range(n)])]
    pallas_call x12 -> x16, Pallas kernels: 14 us -> 14.1 us  [local_call(): pl.pallas_call(body, out_shape=outs, in_specs=[whole(a.shape) for a in ar...]
  transfers between devices with their start and end apart: 38 -> 38, of which waited for: 15 -> 15; matrix products, arithmetic and copies ran while one was open for 1% -> 1% of each run, Pallas kernels for 15% -> 14%
where the time goes in v6:
time: 141 us; the launch traced here: 139 us
  starting transfers between devices  70.8 us (50%)
  Pallas kernels  33.1 us (23%)
  waiting for transfers between devices  32.6 us (23%)
  local copies, waits for them, and re-layouts  1.63 us (1%)
    ppermute x38, starting transfers between devices, move(): return lax.ppermute(value, axis, [(i, (i + by) % n) for i in range(n)])  70.8 us
    ppermute x38, waiting for transfers between devices, move(): return lax.ppermute(value, axis, [(i, (i + by) % n) for i in range(n)])  32.6 us
    pallas_call x16, Pallas kernels, local_call(): pl.pallas_call(body, out_shape=outs, in_specs=[whole(a.shape) for a in ar...  14.1 us
    pallas_call x2, Pallas kernels, block_call(): pl.pallas_call(body, out_shape=outs, in_specs=[pl.BlockSpec(memory_space=...  10.6 us
    pallas_call x2, Pallas kernels, pick(): pl.pallas_call(body, out_shape=jax.ShapeDtypeStruct((n, TOK, WIDE), BF16)...  8.43 us
  transfers between devices with their start and end apart: 38, of which 15 were waited for; matrix products, arithmetic and copies ran while one was open for 1% of the time, Pallas kernels for 14%

profile of v6, /device:TPU:8, one launch (start us, length us, event | category | flops | bytes accessed | tf_op | source)
XLA Modules:
  0.0 139.4 jit_solution(3515571231695122223)
XLA Ops:
  4.9 3.3 %collective-permute-start = (bf16[192,512]{1,0:T(8,128)(2,1)S(1)}, bf16[192,512]{1,0:T(8,128)(2,1)S(1)}, u32[]{:S(2)}, u32[]{:S(2)}) collective-permute-start(bf16[192,512]{1,0:T(8,128)(2,1)S(1)} %slice.34), channel_id=1, source_target_pairs={{0,64},{64,128},{128,192},{192,0},{1,65},{65,129},{129,193},{193,1... | collective-permute-start | bytes 589832 | tf_op jit(solution)/shard_map/ppermute | solution.py:30
  8.3 3.1 %collective-permute-start.1 = (bf16[192,512]{1,0:T(8,128)(2,1)S(1)}, bf16[192,512]{1,0:T(8,128)(2,1)S(1)}, u32[]{:S(2)}, u32[]{:S(2)}) collective-permute-start(bf16[192,512]{1,0:T(8,128)(2,1)S(1)} %slice.34), channel_id=1, source_target_pairs={{0,192},{64,0},{128,64},{192,128},{1,193},{65,1},{129,65},{193,129... | collective-permute-start | bytes 589832 | tf_op jit(solution)/shard_map/ppermute | solution.py:30
  11.4 4.2 %shard_map.77 = bf16[16,512,512]{2,1,0:T(8,128)(2,1)S(1)} custom-call(s32[16]{0:T(128)S(1)} %broadcast_add_fusion.1.at_ref, bf16[512,16384]{1,0:T(8,128)(2,1)} %h_ref.3), custom_call_target="tpu_custom_call" | custom-call | bytes 16777216 | tf_op jit(solution)/shard_map/pallas_call | solution.py:83
  17.2 3.8 %collective-permute-done.1.refs_0_ = bf16[192,512]{1,0:T(8,128)(2,1)S(1)} collective-permute-done((bf16[192,512]{1,0:T(8,128)(2,1)S(1)}, bf16[192,512]{1,0:T(8,128)(2,1)S(1)}, u32[]{:S(2)}, u32[]{:S(2)}) %collective-permute-start.1) | collective-permute-done | bytes 196640 | tf_op jit(solution)/shard_map/ppermute | solution.py:30
  21.1 3.7 %collective-permute-start.4 = (bf16[96,512]{1,0:T(8,128)(2,1)S(1)}, bf16[96,512]{1,0:T(8,128)(2,1)S(1)}, u32[]{:S(2)}, u32[]{:S(2)}) collective-permute-start(bf16[96,512]{1,0:T(8,128)(2,1)S(1)} %slice.35), channel_id=1, source_target_pairs={{0,64},{64,128},{128,192},{192,0},{1,65},{65,129},{129,193},{193,1... | collective-permute-start | bytes 294920 | tf_op jit(solution)/shard_map/ppermute | solution.py:30
  25.6 3.0 %collective-permute-start.8 = (bf16[32,512]{1,0:T(8,128)(2,1)S(1)}, bf16[32,512]{1,0:T(8,128)(2,1)S(1)}, u32[]{:S(2)}, u32[]{:S(2)}) collective-permute-start(bf16[32,512]{1,0:T(8,128)(2,1)S(1)} %slice.38), channel_id=1, source_target_pairs={{0,48},{16,0},{32,16},{48,32},{1,49},{17,1},{33,17},{49,33},{2,50}... | collective-permute-start | bytes 98312 | tf_op jit(solution)/shard_map/ppermute | solution.py:30
  30.5 1.9 %collective-permute-done.5.refs_2_ = bf16[96,512]{1,0:T(8,128)(2,1)S(1)} collective-permute-done((bf16[96,512]{1,0:T(8,128)(2,1)S(1)}, bf16[96,512]{1,0:T(8,128)(2,1)S(1)}, u32[]{:S(2)}, u32[]{:S(2)}) %collective-permute-start.5) | collective-permute-done | bytes 98336 | tf_op jit(solution)/shard_map/ppermute | solution.py:30
  32.8 3.0 %collective-permute-start.10 = (bf16[576,512]{1,0:T(8,128)(2,1)S(1)}, bf16[576,512]{1,0:T(8,128)(2,1)S(1)}, u32[]{:S(2)}, u32[]{:S(2)}) collective-permute-start(bf16[576,512]{1,0:T(8,128)(2,1)S(1)} %shard_map.80.refs_5_), channel_id=1, source_target_pairs={{0,48},{16,0},{32,16},{48,32},{1,49},{17,1},{33,17},{49,33},{2,50}... | collective-permute-start | bytes 1769480 | tf_op jit(solution)/shard_map/ppermute | solution.py:30
  36.6 3.3 %collective-permute-start.12 = (bf16[256,512]{1,0:T(8,128)(2,1)S(1)}, bf16[256,512]{1,0:T(8,128)(2,1)S(1)}, u32[]{:S(2)}, u32[]{:S(2)}) collective-permute-start(bf16[256,512]{1,0:T(8,128)(2,1)S(1)} %shard_map.79.refs_4_), channel_id=1, source_target_pairs={{0,192},{64,0},{128,64},{192,128},{1,193},{65,1},{129,65},{193,129... | collective-permute-start | bytes 786440 | tf_op jit(solution)/shard_map/ppermute | solution.py:30
  39.9 4.2 %shard_map.78.m_ref = bf16[16,512,512]{2,1,0:T(8,128)(2,1)S(1)} custom-call(s32[16]{0:T(128)S(1)} %broadcast_add_fusion.at_ref, bf16[512,16384]{1,0:T(8,128)(2,1)} %h_ref.3), custom_call_target="tpu_custom_call" | custom-call | bytes 16777216 | tf_op jit(solution)/shard_map/pallas_call | solution.py:83
  44.2 2.6 %shard_map.81.refs_4_ = f32[256,1024]{1,0:T(8,128)S(1)} custom-call(bf16[16,512,512]{2,1,0:T(8,128)(2,1)S(1)} %shard_map.78.m_ref, bf16[16,512,512]{2,1,0:T(8,128)(2,1)S(1)} %collective-permute-done.6.t_ref, bf16[256,512]{1,0:T(8,128)(2,1)S(1)} %copy-done.2, bf16[256,512]{1,0:T(8,128)(2,1)S(1)} %collective-permute-done.3.refs_1_, ...), custom_call_target="tpu_custom_call" | custom-call | bytes 19267584 | tf_op jit(solution)/shard_map/pallas_call | solution.py:45
  49.8 3.3 %collective-permute-start.14 = (bf16[384,512]{1,0:T(8,128)(2,1)S(1)}, bf16[384,512]{1,0:T(8,128)(2,1)S(1)}, u32[]{:S(2)}, u32[]{:S(2)}) collective-permute-start(bf16[384,512]{1,0:T(8,128)(2,1)S(1)} %shard_map.83), channel_id=1, source_target_pairs={{0,48},{16,0},{32,16},{48,32},{1,49},{17,1},{33,17},{49,33},{2,50}... | collective-permute-start | bytes 1179656 | tf_op jit(solution)/shard_map/ppermute | solution.py:30
  54.7 2.8 %collective-permute-start.16 = (bf16[128,512]{1,0:T(8,128)(2,1)S(1)}, bf16[128,512]{1,0:T(8,128)(2,1)S(1)}, u32[]{:S(2)}, u32[]{:S(2)}) collective-permute-start(bf16[128,512]{1,0:T(8,128)(2,1)S(1)} %slice.40), channel_id=1, source_target_pairs={{0,192},{64,0},{128,64},{192,128},{1,193},{65,1},{129,65},{193,129... | collective-permute-start | bytes 393224 | tf_op jit(solution)/shard_map/ppermute | solution.py:30
  57.5 5.6 %shard_map.84.refs_4_ = f32[256,1024]{1,0:T(8,128)S(1)} custom-call(bf16[16,512,512]{2,1,0:T(8,128)(2,1)S(1)} %shard_map.78.m_ref, bf16[16,512,512]{2,1,0:T(8,128)(2,1)S(1)} %collective-permute-done.6.t_ref, bf16[576,512]{1,0:T(8,128)(2,1)S(1)} %collective-permute-done.10.refs_0_, bf16[576,512]{1,0:T(8,128)(2,1)S(1)} %collective-permute-done.9.refs_0_.refs_1_, ...), custom_call_target="tpu_custom_call" | custom-call | bytes 20578304 | tf_op jit(solution)/shard_map/pallas_call | solution.py:45
  63.2 3.3 %shard_map.85.mine = f32[256,1024]{1,0:T(8,128)S(1)} custom-call(bf16[16,512,512]{2,1,0:T(8,128)(2,1)S(1)} %shard_map.78.m_ref, bf16[16,512,512]{2,1,0:T(8,128)(2,1)S(1)} %collective-permute-done.6.t_ref, bf16[384,512]{1,0:T(8,128)(2,1)S(1)} %collective-permute-done.13.refs_0_, bf16[384,512]{1,0:T(8,128)(2,1)S(1)} %collective-permute-done.14.refs_1_, ...), custom_call_target="tpu_custom_call" | custom-call | bytes 19922944 | tf_op jit(solution)/shard_map/pallas_call | solution.py:45
  67.3 1.9 %collective-permute-done.18 = f32[3,512]{1,0:T(4,128)S(1)} collective-permute-done((f32[3,512]{1,0:T(4,128)S(1)}, f32[3,512]{1,0:T(4,128)S(1)}, u32[]{:S(2)}, u32[]{:S(2)}) %collective-permute-start.18) | collective-permute-done | bytes 6176 | tf_op jit(solution)/shard_map/ppermute | solution.py:30
  72.6 2.4 %collective-permute-start.21 = (f32[3,1024]{1,0:T(4,128)S(1)}, f32[3,1024]{1,0:T(4,128)S(1)}, u32[]{:S(2)}, u32[]{:S(2)}) collective-permute-start(f32[3,1024]{1,0:T(4,128)S(1)} %get-tuple-element.58.a), channel_id=1, source_target_pairs={{0,3},{1,0},{2,1},{3,2},{4,7},{5,4},{6,5},{7,6},{8,11},{9,8},{10,9... | collective-permute-start | bytes 36872 | tf_op jit(solution)/shard_map/ppermute | solution.py:30
  77.0 2.7 %collective-permute-start.22 = (f32[3,1024]{1,0:T(4,128)S(1)}, f32[3,1024]{1,0:T(4,128)S(1)}, u32[]{:S(2)}, u32[]{:S(2)}) collective-permute-start(f32[3,1024]{1,0:T(4,128)S(1)} %shard_map.87.s), channel_id=1, source_target_pairs={{0,4},{4,0},{1,5},{5,1},{2,6},{6,2},{3,7},{7,3},{8,12},{12,8},{9,1... | collective-permute-start | bytes 36872 | tf_op jit(solution)/shard_map/ppermute | solution.py:30
  81.7 7.5 %shard_map.89 = (bf16[576,512]{1,0:T(8,128)(2,1)S(1)}, bf16[576,512]{1,0:T(8,128)(2,1)S(1)}, bf16[256,512]{1,0:T(8,128)(2,1)S(1)}, bf16[256,512]{1,0:T(8,128)(2,...) custom-call(bf16[16,512,512]{2,1,0:T(8,128)(2,1)} %copy-done, ...), custom_call_target="tpu_custom_call" | custom-call | flops 3221225472 | bytes 12582912 | tf_op jit(solution)/shard_map/pallas_call | solution.py:124
  89.3 3.2 %collective-permute-start.24 = (bf16[576,512]{1,0:T(8,128)(2,1)S(1)}, bf16[576,512]{1,0:T(8,128)(2,1)S(1)}, u32[]{:S(2)}, u32[]{:S(2)}) collective-permute-start(bf16[576,512]{1,0:T(8,128)(2,1)S(1)} %get-tuple-element.62), channel_id=1, source_target_pairs={{0,48},{16,0},{32,16},{48,32},{1,49},{17,1},{33,17},{49,33},{2,50}... | collective-permute-start | bytes 1769480 | tf_op jit(solution)/shard_map/ppermute | solution.py:30
  94.0 2.7 %collective-permute-start.26 = (bf16[256,512]{1,0:T(8,128)(2,1)S(1)}, bf16[256,512]{1,0:T(8,128)(2,1)S(1)}, u32[]{:S(2)}, u32[]{:S(2)}) collective-permute-start(bf16[256,512]{1,0:T(8,128)(2,1)S(1)} %get-tuple-element.68), channel_id=1, source_target_pairs={{0,192},{64,0},{128,64},{192,128},{1,193},{65,1},{129,65},{193,129... | collective-permute-start | bytes 786440 | tf_op jit(solution)/shard_map/ppermute | solution.py:30
  96.7 3.1 %shard_map.90 = (f32[768,512]{1,0:T(8,128)S(1)}, f32[256,512]{1,0:T(8,128)S(1)}) custom-call(bf16[16,512,512]{2,1,0:T(8,128)(2,1)} %copy-done, bf16[16,512,512]{2,1,0:T(8,128)(2,1)} %copy-done.1, bf16[256,1024]{1,0:T(8,128)(2,1)S(1)} %get-tuple-element.60.refs_0_), custom_call_target="tpu_custom_call" | custom-call | flops 1073741824 | bytes 4194304 | tf_op jit(solution)/shard_map/pallas_call | solution.py:124
  99.8 3.8 %collective-permute-done.23.u.up = bf16[576,512]{1,0:T(8,128)(2,1)S(1)} collective-permute-done((bf16[576,512]{1,0:T(8,128)(2,1)S(1)}, bf16[576,512]{1,0:T(8,128)(2,1)S(1)}, u32[]{:S(2)}, u32[]{:S(2)}) %collective-permute-start.23) | collective-permute-done | bytes 589856 | tf_op jit(solution)/shard_map/ppermute | solution.py:30
  103.8 3.2 %collective-permute-start.30 = (bf16[288,512]{1,0:T(8,128)(2,1)S(1)}, bf16[288,512]{1,0:T(8,128)(2,1)S(1)}, u32[]{:S(2)}, u32[]{:S(2)}) collective-permute-start(bf16[288,512]{1,0:T(8,128)(2,1)S(1)} %get-tuple-element.79), channel_id=1, source_target_pairs={{0,48},{16,0},{32,16},{48,32},{1,49},{17,1},{33,17},{49,33},{2,50}... | collective-permute-start | bytes 884744 | tf_op jit(solution)/shard_map/ppermute | solution.py:30
  108.5 2.8 %collective-permute-start.28 = (bf16[128,512]{1,0:T(8,128)(2,1)S(1)}, bf16[128,512]{1,0:T(8,128)(2,1)S(1)}, u32[]{:S(2)}, u32[]{:S(2)}) collective-permute-start(bf16[128,512]{1,0:T(8,128)(2,1)S(1)} %get-tuple-element.72), channel_id=1, source_target_pairs={{0,192},{64,0},{128,64},{192,128},{1,193},{65,1},{129,65},{193,129... | collective-permute-start | bytes 393224 | tf_op jit(solution)/shard_map/ppermute | solution.py:30
  111.9 3.4 %collective-permute-done.27.up2 = bf16[128,512]{1,0:T(8,128)(2,1)S(1)} collective-permute-done((bf16[128,512]{1,0:T(8,128)(2,1)S(1)}, bf16[128,512]{1,0:T(8,128)(2,1)S(1)}, u32[]{:S(2)}, u32[]{:S(2)}) %collective-permute-start.27) | collective-permute-done | bytes 131104 | tf_op jit(solution)/shard_map/ppermute | solution.py:30
  115.5 3.2 %collective-permute-start.32 = (bf16[256,512]{1,0:T(8,128)(2,1)S(1)}, bf16[256,512]{1,0:T(8,128)(2,1)S(1)}, u32[]{:S(2)}, u32[]{:S(2)}) collective-permute-start(bf16[256,512]{1,0:T(8,128)(2,1)S(1)} %get-tuple-element.83), channel_id=1, source_target_pairs={{0,48},{16,0},{32,16},{48,32},{1,49},{17,1},{33,17},{49,33},{2,50}... | collective-permute-start | bytes 786440 | tf_op jit(solution)/shard_map/ppermute | solution.py:30
  118.8 2.9 %collective-permute-start.35 = (bf16[192,512]{1,0:T(8,128)(2,1)S(1)}, bf16[192,512]{1,0:T(8,128)(2,1)S(1)}, u32[]{:S(2)}, u32[]{:S(2)}) collective-permute-start(bf16[192,512]{1,0:T(8,128)(2,1)S(1)} %get-tuple-element.80._), channel_id=1, source_target_pairs={{0,64},{64,128},{128,192},{192,0},{1,65},{65,129},{129,193},{193,1... | collective-permute-start | bytes 589832 | tf_op jit(solution)/shard_map/ppermute | solution.py:30
  121.7 3.9 %collective-permute-start.36 = (bf16[192,512]{1,0:T(8,128)(2,1)S(1)}, bf16[192,512]{1,0:T(8,128)(2,1)S(1)}, u32[]{:S(2)}, u32[]{:S(2)}) collective-permute-start(bf16[192,512]{1,0:T(8,128)(2,1)S(1)} %get-tuple-element.88), channel_id=1, source_target_pairs={{0,128},{64,192},{128,0},{192,64},{1,129},{65,193},{129,1},{193,65... | collective-permute-start | bytes 589832 | tf_op jit(solution)/shard_map/ppermute | solution.py:30
  127.1 3.2 %collective-permute-start.34 = (bf16[128,512]{1,0:T(8,128)(2,1)S(1)}, bf16[128,512]{1,0:T(8,128)(2,1)S(1)}, u32[]{:S(2)}, u32[]{:S(2)}) collective-permute-start(bf16[128,512]{1,0:T(8,128)(2,1)S(1)} %get-tuple-element.87), channel_id=1, source_target_pairs={{0,48},{16,0},{32,16},{48,32},{1,49},{17,1},{33,17},{49,33},{2,50}... | collective-permute-start | bytes 393224 | tf_op jit(solution)/shard_map/ppermute | solution.py:30
  130.9 5.5 %collective-permute-done.36.z2 = bf16[192,512]{1,0:T(8,128)(2,1)S(1)} collective-permute-done((bf16[192,512]{1,0:T(8,128)(2,1)S(1)}, bf16[192,512]{1,0:T(8,128)(2,1)S(1)}, u32[]{:S(2)}, u32[]{:S(2)}) %collective-permute-start.36) | collective-permute-done | bytes 196640 | tf_op jit(solution)/shard_map/ppermute | solution.py:30
  136.5 1.9 %collective-permute-done.37.z3 = bf16[192,512]{1,0:T(8,128)(2,1)S(1)} collective-permute-done((bf16[192,512]{1,0:T(8,128)(2,1)S(1)}, bf16[192,512]{1,0:T(8,128)(2,1)S(1)}, u32[]{:S(2)}, u32[]{:S(2)}) %collective-permute-start.37) | collective-permute-done | bytes 196640 | tf_op jit(solution)/shard_map/ppermute | solution.py:30
  (95 shorter events, 29.8 us)
Async XLA Ops:
  0.6 20.4 %collective-permute-start.2 = (bf16[256,512]{1,0:T(8,128)(2,1)}, bf16[256,512]{1,0:T(8,128)(2,1)S(1)}, u32[]{:S(2)}, u32[]{:S(2)}) collective-permute-start(bf16[256,512]{1,0:T(8,128)(2,1)} %refs_0_.3), channel_id=1, source_target_pairs={{0,16},{16,32},{32,48},{48,0},{1,17},{17,33},{33,49},{49,1},{2,18}... | collective-permute-start | bytes 786440 | tf_op jit(solution)/shard_map/ppermute | solution.py:30
  2.2 18.8 %collective-permute-start.3 = (bf16[256,512]{1,0:T(8,128)(2,1)}, bf16[256,512]{1,0:T(8,128)(2,1)S(1)}, u32[]{:S(2)}, u32[]{:S(2)}) collective-permute-start(bf16[256,512]{1,0:T(8,128)(2,1)} %refs_0_.3), channel_id=1, source_target_pairs={{0,48},{16,0},{32,16},{48,32},{1,49},{17,1},{33,17},{49,33},{2,50}... | collective-permute-start | bytes 786440 | tf_op jit(solution)/shard_map/ppermute | solution.py:30
  4.9 12.3 %collective-permute-start = (bf16[192,512]{1,0:T(8,128)(2,1)S(1)}, bf16[192,512]{1,0:T(8,128)(2,1)S(1)}, u32[]{:S(2)}, u32[]{:S(2)}) collective-permute-start(bf16[192,512]{1,0:T(8,128)(2,1)S(1)} %slice.34), channel_id=1, source_target_pairs={{0,64},{64,128},{128,192},{192,0},{1,65},{65,129},{129,193},{193,1... | collective-permute-start | bytes 589832 | tf_op jit(solution)/shard_map/ppermute | solution.py:30
  8.3 12.8 %collective-permute-start.1 = (bf16[192,512]{1,0:T(8,128)(2,1)S(1)}, bf16[192,512]{1,0:T(8,128)(2,1)S(1)}, u32[]{:S(2)}, u32[]{:S(2)}) collective-permute-start(bf16[192,512]{1,0:T(8,128)(2,1)S(1)} %slice.34), channel_id=1, source_target_pairs={{0,192},{64,0},{128,64},{192,128},{1,193},{65,1},{129,65},{193,129... | collective-permute-start | bytes 589832 | tf_op jit(solution)/shard_map/ppermute | solution.py:30
  21.0 23.1 %collective-permute-start.6 = (bf16[16,512,512]{2,1,0:T(8,128)(2,1)S(1)}, bf16[16,512,512]{2,1,0:T(8,128)(2,1)S(1)}, u32[]{:S(2)}, u32[]{:S(2)}) collective-permute-start(bf16[16,512,512]{2,1,0:T(8,128)(2,1)S(1)} %shard_map.77), channel_id=1, source_target_pairs={{0,8},{8,0},{1,9},{9,1},{2,10},{10,2},{3,11},{11,3},{4,12},{12,4},... | collective-permute-start | bytes 25165832 | tf_op jit(solution)/shard_map/ppermute | solution.py:30
  21.1 9.5 %collective-permute-start.4 = (bf16[96,512]{1,0:T(8,128)(2,1)S(1)}, bf16[96,512]{1,0:T(8,128)(2,1)S(1)}, u32[]{:S(2)}, u32[]{:S(2)}) collective-permute-start(bf16[96,512]{1,0:T(8,128)(2,1)S(1)} %slice.35), channel_id=1, source_target_pairs={{0,64},{64,128},{128,192},{192,0},{1,65},{65,129},{129,193},{193,1... | collective-permute-start | bytes 294920 | tf_op jit(solution)/shard_map/ppermute | solution.py:30
  24.8 7.6 %collective-permute-start.5 = (bf16[96,512]{1,0:T(8,128)(2,1)S(1)}, bf16[96,512]{1,0:T(8,128)(2,1)S(1)}, u32[]{:S(2)}, u32[]{:S(2)}) collective-permute-start(bf16[96,512]{1,0:T(8,128)(2,1)S(1)} %slice.36), channel_id=1, source_target_pairs={{0,192},{64,0},{128,64},{192,128},{1,193},{65,1},{129,65},{193,129... | collective-permute-start | bytes 294920 | tf_op jit(solution)/shard_map/ppermute | solution.py:30
  25.4 5.1 %collective-permute-start.7 = (bf16[32,512]{1,0:T(8,128)(2,1)S(1)}, bf16[32,512]{1,0:T(8,128)(2,1)S(1)}, u32[]{:S(2)}, u32[]{:S(2)}) collective-permute-start(bf16[32,512]{1,0:T(8,128)(2,1)S(1)} %slice.37), channel_id=1, source_target_pairs={{0,16},{16,32},{32,48},{48,0},{1,17},{17,33},{33,49},{49,1},{2,18}... | collective-permute-start | bytes 98312 | tf_op jit(solution)/shard_map/ppermute | solution.py:30
  32.5 17.0 %collective-permute-start.9 = (bf16[576,512]{1,0:T(8,128)(2,1)S(1)}, bf16[576,512]{1,0:T(8,128)(2,1)S(1)}, u32[]{:S(2)}, u32[]{:S(2)}) collective-permute-start(bf16[576,512]{1,0:T(8,128)(2,1)S(1)} %shard_map.80.refs_5_), channel_id=1, source_target_pairs={{0,16},{16,32},{32,48},{48,0},{1,17},{17,33},{33,49},{49,1},{2,18}... | collective-permute-start | bytes 1769480 | tf_op jit(solution)/shard_map/ppermute | solution.py:30
  32.8 16.6 %collective-permute-start.10 = (bf16[576,512]{1,0:T(8,128)(2,1)S(1)}, bf16[576,512]{1,0:T(8,128)(2,1)S(1)}, u32[]{:S(2)}, u32[]{:S(2)}) collective-permute-start(bf16[576,512]{1,0:T(8,128)(2,1)S(1)} %shard_map.80.refs_5_), channel_id=1, source_target_pairs={{0,48},{16,0},{32,16},{48,32},{1,49},{17,1},{33,17},{49,33},{2,50}... | collective-permute-start | bytes 1769480 | tf_op jit(solution)/shard_map/ppermute | solution.py:30
  35.8 12.5 %collective-permute-start.11 = (bf16[256,512]{1,0:T(8,128)(2,1)S(1)}, bf16[256,512]{1,0:T(8,128)(2,1)S(1)}, u32[]{:S(2)}, u32[]{:S(2)}) collective-permute-start(bf16[256,512]{1,0:T(8,128)(2,1)S(1)} %shard_map.79.refs_4_), channel_id=1, source_target_pairs={{0,64},{64,128},{128,192},{192,0},{1,65},{65,129},{129,193},{193,1... | collective-permute-start | bytes 786440 | tf_op jit(solution)/shard_map/ppermute | solution.py:30
  36.6 12.9 %collective-permute-start.12 = (bf16[256,512]{1,0:T(8,128)(2,1)S(1)}, bf16[256,512]{1,0:T(8,128)(2,1)S(1)}, u32[]{:S(2)}, u32[]{:S(2)}) collective-permute-start(bf16[256,512]{1,0:T(8,128)(2,1)S(1)} %shard_map.79.refs_4_), channel_id=1, source_target_pairs={{0,192},{64,0},{128,64},{192,128},{1,193},{65,1},{129,65},{193,129... | collective-permute-start | bytes 786440 | tf_op jit(solution)/shard_map/ppermute | solution.py:30
  49.5 13.7 %collective-permute-start.13 = (bf16[384,512]{1,0:T(8,128)(2,1)S(1)}, bf16[384,512]{1,0:T(8,128)(2,1)S(1)}, u32[]{:S(2)}, u32[]{:S(2)}) collective-permute-start(bf16[384,512]{1,0:T(8,128)(2,1)S(1)} %shard_map.82), channel_id=1, source_target_pairs={{0,16},{16,32},{32,48},{48,0},{1,17},{17,33},{33,49},{49,1},{2,18}... | collective-permute-start | bytes 1179656 | tf_op jit(solution)/shard_map/ppermute | solution.py:30
  49.8 13.4 %collective-permute-start.14 = (bf16[384,512]{1,0:T(8,128)(2,1)S(1)}, bf16[384,512]{1,0:T(8,128)(2,1)S(1)}, u32[]{:S(2)}, u32[]{:S(2)}) collective-permute-start(bf16[384,512]{1,0:T(8,128)(2,1)S(1)} %shard_map.83), channel_id=1, source_target_pairs={{0,48},{16,0},{32,16},{48,32},{1,49},{17,1},{33,17},{49,33},{2,50}... | collective-permute-start | bytes 1179656 | tf_op jit(solution)/shard_map/ppermute | solution.py:30
  53.1 10.0 %collective-permute-start.15 = (bf16[128,512]{1,0:T(8,128)(2,1)S(1)}, bf16[128,512]{1,0:T(8,128)(2,1)S(1)}, u32[]{:S(2)}, u32[]{:S(2)}) collective-permute-start(bf16[128,512]{1,0:T(8,128)(2,1)S(1)} %slice.39), channel_id=1, source_target_pairs={{0,64},{64,128},{128,192},{192,0},{1,65},{65,129},{129,193},{193,1... | collective-permute-start | bytes 393224 | tf_op jit(solution)/shard_map/ppermute | solution.py:30
  54.7 8.4 %collective-permute-start.16 = (bf16[128,512]{1,0:T(8,128)(2,1)S(1)}, bf16[128,512]{1,0:T(8,128)(2,1)S(1)}, u32[]{:S(2)}, u32[]{:S(2)}) collective-permute-start(bf16[128,512]{1,0:T(8,128)(2,1)S(1)} %slice.40), channel_id=1, source_target_pairs={{0,192},{64,0},{128,64},{192,128},{1,193},{65,1},{129,65},{193,129... | collective-permute-start | bytes 393224 | tf_op jit(solution)/shard_map/ppermute | solution.py:30
  71.7 5.2 %collective-permute-start.20 = (f32[3,1024]{1,0:T(4,128)S(1)}, f32[3,1024]{1,0:T(4,128)S(1)}, u32[]{:S(2)}, u32[]{:S(2)}) collective-permute-start(f32[3,1024]{1,0:T(4,128)S(1)} %get-tuple-element.58.a), channel_id=1, source_target_pairs={{0,2},{1,3},{2,0},{3,1},{4,6},{5,7},{6,4},{7,5},{8,10},{9,11},{10,... | collective-permute-start | bytes 36872 | tf_op jit(solution)/shard_map/ppermute | solution.py:30
  89.2 14.4 %collective-permute-start.23 = (bf16[576,512]{1,0:T(8,128)(2,1)S(1)}, bf16[576,512]{1,0:T(8,128)(2,1)S(1)}, u32[]{:S(2)}, u32[]{:S(2)}) collective-permute-start(bf16[576,512]{1,0:T(8,128)(2,1)S(1)} %get-tuple-element.61), channel_id=1, source_target_pairs={{0,16},{16,32},{32,48},{48,0},{1,17},{17,33},{33,49},{49,1},{2,18}... | collective-permute-start | bytes 1769480 | tf_op jit(solution)/shard_map/ppermute | solution.py:30
  89.3 14.3 %collective-permute-start.24 = (bf16[576,512]{1,0:T(8,128)(2,1)S(1)}, bf16[576,512]{1,0:T(8,128)(2,1)S(1)}, u32[]{:S(2)}, u32[]{:S(2)}) collective-permute-start(bf16[576,512]{1,0:T(8,128)(2,1)S(1)} %get-tuple-element.62), channel_id=1, source_target_pairs={{0,48},{16,0},{32,16},{48,32},{1,49},{17,1},{33,17},{49,33},{2,50}... | collective-permute-start | bytes 1769480 | tf_op jit(solution)/shard_map/ppermute | solution.py:30
  92.5 14.5 %collective-permute-start.25 = (bf16[256,512]{1,0:T(8,128)(2,1)S(1)}, bf16[256,512]{1,0:T(8,128)(2,1)S(1)}, u32[]{:S(2)}, u32[]{:S(2)}) collective-permute-start(bf16[256,512]{1,0:T(8,128)(2,1)S(1)} %get-tuple-element.67), channel_id=1, source_target_pairs={{0,64},{64,128},{128,192},{192,0},{1,65},{65,129},{129,193},{193,1... | collective-permute-start | bytes 786440 | tf_op jit(solution)/shard_map/ppermute | solution.py:30
  94.0 13.0 %collective-permute-start.26 = (bf16[256,512]{1,0:T(8,128)(2,1)S(1)}, bf16[256,512]{1,0:T(8,128)(2,1)S(1)}, u32[]{:S(2)}, u32[]{:S(2)}) collective-permute-start(bf16[256,512]{1,0:T(8,128)(2,1)S(1)} %get-tuple-element.68), channel_id=1, source_target_pairs={{0,192},{64,0},{128,64},{192,128},{1,193},{65,1},{129,65},{193,129... | collective-permute-start | bytes 786440 | tf_op jit(solution)/shard_map/ppermute | solution.py:30
  103.7 8.0 %collective-permute-start.29 = (bf16[288,512]{1,0:T(8,128)(2,1)S(1)}, bf16[288,512]{1,0:T(8,128)(2,1)S(1)}, u32[]{:S(2)}, u32[]{:S(2)}) collective-permute-start(bf16[288,512]{1,0:T(8,128)(2,1)S(1)} %get-tuple-element.78), channel_id=1, source_target_pairs={{0,16},{16,32},{32,48},{48,0},{1,17},{17,33},{33,49},{49,1},{2,18}... | collective-permute-start | bytes 884744 | tf_op jit(solution)/shard_map/ppermute | solution.py:30
  103.8 7.9 %collective-permute-start.30 = (bf16[288,512]{1,0:T(8,128)(2,1)S(1)}, bf16[288,512]{1,0:T(8,128)(2,1)S(1)}, u32[]{:S(2)}, u32[]{:S(2)}) collective-permute-start(bf16[288,512]{1,0:T(8,128)(2,1)S(1)} %get-tuple-element.79), channel_id=1, source_target_pairs={{0,48},{16,0},{32,16},{48,32},{1,49},{17,1},{33,17},{49,33},{2,50}... | collective-permute-start | bytes 884744 | tf_op jit(solution)/shard_map/ppermute | solution.py:30
  107.0 8.2 %collective-permute-start.27 = (bf16[128,512]{1,0:T(8,128)(2,1)S(1)}, bf16[128,512]{1,0:T(8,128)(2,1)S(1)}, u32[]{:S(2)}, u32[]{:S(2)}) collective-permute-start(bf16[128,512]{1,0:T(8,128)(2,1)S(1)} %get-tuple-element.71), channel_id=1, source_target_pairs={{0,64},{64,128},{128,192},{192,0},{1,65},{65,129},{129,193},{193,1... | collective-permute-start | bytes 393224 | tf_op jit(solution)/shard_map/ppermute | solution.py:30
  108.5 6.8 %collective-permute-start.28 = (bf16[128,512]{1,0:T(8,128)(2,1)S(1)}, bf16[128,512]{1,0:T(8,128)(2,1)S(1)}, u32[]{:S(2)}, u32[]{:S(2)}) collective-permute-start(bf16[128,512]{1,0:T(8,128)(2,1)S(1)} %get-tuple-element.72), channel_id=1, source_target_pairs={{0,192},{64,0},{128,64},{192,128},{1,193},{65,1},{129,65},{193,129... | collective-permute-start | bytes 393224 | tf_op jit(solution)/shard_map/ppermute | solution.py:30
  115.5 11.5 %collective-permute-start.31 = (bf16[256,512]{1,0:T(8,128)(2,1)S(1)}, bf16[256,512]{1,0:T(8,128)(2,1)S(1)}, u32[]{:S(2)}, u32[]{:S(2)}) collective-permute-start(bf16[256,512]{1,0:T(8,128)(2,1)S(1)} %get-tuple-element.82), channel_id=1, source_target_pairs={{0,16},{16,32},{32,48},{48,0},{1,17},{17,33},{33,49},{49,1},{2,18}... | collective-permute-start | bytes 786440 | tf_op jit(solution)/shard_map/ppermute | solution.py:30
  115.5 11.4 %collective-permute-start.32 = (bf16[256,512]{1,0:T(8,128)(2,1)S(1)}, bf16[256,512]{1,0:T(8,128)(2,1)S(1)}, u32[]{:S(2)}, u32[]{:S(2)}) collective-permute-start(bf16[256,512]{1,0:T(8,128)(2,1)S(1)} %get-tuple-element.83), channel_id=1, source_target_pairs={{0,48},{16,0},{32,16},{48,32},{1,49},{17,1},{33,17},{49,33},{2,50}... | collective-permute-start | bytes 786440 | tf_op jit(solution)/shard_map/ppermute | solution.py:30
  118.8 12.1 %collective-permute-start.35 = (bf16[192,512]{1,0:T(8,128)(2,1)S(1)}, bf16[192,512]{1,0:T(8,128)(2,1)S(1)}, u32[]{:S(2)}, u32[]{:S(2)}) collective-permute-start(bf16[192,512]{1,0:T(8,128)(2,1)S(1)} %get-tuple-element.80._), channel_id=1, source_target_pairs={{0,64},{64,128},{128,192},{192,0},{1,65},{65,129},{129,193},{193,1... | collective-permute-start | bytes 589832 | tf_op jit(solution)/shard_map/ppermute | solution.py:30
  121.7 14.7 %collective-permute-start.36 = (bf16[192,512]{1,0:T(8,128)(2,1)S(1)}, bf16[192,512]{1,0:T(8,128)(2,1)S(1)}, u32[]{:S(2)}, u32[]{:S(2)}) collective-permute-start(bf16[192,512]{1,0:T(8,128)(2,1)S(1)} %get-tuple-element.88), channel_id=1, source_target_pairs={{0,128},{64,192},{128,0},{192,64},{1,129},{65,193},{129,1},{193,65... | collective-permute-start | bytes 589832 | tf_op jit(solution)/shard_map/ppermute | solution.py:30
  125.6 12.8 %collective-permute-start.37 = (bf16[192,512]{1,0:T(8,128)(2,1)S(1)}, bf16[192,512]{1,0:T(8,128)(2,1)S(1)}, u32[]{:S(2)}, u32[]{:S(2)}) collective-permute-start(bf16[192,512]{1,0:T(8,128)(2,1)S(1)} %get-tuple-element.89), channel_id=1, source_target_pairs={{0,192},{64,0},{128,64},{192,128},{1,193},{65,1},{129,65},{193,129... | collective-permute-start | bytes 589832 | tf_op jit(solution)/shard_map/ppermute | solution.py:30
  127.0 11.4 %collective-permute-start.33 = (bf16[128,512]{1,0:T(8,128)(2,1)S(1)}, bf16[128,512]{1,0:T(8,128)(2,1)S(1)}, u32[]{:S(2)}, u32[]{:S(2)}) collective-permute-start(bf16[128,512]{1,0:T(8,128)(2,1)S(1)} %get-tuple-element.86), channel_id=1, source_target_pairs={{0,16},{16,32},{32,48},{48,0},{1,17},{17,33},{33,49},{49,1},{2,18}... | collective-permute-start | bytes 393224 | tf_op jit(solution)/shard_map/ppermute | solution.py:30
  127.1 11.3 %collective-permute-start.34 = (bf16[128,512]{1,0:T(8,128)(2,1)S(1)}, bf16[128,512]{1,0:T(8,128)(2,1)S(1)}, u32[]{:S(2)}, u32[]{:S(2)}) collective-permute-start(bf16[128,512]{1,0:T(8,128)(2,1)S(1)} %get-tuple-element.87), channel_id=1, source_target_pairs={{0,48},{16,0},{32,16},{48,32},{1,49},{17,1},{33,17},{49,33},{2,50}... | collective-permute-start | bytes 393224 | tf_op jit(solution)/shard_map/ppermute | solution.py:30
  (13 other events, 95.9 us)
